TPU v7x, 128 devices: a whole 4x4x4 slice. The times are simulated.
128 devices in a mesh: box: 32 (over x, z, core), rep: 4 (over y).
Axes of the slice: x: 4, y: 4, z: 4, core: 2. Of those that a mesh axis runs over, the one named last changes fastest.
Arguments:
- currents: bfloat16 [2, 2, 1024, 128], P(None, None, 'box'), may hold values from -6 to 6
- populations: int32 [1024], P('box'), may hold values from 1 to 128, as said below
- radiate: bfloat16 [1024, 2, 4, 64, 128], P('box', None, 'rep'), may hold values from -0.5 to 0.5
- receive: bfloat16 [1024, 2, 4, 64, 128], P('box', None, 'rep'), may hold values from -0.375 to 0.375
- translation: float32 [2, 4, 64, 316], P(None, 'rep'), may hold values from -1 to 1
- far_list: int32 [1024, 32], replicated, may hold values from 0 to 1023
- far_type: int32 [1024, 32], replicated, may hold values from 0 to 315
- near_list: int32 [1024, 8], P('box', 'rep'), may hold values from 0 to 1023, as said below
- near_block: bfloat16 [1024, 8, 2, 128, 128], P('box', 'rep'), may hold values from -0.125 to 0.125
Outputs:
- field: float32 [2, 2, 1024, 128], P(None, None, 'box')
Inputs may be any that keep to these rules, and one draw needn't show every extreme that they name: `populations`: each box has at least one live slot, and some box has all 128 slots live. near_list[b, n] lies within 32 of b; near_list[b, 0] is b itself.
All inputs are finite; a program needn't handle non-finite values.
Results may differ from a plain program's by a relative error of at most 0.0026.
Values may be sent and summed in bfloat16 or wider, within the bound.
No kernel may reach another device: no remote copies, remote signals or barrier semaphores. Data moves between devices by JAX's collectives and lax.ppermute only.
A program may use at most 320 MiB of HBM per device.

v0:
```python
import jax
import jax.numpy as jnp
from jax import lax
from jax.sharding import PartitionSpec as P


def extended(array, sides, width):
    for axis, dim in sides:
        count, length = (lax.axis_size(axis), array.shape[dim])
        up = [(i, (i + 1) % count) for i in range(count - 1)]
        down = [(j, i) for i, j in up]
        last = lax.slice_in_dim(array, length - width, length, axis=dim)
        leading = lax.slice_in_dim(array, 0, width, axis=dim)
        before = lax.ppermute(last, axis, up)
        after = lax.ppermute(leading, axis, down)
        array = jnp.concatenate([before, array, after], axis=dim)
    return array


def complex_einsum(a_re, a_im, b_re, b_im, form):

    def single(a, b):
        return jnp.einsum(form, a, b, preferred_element_type=jnp.float32)

    return (single(a_re, b_re) - single(a_im, b_im), single(a_re, b_im) + single(a_im, b_re))


def translate(patterns, partners, kinds, table):
    source = jnp.take(patterns, partners.T, axis=3)
    coef = jnp.take(table, kinds.T, axis=2)
    real = jnp.sum(coef[0][None] * source[0] - coef[1][None] * source[1], axis=2)
    imag = jnp.sum(coef[0][None] * source[1] + coef[1][None] * source[0], axis=2)
    return jnp.stack([real, imag]).astype(jnp.bfloat16)


def body(
    currents, populations, radiate, receive, translation, far_list, far_type, near_list, near_block
):
    position = lax.axis_index("box")
    box_dev = currents.shape[2]
    slots = currents.shape[3]
    live = jnp.arange(slots)[None, :] < populations[:, None]
    masked = jnp.where(live[None, None], currents, jnp.zeros_like(currents))
    table = radiate[:, :, 0]
    pat_re, pat_im = complex_einsum(table[:, 0], table[:, 1], masked[0], masked[1], "bkp,ibp->ikb")
    pattern = jnp.stack([pat_re, pat_im])
    trans_all = translation[:, 0]
    every = lax.all_gather(pattern, "box", axis=3, tiled=True)
    own_partners = lax.dynamic_slice_in_dim(far_list, position * box_dev, box_dev, 0)
    own_kinds = lax.dynamic_slice_in_dim(far_type, position * box_dev, box_dev, 0)
    incoming = translate(every, own_partners, own_kinds, trans_all)
    rcv = receive[:, :, 0]
    far_re, far_im = complex_einsum(rcv[:, 0], rcv[:, 1], incoming[0], incoming[1], "bkp,ikb->ibp")
    widened = extended(masked, (("box", 2),), box_dev)
    local_index = near_list - (position * box_dev - box_dev)
    neighbours = jnp.take(widened, local_index, axis=2)
    near_re, near_im = complex_einsum(
        near_block[:, :, 0], near_block[:, :, 1], neighbours[0], neighbours[1], "bnqp,ibnp->ibq"
    )
    partial_total = jnp.stack([far_re + near_re, far_im + near_im])
    total = lax.psum(partial_total, "rep")
    return jnp.where(live[None, None], total, jnp.zeros_like(total))


def solution(mesh):
    return jax.shard_map(
        body,
        mesh=mesh,
        in_specs=(
            P(None, None, "box", None),
            P("box"),
            P("box", None, "rep", None, None),
            P("box", None, "rep", None, None),
            P(None, "rep", None, None),
            P(),
            P(),
            P("box", "rep"),
            P("box", "rep", None, None, None),
        ),
        out_specs=P(None, None, "box", None),
        check_vma=False,
    )
```

profile of v0, /device:TPU:0, one launch (start us, length us, event | category | flops | bytes accessed | tf_op | source)
XLA Modules:
  0.0 123.7 jit_solution(11204714711270127743)
XLA Ops:
  6.5 0.7 iota_compare_fusion
  7.3 0.8 broadcast_select_fusion.2
  8.1 1.4 %collective-permute-start = (bf16[2,2,32,128]{3,1,2,0:T(2,128)(2,1)S(1)}, bf16[2,2,32,128]{3,1,2,0:T(2,128)(2,1)S(1)}, u32[]{:S(2)}, u32[]{:S(2)}) collective-permute-start(bf16[2,2,32,128]{3,1,2,0:T(2,128)(2,1)S(1)} %broadcast_select_fusion.2), channel_id=1, source_target_pairs={{0,4},{4,8},{8,12},{12,16},{16,20},{20,24},{24,28},{28,32},{32,36}... | collective-permute-start | bytes 98312 | tf_op jit(solution)/shard_map/ppermute | solution.py:14
  9.5 1.3 %collective-permute-start.1 = (bf16[2,2,32,128]{3,1,2,0:T(2,128)(2,1)S(1)}, bf16[2,2,32,128]{3,1,2,0:T(2,128)(2,1)S(1)}, u32[]{:S(2)}, u32[]{:S(2)}) collective-permute-start(bf16[2,2,32,128]{3,1,2,0:T(2,128)(2,1)S(1)} %broadcast_select_fusion.2), channel_id=1, source_target_pairs={{4,0},{8,4},{12,8},{16,12},{20,16},{24,20},{28,24},{32,28},{36,32}... | collective-permute-start | bytes 98312 | tf_op jit(solution)/shard_map/ppermute | solution.py:15
  10.8 1.3 %copy.46 = bf16[32,2,1,64,128]{4,3,0,1,2:T(8,128)(2,1)S(1)} copy(bf16[32,2,1,64,128]{4,3,2,1,0:T(8,128)(2,1)} %param.11) | data formatting | bytes 2097152 | tf_op args[2]
  12.9 0.4 fusion.28
  13.7 0.7 pad_maximum_fusion.1
  14.4 0.8 compare_and_fusion
  15.3 0.8 compare_and_fusion.1
  16.4 3.6 %gather_fusion = f32[1024,2,64]{2,1,0:T(2,128)S(1)} fusion(f32[2,64,316]{1,0,2:T(2,128)S(1)} %bitcast.135, s32[1024]{0:T(1024)S(1)} %broadcast_clamp_fusion.1), kind=kCustom, calls=%fused_computation | custom fusion | bytes 1052672 | tf_op jit(solution)/shard_map/jit(_take)/gather | solution.py:30
  20.5 1.1 slice_bitcast_fusion.7
  21.9 0.7 gather_fusion.2
  22.8 2.4 %fusion.12 = f32[32,2,128]{2,1,0:T(2,128)S(1)} fusion(bf16[32,2,2,128,128]{4,3,2,1,0:T(8,128)(2,1)} %param.17, bf16[2,2,32,2,128]{4,1,3,2,0:T(2,128)(2,1)S(1)} %fusion.40), kind=kOutput, calls=%fused_computation.16 | convolution fusion | flops 4194304 | bytes 2162688 | tf_op jit(solution)/shard_map/bnqp,ibnp->ibq/dot_general | solution.py:23
  25.2 2.3 %fusion.15 = f32[32,2,128]{2,1,0:T(2,128)S(1)} fusion(bf16[32,2,2,128,128]{4,3,2,1,0:T(8,128)(2,1)} %param.17, bf16[2,2,32,2,128]{4,1,3,2,0:T(2,128)(2,1)S(1)} %fusion.40), kind=kOutput, calls=%fused_computation.17 | convolution fusion | flops 4194304 | bytes 2162688 | tf_op jit(solution)/shard_map/bnqp,ibnp->ibq/dot_general | solution.py:23
  27.5 0.6 fusion.33
  28.1 0.7 fusion.30
  28.8 35.2 %all-gather.2.cloned.1.call-done = f32[2,2,64,1024]{2,1,3,0:T(2,128)} async-done(((f32[2,2,64,32]{2,1,3,0:T(2,128)}), f32[2,2,64,1024]{2,1,3,0:T(2,128)}) %all-gather.2.cloned.1.call-update) | async-done | bytes 1048592 | tf_op jit(solution)/shard_map/all_gather | solution.py:48
  64.0 6.3 %gather_fusion.1 = f32[1024,2,2,64]{3,2,1,0:T(2,128)S(1)} fusion(f32[2,2,64,1024]{2,1,3,0:T(2,128)} %all-gather.2.cloned.1.call-done, s32[1024]{0:T(1024)S(1)} %broadcast_clamp_fusion), kind=kCustom, calls=%fused_computation.1 | custom fusion | bytes 2101248 | tf_op jit(solution)/shard_map/jit(_take)/gather | solution.py:29
  70.2 1.4 %select_bitcast_fusion = f32[2,2,64,32,32]{2,1,0,4,3:T(2,128)S(1)} fusion(f32[32,32,2,2,64]{4,3,2,1,0:T(2,128)S(1)} %bitcast.134, pred[32,32]{1,0:T(8,128)(4,1)S(1)} %get-tuple-element.9), kind=kLoop, calls=%fused_computation.11 | loop fusion | flops 262144 | bytes 2098176 | tf_op jit(solution)/shard_map/jit(_take)/select_n | solution.py:29
  71.7 1.8 %subtract_reduce_fusion = (bf16[2,64,32]{1,0,2:T(2,128)(2,1)S(1)}, bf16[2,64,32]{1,0,2:T(2,128)(2,1)S(1)}) fusion(f32[2,2,64,32,32]{2,1,0,4,3:T(2,128)S(1)} %select_bitcast_fusion, f32[64,32,32]{0,2,1:T(8,128)S(1)} %copy-done.1, f32[64,32,32]{0,2,1:T(8,128)S(1)} %copy-done), kind=kLoop, calls=%fused_computation.38 | loop fusion | flops 1040384 | bytes 1589248 | tf_op jit(solution)/shard_map/reduce_sum | solution.py:31
  74.5 0.7 pad_maximum_fusion.2
  75.1 40.2 %all-reduce.2.cloned.1.call-done = f32[2,2,32,128]{3,1,2,0:T(2,128)} async-done(((f32[2,2,32,128]{3,1,2,0:T(2,128)}), f32[2,2,32,128]{3,1,2,0:T(2,128)}) %all-reduce.2.cloned.1.call-update) | async-done | bytes 65552 | tf_op jit(solution)/shard_map/psum | solution.py:61
  115.4 0.9 broadcast_select_fusion.1
  116.3 0.6 copy.33
  (40 shorter events, 3.6 us)
Async XLA Ops:
  6.5 57.4 %all-gather.2.cloned.1.call-start = ((), (), s32[]{:S(2)}) async-start(), calls=%async_computation | async-start | bytes 2162688 | tf_op jit(solution)/shard_map/all_gather | solution.py:48
  8.1 8.1 %copy-start.4 = (s32[32,2]{0,1:T(2,128)S(1)}, s32[32,2]{0,1:T(2,128)}, u32[]{:S(2)}) copy-start(s32[32,2]{0,1:T(2,128)} %param.16) | copy-start | bytes 772
  8.1 8.1 %copy-start.3 = (f32[2,1,64,316]{3,2,1,0:T(8,128)S(1)}, f32[2,1,64,316]{3,2,1,0:T(8,128)}, u32[]{:S(2)}) copy-start(f32[2,1,64,316]{3,2,1,0:T(8,128)} %param.13) | copy-start | bytes 485380
  8.1 13.7 %collective-permute-start = (bf16[2,2,32,128]{3,1,2,0:T(2,128)(2,1)S(1)}, bf16[2,2,32,128]{3,1,2,0:T(2,128)(2,1)S(1)}, u32[]{:S(2)}, u32[]{:S(2)}) collective-permute-start(bf16[2,2,32,128]{3,1,2,0:T(2,128)(2,1)S(1)} %broadcast_select_fusion.2), channel_id=1, source_target_pairs={{0,4},{4,8},{8,12},{12,16},{16,20},{20,24},{24,28},{28,32},{32,36}... | collective-permute-start | bytes 98312 | tf_op jit(solution)/shard_map/ppermute | solution.py:14
  9.5 12.2 %collective-permute-start.1 = (bf16[2,2,32,128]{3,1,2,0:T(2,128)(2,1)S(1)}, bf16[2,2,32,128]{3,1,2,0:T(2,128)(2,1)S(1)}, u32[]{:S(2)}, u32[]{:S(2)}) collective-permute-start(bf16[2,2,32,128]{3,1,2,0:T(2,128)(2,1)S(1)} %broadcast_select_fusion.2), channel_id=1, source_target_pairs={{4,0},{8,4},{12,8},{16,12},{20,16},{24,20},{28,24},{32,28},{36,32}... | collective-permute-start | bytes 98312 | tf_op jit(solution)/shard_map/ppermute | solution.py:15
  14.4 101.0 %all-reduce.2.cloned.1.call-start = ((), (), s32[]{:S(2)}) async-start(), calls=%async_computation.1 | async-start | bytes 131072 | tf_op jit(solution)/shard_map/psum | solution.py:61
  20.2 1.3 %copy-start.2 = (bf16[32,2,1,64,128]{4,3,2,1,0:T(8,128)(2,1)S(1)}, bf16[32,2,1,64,128]{4,3,2,1,0:T(8,128)(2,1)}, u32[]{:S(2)}) copy-start(bf16[32,2,1,64,128]{4,3,2,1,0:T(8,128)(2,1)} %param.12) | copy-start | bytes 3145732
  22.8 4.7 %copy-start.5 = (bf16[32,2,2,128,128]{4,3,2,1,0:T(8,128)(2,1)S(1)}, bf16[32,2,2,128,128]{4,3,2,1,0:T(8,128)(2,1)}, u32[]{:S(2)}) copy-start(bf16[32,2,2,128,128]{4,3,2,1,0:T(8,128)(2,1)} %param.17) | copy-start | bytes 12582916
  70.2 1.4 %copy-start = (f32[64,32,32]{0,2,1:T(8,128)S(1)}, f32[64,32,32]{0,2,1:T(8,128)}, u32[]{:S(2)}) copy-start(f32[64,32,32]{0,2,1:T(8,128)} %get-tuple-element.13) | copy-start | bytes 786436
  70.2 1.4 %copy-start.1 = (f32[64,32,32]{0,2,1:T(8,128)S(1)}, f32[64,32,32]{0,2,1:T(8,128)}, u32[]{:S(2)}) copy-start(f32[64,32,32]{0,2,1:T(8,128)} %get-tuple-element.14) | copy-start | bytes 786436
Sparse Core Ops, SparseCore 0:
  14.5 49.4 all-gather.1
  75.3 40.0 all-reduce.1
where the time goes:
time: 124 us
  waiting for transfers between devices  75.4 us (61%)
  local copies, waits for them, and re-layouts  14.4 us (12%)
  between operations  13.6 us (11%)
  other arithmetic  9.07 us (7%)
  matrix products  8.51 us (7%)
  starting transfers between devices  2.76 us (2%)
    psum x1, waiting for transfers between devices, body(): total = lax.psum(partial_total, 'rep')  40.2 us
    all_gather x1, waiting for transfers between devices, body(): every = lax.all_gather(pattern, 'box', axis=3, tiled=True)  35.2 us
    dot_general x12, matrix products, single(): return jnp.einsum(form, a, b, preferred_element_type=jnp.float32)  8.51 us
    gather x1, local copies, waits for them, and re-layouts, translate(): source = jnp.take(patterns, partners.T, axis=3)  6.26 us
    gather x2, local copies, waits for them, and re-layouts, translate(): coef = jnp.take(table, kinds.T, axis=2)  3.62 us
  transfers between devices with their start and end apart: 4, of which 2 were waited for; matrix products, arithmetic and copies ran while one was open for 14% of the time, Pallas kernels for 0%

commit v1 on v0

v1 whole, which is shorter than its diff:
```python
import jax
import jax.numpy as jnp
from jax import lax
from jax.experimental import pallas as pl
from jax.experimental.pallas import tpu as pltpu
from jax.sharding import PartitionSpec as P

F32 = jnp.float32
BF16 = jnp.bfloat16
NT = (((1,), (1,)), ((), ()))
NN = (((1,), (0,)), ((), ()))
VMEM = pl.BlockSpec(memory_space=pltpu.VMEM)
SMEM = pl.BlockSpec(memory_space=pltpu.SMEM)
XS = ZS = 4


def iota(shape, dim):
    return lax.broadcasted_iota(jnp.int32, shape, dim)


def dot(a, b, dims=NN):
    return lax.dot_general(a, b, dims, preferred_element_type=F32)


def chip_index(x, z, core):
    return (x * ZS + z) * 2 + core


def plane_perm(move):
    places = [(x, z, c) for x in range(XS) for z in range(ZS) for c in range(2)]
    return [(chip_index(*move(*place)), chip_index(*place)) for place in places]


def from_z(d):
    return plane_perm(lambda x, z, c: (x, (z + d) % ZS, c))


def from_x(d):
    return plane_perm(lambda x, z, c: ((x + d) % XS, z, c))


def from_core():
    return plane_perm(lambda x, z, c: (x, z, 1 - c))


def from_next_chip():
    def move(x, z, c):
        chip = (x * ZS + z + (1 if c else -1)) % (XS * ZS)
        return chip // ZS, chip % ZS, 1 - c

    return plane_perm(move)


def live_rows(pop_ref, boxes, slots):
    row = iota((boxes, slots), 0)
    count = jnp.zeros((boxes, slots), jnp.int32)
    for b in range(boxes):
        count = jnp.where(row == b, pop_ref[b], count)
    return iota((boxes, slots), 1) < count


def pattern_kernel(pop_ref, cur_ref, rad_ref, masked_ref, pat_ref):
    lines, boxes, slots = cur_ref.shape
    live = live_rows(pop_ref, boxes, slots)
    masked = [jnp.where(live, cur_ref[j].astype(F32), 0.0) for j in range(lines)]
    for j in range(lines):
        masked_ref[j] = masked[j].astype(BF16)
    rows = jnp.concatenate(masked, axis=0)
    box_of_row = iota(rows.shape, 0) & (boxes - 1)
    total = jnp.zeros((lines * boxes, slots), F32)
    for b in range(0, boxes, 2):
        left = jnp.concatenate(
            [jnp.where(box_of_row == b + h, rows, 0.0).astype(BF16) for h in range(2)], axis=1
        )
        right = jnp.concatenate([rad_ref[b], rad_ref[b + 1]], axis=1)
        total = total + dot(left, right, NT)
    half = slots // 2
    sign = jnp.where(iota((boxes, slots), 1) < half, -1.0, 1.0)
    for i in range(2):
        real = total[i * boxes : (i + 1) * boxes]
        imag = total[(2 + i) * boxes : (3 + i) * boxes]
        out = real + sign * pltpu.roll(imag, half, 1)
        pat_ref[:, i * slots : (i + 1) * slots] = out.astype(BF16)


def coef_kernel(type_ref, trans_ref, coef_ref, table_ref):
    boxes, far = type_ref.shape
    half, types = trans_ref.shape[1:]
    wide = table_ref.shape[2]
    table_ref[...] = jnp.zeros_like(table_ref)
    for c in range(2):
        value = trans_ref[c]
        high = value.astype(BF16)
        low = (value - high.astype(F32)).astype(BF16)
        for k in range(2):
            place = pl.ds((2 * c + k) * half, half)
            table_ref[0, place, :types] = high
            table_ref[1, place, :types] = low
    lane = iota((boxes, wide), 1)
    pieces = []
    for f in range(far):
        column = type_ref[:, f : f + 1]
        pieces.append(jnp.where(lane == column, 1.0, 0.0).astype(BF16))
    hot = jnp.concatenate(pieces, axis=0)
    coef_ref[...] = dot(hot, table_ref[0], NT) + dot(hot, table_ref[1], NT)


def near_kernel(pop_ref, list_ref, own_ref, core_ref, next_ref, block_ref, out_ref):
    lines, boxes, slots = own_ref.shape
    pairs = list_ref.shape[1]
    place = lax.axis_index("box")
    core = place & 1
    beyond = place + 2 * core - 1
    lane = iota((boxes, slots), 1)
    first = jnp.where(
        lane < boxes,
        place * boxes,
        jnp.where(lane < 2 * boxes, (place + 1 - 2 * core) * boxes, beyond * boxes),
    )
    ids = jnp.where(lane < 3 * boxes, first + (lane & (boxes - 1)), -1000000)
    hot = jnp.concatenate(
        [jnp.where(ids == list_ref[:, n : n + 1], 1.0, 0.0).astype(BF16) for n in range(pairs)],
        axis=0,
    )
    zero = jnp.zeros((slots - 3 * boxes, slots), BF16)
    picked = []
    for j in range(lines):
        source = jnp.concatenate([own_ref[j], core_ref[j], next_ref[j], zero], axis=0)
        picked.append(dot(hot, source))
    box_of_row = iota((lines * boxes, slots), 0) & (boxes - 1)
    lefts = []
    for n in range(pairs):
        part = [value[n * boxes : (n + 1) * boxes] for value in picked]
        lefts.append(jnp.concatenate(part, axis=0))
        lefts.append(jnp.concatenate([-part[2], -part[3], part[0], part[1]], axis=0))
    total = jnp.zeros((lines * boxes, slots), F32)
    for b in range(boxes):
        mine = box_of_row == b
        for n in range(pairs):
            left = jnp.concatenate(
                [jnp.where(mine, lefts[2 * n + c], 0.0).astype(BF16) for c in range(2)], axis=1
            )
            right = jnp.concatenate([block_ref[b, n, 0], block_ref[b, n, 1]], axis=1)
            total = total + dot(left, right, NT)
    out_ref[...] = total


def far_kernel(
    pop_ref, list_ref, coef_ref, near_ref, mine_ref, theirs_ref, receive_ref, out_ref
):
    boxes, far = list_ref.shape
    slots = receive_ref.shape[2]
    held, wide = mine_ref.shape
    place = lax.axis_index("box")
    core = place & 1
    chip = place >> 1
    x, z = chip >> 2, chip & 3
    lane = iota((boxes, held), 1)
    from_x_ = (x + (lane >> 7)) & 3
    from_z_ = (z + ((lane >> 5) & 3)) & 3
    ids = (((from_x_ * ZS + from_z_) * 2 + core) * boxes) + (lane & (boxes - 1))
    other = ids + (1 - 2 * core) * boxes
    acc = [jnp.zeros((boxes, slots), F32) for _ in range(4)]
    group = 8
    for f in range(0, far, group):
        columns = [list_ref[:, g : g + 1] for g in range(f, f + group)]
        hot_mine = jnp.concatenate(
            [jnp.where(ids == col, 1.0, 0.0).astype(BF16) for col in columns], axis=0
        )
        hot_theirs = jnp.concatenate(
            [jnp.where(other == col, 1.0, 0.0).astype(BF16) for col in columns], axis=0
        )
        source = dot(hot_mine, mine_ref[...]) + dot(hot_theirs, theirs_ref[...])
        for g in range(group):
            rows = slice(g * boxes, (g + 1) * boxes)
            at = (f + g) * boxes
            straight = coef_ref[at : at + boxes, :slots]
            crossed = coef_ref[at : at + boxes, slots:]
            for i in range(2):
                value = source[rows, i * slots : (i + 1) * slots]
                acc[2 * i] = acc[2 * i] + straight * value
                acc[2 * i + 1] = acc[2 * i + 1] + crossed * value
    half = slots // 2
    low = iota((boxes, slots), 1) < half
    minus = jnp.where(low, -1.0, 1.0)
    reals, imags = [], []
    for i in range(2):
        incoming = acc[2 * i] + minus * pltpu.roll(acc[2 * i + 1], half, 1)
        incoming = incoming.astype(BF16).astype(F32)
        reals.append(-minus * incoming)
        imags.append(pltpu.roll(incoming, half, 1))
    left_rows = jnp.concatenate(reals + imags, axis=0)
    box_of_row = iota(left_rows.shape, 0) & (boxes - 1)
    total = near_ref[...]
    for b in range(0, boxes, 2):
        left = jnp.concatenate(
            [jnp.where(box_of_row == b + h, left_rows, 0.0).astype(BF16) for h in range(2)], axis=1
        )
        right = jnp.concatenate([receive_ref[b], receive_ref[b + 1]], axis=0)
        total = total + dot(left, right)
    live = live_rows(pop_ref, boxes, slots)
    for j in range(4):
        out_ref[j] = jnp.where(live, total[j * boxes : (j + 1) * boxes], 0.0)


def call(kernel, out_shape, specs, out_specs, scratch=(), flops=0, size=0):
    return pl.pallas_call(
        kernel,
        out_shape=out_shape,
        in_specs=specs,
        out_specs=out_specs,
        scratch_shapes=list(scratch),
        cost_estimate=pl.CostEstimate(flops=flops, bytes_accessed=size, transcendentals=0),
        compiler_params=pltpu.CompilerParams(vmem_limit_bytes=32 * 1024 * 1024),
    )


def body(
    currents, populations, radiate, receive, translation, far_list, far_type, near_list, near_block
):
    place = lax.axis_index("box")
    incs, boxes, slots = currents.shape[1:]
    lines = 2 * incs
    half = radiate.shape[3]
    far = far_list.shape[1]
    shape = jax.ShapeDtypeStruct
    cur = currents.reshape(lines, boxes, slots)
    rad = radiate.reshape(boxes, 2 * half, slots)
    rec = receive.reshape(boxes, 2 * half, slots)
    trans = translation.reshape(2, half, translation.shape[3])
    block = near_block
    own_list = lax.dynamic_slice_in_dim(far_list, place * boxes, boxes, 0)
    own_type = lax.dynamic_slice_in_dim(far_type, place * boxes, boxes, 0)

    masked, pattern = call(
        pattern_kernel,
        (shape((lines, boxes, slots), BF16), shape((boxes, incs * slots), BF16)),
        [SMEM, VMEM, VMEM],
        (VMEM, VMEM),
    )(populations, cur, rad)

    around = [lax.ppermute(pattern, "box", from_z(d)) for d in (1, 2, 3)]
    line = jnp.concatenate([pattern] + around, axis=0)
    planes = [lax.ppermute(line, "box", from_x(d)) for d in (1, 2, 3)]
    mine = jnp.concatenate([line] + planes, axis=0)
    theirs = lax.ppermute(mine, "box", from_core())

    near_core = lax.ppermute(masked, "box", from_core())
    near_next = lax.ppermute(masked, "box", from_next_chip())

    types = trans.shape[2]
    padded = -(-types // 128) * 128
    coef = call(
        coef_kernel,
        shape((far * boxes, 2 * slots), F32),
        [VMEM, VMEM],
        VMEM,
        [pltpu.VMEM((2, 4 * half, padded), BF16)],
    )(own_type, trans)

    near = call(
        near_kernel,
        shape((lines * boxes, slots), F32),
        [SMEM, VMEM, VMEM, VMEM, VMEM, VMEM],
        VMEM,
    )(populations, near_list, masked, near_core, near_next, block)

    part = call(
        far_kernel,
        shape((lines, boxes, slots), F32),
        [SMEM] + [VMEM] * 6,
        VMEM,
    )(populations, own_list, coef, near, mine, theirs, rec)

    reps = lax.axis_size("rep")
    others = [
        lax.ppermute(part, "rep", [((r + d) % reps, r) for r in range(reps)]) for d in (1, 2, 3)
    ]
    total = (part + others[1]) + (others[0] + others[2])
    return total.reshape(2, incs, boxes, slots)


def solution(mesh):
    return jax.shard_map(
        body,
        mesh=mesh,
        in_specs=(
            P(None, None, "box", None),
            P("box"),
            P("box", None, "rep", None, None),
            P("box", None, "rep", None, None),
            P(None, "rep", None, None),
            P(),
            P(),
            P("box", "rep"),
            P("box", "rep", None, None, None),
        ),
        out_specs=P(None, None, "box", None),
        check_vma=False,
    )
```

time: 124 us -> 47.2 us (0.38)
  waiting for transfers between devices: 75.4 us -> 10.4 us
  starting transfers between devices: 2.76 us -> 21.8 us
  between operations: 13.6 us -> 0.11 us
  matrix products: 8.51 us -> 0 us
  other arithmetic: 9.07 us -> 0.65 us
  local copies, waits for them, and re-layouts: 14.4 us -> 8.25 us
  Pallas kernels: 0 us -> 5.65 us
    psum x1 -> x0, waiting for transfers between devices: 40.2 us -> none  [body(): total = lax.psum(partial_total, 'rep')]
    all_gather x1 -> x0, waiting for transfers between devices: 35.2 us -> none  [body(): every = lax.all_gather(pattern, 'box', axis=3, tiled=True)]
    ppermute x2 -> x12, starting transfers between devices: 2.72 us -> 21.8 us  [the longest x3 6.66 us: body(): around = [lax.ppermute(pattern, 'box', from_z(d)) for d in (1, 2, 3)]]
    gather x4 -> x0, local copies, waits for them, and re-layouts: 10.6 us -> none  [the longest x1 6.26 us: translate(): source = jnp.take(patterns, partners.T, axis=3)]
    ppermute x2 -> x12, waiting for transfers between devices: 0.01 us -> 10.4 us  [the longest x3 3.87 us: body(): planes = [lax.ppermute(line, 'box', from_x(d)) for d in (1, 2, 3)]]
    dot_general x12 -> x0, matrix products: 8.51 us -> none  [single(): return jnp.einsum(form, a, b, preferred_element_type=jnp.float32)]
    unnamed x15 -> x24, local copies, waits for them, and re-layouts: 1.61 us -> 7.38 us
    pallas_call x0 -> x4, Pallas kernels: none -> 5.65 us  [the longest x1 1.95 us: body(): call(near_kernel, shape((lines * boxes, slots), F32), [SMEM, VMEM, VMEM,...]
  transfers between devices with their start and end apart: 4 -> 12, of which waited for: 2 -> 7; matrix products, arithmetic and copies ran while one was open for 14% -> 4% of each run, Pallas kernels for 0% -> 6%
where the time goes in v1:
time: 47.2 us; the launch traced here: 46.8 us
  starting transfers between devices  21.8 us (46%)
  waiting for transfers between devices  10.4 us (22%)
  local copies, waits for them, and re-layouts  8.25 us (17%)
  Pallas kernels  5.65 us (12%)
  other arithmetic  0.65 us (1%)
    unnamed x24, local copies, waits for them, and re-layouts  7.38 us
    ppermute x3, starting transfers between devices, body(): around = [lax.ppermute(pattern, 'box', from_z(d)) for d in (1, 2, 3)]  6.66 us
    ppermute x3, starting transfers between devices, body(): lax.ppermute(part, 'rep', [((r + d) % reps, r) for r in range(reps)])  5.31 us
    ppermute x3, starting transfers between devices, body(): planes = [lax.ppermute(line, 'box', from_x(d)) for d in (1, 2, 3)]  5.12 us
    ppermute x1, starting transfers between devices, body(): near_next = lax.ppermute(masked, 'box', from_next_chip())  4.69 us
    ppermute x3, waiting for transfers between devices, body(): planes = [lax.ppermute(line, 'box', from_x(d)) for d in (1, 2, 3)]  3.87 us
    ppermute x3, waiting for transfers between devices, body(): lax.ppermute(part, 'rep', [((r + d) % reps, r) for r in range(reps)])  3.78 us
    ppermute x3, waiting for transfers between devices, body(): around = [lax.ppermute(pattern, 'box', from_z(d)) for d in (1, 2, 3)]  2.73 us
  transfers between devices with their start and end apart: 12, of which 7 were waited for; matrix products, arithmetic and copies ran while one was open for 4% of the time, Pallas kernels for 6%

profile of v1, /device:TPU:0, one launch (start us, length us, event | category | flops | bytes accessed | tf_op | source)
XLA Modules:
  0.0 46.8 jit_solution(17265168583136908431)
XLA Ops:
  0.0 1.3 %copy-done.2 = bf16[32,2,1,64,128]{4,3,2,1,0:T(8,128)(2,1)S(1)} copy-done((bf16[32,2,1,64,128]{4,3,2,1,0:T(8,128)(2,1)S(1)}, bf16[32,2,1,64,128]{4,3,2,1,0:T(8,128)(2,1)}, u32[]{:S(2)}) %copy-start.2) | copy-done | bytes 1048600
  1.3 0.8 %copy-done.5 = bf16[2,2,32,128]{3,2,1,0:T(8,128)(2,1)S(1)} copy-done((bf16[2,2,32,128]{3,2,1,0:T(8,128)(2,1)S(1)}, bf16[2,2,32,128]{3,2,1,0:T(8,128)(2,1)}, u32[]{:S(2)}) %copy-start.5) | copy-done | bytes 32792
  2.0 0.7 %copy-done.6 = s32[32]{0:T(128)S(1)} copy-done((s32[32]{0:T(128)S(1)}, s32[32]{0:T(128)}, u32[]{:S(2)}) %copy-start.6) | copy-done | bytes 152
  2.7 1.0 %shard_map.92 = (bf16[4,32,128]{2,1,0:T(8,128)(2,1)S(1)}, bf16[32,256]{1,0:T(8,128)(2,1)S(1)}) custom-call(s32[32]{0:T(128)S(1)} %copy-done.6, bf16[4,32,128]{2,1,0:T(8,128)(2,1)S(1)} %bitcast.8, bf16[32,128,128]{2,1,0:T(8,128)(2,1)S(1)} %bitcast.5), custom_call_target="tpu_custom_call" | custom-call | tf_op jit(solution)/shard_map/pallas_call | solution.py:235
  3.7 2.1 %collective-permute-start.4 = (bf16[32,256]{1,0:T(8,128)(2,1)S(1)}, bf16[32,256]{1,0:T(8,128)(2,1)S(1)}, u32[]{:S(2)}, u32[]{:S(2)}) collective-permute-start(bf16[32,256]{1,0:T(8,128)(2,1)S(1)} %get-tuple-element.8), channel_id=1, source_target_pairs={{24,0},{28,4},{0,8},{4,12},{8,16},{12,20},{16,24},{20,28},{56,32},... | collective-permute-start | bytes 49160 | tf_op jit(solution)/shard_map/ppermute | solution.py:242
  5.8 3.6 %collective-permute-start.3 = (bf16[32,256]{1,0:T(8,128)(2,1)S(1)}, bf16[32,256]{1,0:T(8,128)(2,1)S(1)}, u32[]{:S(2)}, u32[]{:S(2)}) collective-permute-start(bf16[32,256]{1,0:T(8,128)(2,1)S(1)} %get-tuple-element.8), channel_id=1, source_target_pairs={{16,0},{20,4},{24,8},{28,12},{0,16},{4,20},{8,24},{12,28},{48,32},... | collective-permute-start | bytes 49160 | tf_op jit(solution)/shard_map/ppermute | solution.py:242
  9.4 1.0 %collective-permute-start.2 = (bf16[32,256]{1,0:T(8,128)(2,1)S(1)}, bf16[32,256]{1,0:T(8,128)(2,1)S(1)}, u32[]{:S(2)}, u32[]{:S(2)}) collective-permute-start(bf16[32,256]{1,0:T(8,128)(2,1)S(1)} %get-tuple-element.8), channel_id=1, source_target_pairs={{8,0},{12,4},{16,8},{20,12},{24,16},{28,20},{0,24},{4,28},{40,32},... | collective-permute-start | bytes 49160 | tf_op jit(solution)/shard_map/ppermute | solution.py:242
  10.4 2.7 %collective-permute-done.2 = bf16[32,256]{1,0:T(8,128)(2,1)S(1)} collective-permute-done((bf16[32,256]{1,0:T(8,128)(2,1)S(1)}, bf16[32,256]{1,0:T(8,128)(2,1)S(1)}, u32[]{:S(2)}, u32[]{:S(2)}) %collective-permute-start.2) | collective-permute-done | bytes 16416 | tf_op jit(solution)/shard_map/ppermute | solution.py:242
  13.2 2.8 %collective-permute-start.5 = (bf16[128,256]{1,0:T(8,128)(2,1)S(1)}, bf16[128,256]{1,0:T(8,128)(2,1)S(1)}, u32[]{:S(2)}, u32[]{:S(2)}) collective-permute-start(bf16[128,256]{1,0:T(8,128)(2,1)S(1)} %get-tuple-element.9), channel_id=1, source_target_pairs={{32,0},{36,4},{40,8},{44,12},{48,16},{52,20},{56,24},{60,28},{64,3... | collective-permute-start | bytes 196616 | tf_op jit(solution)/shard_map/ppermute | solution.py:244
  16.0 2.3 %collective-permute-start.6 = (bf16[128,256]{1,0:T(8,128)(2,1)S(1)}, bf16[128,256]{1,0:T(8,128)(2,1)S(1)}, u32[]{:S(2)}, u32[]{:S(2)}) collective-permute-start(bf16[128,256]{1,0:T(8,128)(2,1)S(1)} %get-tuple-element.9), channel_id=1, source_target_pairs={{64,0},{68,4},{72,8},{76,12},{80,16},{84,20},{88,24},{92,28},{96,3... | collective-permute-start | bytes 196616 | tf_op jit(solution)/shard_map/ppermute | solution.py:244
  18.5 3.4 %collective-permute-done.6 = bf16[128,256]{1,0:T(8,128)(2,1)S(1)} collective-permute-done((bf16[128,256]{1,0:T(8,128)(2,1)S(1)}, bf16[128,256]{1,0:T(8,128)(2,1)S(1)}, u32[]{:S(2)}, u32[]{:S(2)}) %collective-permute-start.6) | collective-permute-done | bytes 65568 | tf_op jit(solution)/shard_map/ppermute | solution.py:244
  22.2 4.7 %collective-permute-start.1 = (bf16[4,32,128]{2,1,0:T(8,128)(2,1)S(1)}, bf16[4,32,128]{2,1,0:T(8,128)(2,1)S(1)}, u32[]{:S(2)}, u32[]{:S(2)}) collective-permute-start(bf16[4,32,128]{2,1,0:T(8,128)(2,1)S(1)} %get-tuple-element.7.own_ref), channel_id=1, source_target_pairs={{124,0},{8,4},{4,8},{16,12},{12,16},{24,20},{20,24},{32,28},{28,32... | collective-permute-start | bytes 98312 | tf_op jit(solution)/shard_map/ppermute | solution.py:249
  26.9 0.8 %constant_dynamic-slice_fusion = s32[32,32]{0,1:T(8,128)S(1)} fusion(s32[1024,32]{0,1:T(8,128)} %param.15, s32[]{:T(128)S(6)} %select_n.4), kind=kLoop, calls=%fused_computation.12 | loop fusion | bytes 8196 | tf_op jit(solution)/shard_map/dynamic_slice | solution.py:233
  27.9 0.8 %copy.12.list_ref = s32[32,2]{1,0:T(8,128)S(1)} copy(s32[32,2]{0,1:T(2,128)} %param.16) | data formatting | bytes 512 | tf_op args[7]
  28.7 0.9 %copy-done.4 = f32[2,1,64,316]{3,2,1,0:T(8,128)S(1)} copy-done((f32[2,1,64,316]{3,2,1,0:T(8,128)S(1)}, f32[2,1,64,316]{3,2,1,0:T(8,128)}, u32[]{:S(2)}) %copy-start.4) | copy-done | bytes 161816
  29.6 0.8 %shard_map.91.coef_ref = f32[1024,256]{1,0:T(8,128)S(1)} custom-call(s32[32,32]{1,0:T(8,128)S(1)} %copy.14.type_ref, f32[2,64,316]{2,1,0:T(8,128)S(1)} %bitcast.7), custom_call_target="tpu_custom_call" | custom-call | tf_op jit(solution)/shard_map/pallas_call | solution.py:253
  30.4 2.2 %copy-done.1 = bf16[32,2,2,128,128]{4,3,2,1,0:T(8,128)(2,1)S(1)} copy-done((bf16[32,2,2,128,128]{4,3,2,1,0:T(8,128)(2,1)S(1)}, bf16[32,2,2,128,128]{4,3,2,1,0:T(8,128)(2,1)}, u32[]{:S(2)}) %copy-start.1) | copy-done | bytes 4194328
  32.6 0.7 %copy-done.7 = s32[32]{0:T(128)S(1)} copy-done((s32[32]{0:T(128)S(1)}, s32[32]{0:T(128)}, u32[]{:S(2)}) %copy-start.7) | copy-done | bytes 152
  33.2 1.9 %shard_map.93.near_ref = f32[128,128]{1,0:T(8,128)S(1)} custom-call(s32[32]{0:T(128)S(1)} %copy-done.7, s32[32,2]{1,0:T(8,128)S(1)} %copy.12.list_ref, bf16[4,32,128]{2,1,0:T(8,128)(2,1)S(1)} %get-tuple-element.7.own_ref, bf16[4,32,128]{2,1,0:T(8,128)(2,1)S(1)} %collective-permute-done.core_ref, bf16[4,32,128]{2,1,0:T(8,128)(2,1)S(1)} %collective-permute-done.1.next_ref, ...), custom_call_target="tpu_custom_call" | custom-call | tf_op jit(solution)/shard_map/pallas_call | solution.py:261
  35.2 1.9 %shard_map.94 = f32[4,32,128]{2,1,0:T(8,128)S(1)} custom-call(s32[32]{0:T(128)S(1)} %copy-done.7, s32[32,32]{1,0:T(8,128)S(1)} %copy.13.list_ref, f32[1024,256]{1,0:T(8,128)S(1)} %shard_map.91.coef_ref, f32[128,128]{1,0:T(8,128)S(1)} %shard_map.93.near_ref, bf16[512,256]{1,0:T(8,128)(2,1)S(1)} %constant_dynamic-update-slice_fusion.4.mine_ref, ...), custom_call_target="tpu_custom_call" | custom-call | tf_op jit(solution)/shard_map/pallas_call | solution.py:268
  37.1 1.7 %collective-permute-start.11 = (f32[4,32,128]{2,1,0:T(8,128)S(1)}, f32[4,32,128]{2,1,0:T(8,128)S(1)}, u32[]{:S(2)}, u32[]{:S(2)}) collective-permute-start(f32[4,32,128]{2,1,0:T(8,128)S(1)} %shard_map.94), channel_id=1, source_target_pairs={{3,0},{0,1},{1,2},{2,3},{7,4},{4,5},{5,6},{6,7},{11,8},{8,9},{9,10... | collective-permute-start | bytes 196616 | tf_op jit(solution)/shard_map/ppermute | solution.py:277
  38.8 1.7 %collective-permute-start.10 = (f32[4,32,128]{2,1,0:T(8,128)S(1)}, f32[4,32,128]{2,1,0:T(8,128)S(1)}, u32[]{:S(2)}, u32[]{:S(2)}) collective-permute-start(f32[4,32,128]{2,1,0:T(8,128)S(1)} %shard_map.94), channel_id=1, source_target_pairs={{1,0},{2,1},{3,2},{0,3},{5,4},{6,5},{7,6},{4,7},{9,8},{10,9},{11,1... | collective-permute-start | bytes 196616 | tf_op jit(solution)/shard_map/ppermute | solution.py:277
  40.4 2.0 %collective-permute-start.9 = (f32[4,32,128]{2,1,0:T(8,128)S(1)}, f32[4,32,128]{2,1,0:T(8,128)S(1)}, u32[]{:S(2)}, u32[]{:S(2)}) collective-permute-start(f32[4,32,128]{2,1,0:T(8,128)S(1)} %shard_map.94), channel_id=1, source_target_pairs={{2,0},{3,1},{0,2},{1,3},{6,4},{7,5},{4,6},{5,7},{10,8},{11,9},{8,1... | collective-permute-start | bytes 196616 | tf_op jit(solution)/shard_map/ppermute | solution.py:277
  43.0 3.2 %collective-permute-done.9 = f32[4,32,128]{2,1,0:T(8,128)S(1)} collective-permute-done((f32[4,32,128]{2,1,0:T(8,128)S(1)}, f32[4,32,128]{2,1,0:T(8,128)S(1)}, u32[]{:S(2)}, u32[]{:S(2)}) %collective-permute-start.9) | collective-permute-done | bytes 65568 | tf_op jit(solution)/shard_map/ppermute | solution.py:277
  (33 shorter events, 2.1 us)
Async XLA Ops:
  0.0 26.9 %copy-start = (s32[1024,32]{0,1:T(8,128)S(1)}, s32[1024,32]{0,1:T(8,128)}, u32[]{:S(2)}) copy-start(s32[1024,32]{0,1:T(8,128)} %param.14) | copy-start | bytes 393220
  0.0 1.3 %copy-start.2 = (bf16[32,2,1,64,128]{4,3,2,1,0:T(8,128)(2,1)S(1)}, bf16[32,2,1,64,128]{4,3,2,1,0:T(8,128)(2,1)}, u32[]{:S(2)}) copy-start(bf16[32,2,1,64,128]{4,3,2,1,0:T(8,128)(2,1)} %param.11) | copy-start | bytes 3145732
  1.3 0.8 %copy-start.5 = (bf16[2,2,32,128]{3,2,1,0:T(8,128)(2,1)S(1)}, bf16[2,2,32,128]{3,2,1,0:T(8,128)(2,1)}, u32[]{:S(2)}) copy-start(bf16[2,2,32,128]{3,2,1,0:T(8,128)(2,1)} %param.9) | copy-start | bytes 98308
  2.0 0.7 %copy-start.6 = (s32[32]{0:T(128)S(1)}, s32[32]{0:T(128)}, u32[]{:S(2)}) copy-start(s32[32]{0:T(128)} %pop_ref.5) | copy-start | bytes 388
  2.7 32.5 %copy-start.3 = (bf16[32,2,1,64,128]{4,3,2,1,0:T(8,128)(2,1)S(1)}, bf16[32,2,1,64,128]{4,3,2,1,0:T(8,128)(2,1)}, u32[]{:S(2)}) copy-start(bf16[32,2,1,64,128]{4,3,2,1,0:T(8,128)(2,1)} %param.12) | copy-start | bytes 3145732
  3.7 9.4 %collective-permute-start.4 = (bf16[32,256]{1,0:T(8,128)(2,1)S(1)}, bf16[32,256]{1,0:T(8,128)(2,1)S(1)}, u32[]{:S(2)}, u32[]{:S(2)}) collective-permute-start(bf16[32,256]{1,0:T(8,128)(2,1)S(1)} %get-tuple-element.8), channel_id=1, source_target_pairs={{24,0},{28,4},{0,8},{4,12},{8,16},{12,20},{16,24},{20,28},{56,32},... | collective-permute-start | bytes 49160 | tf_op jit(solution)/shard_map/ppermute | solution.py:242
  5.8 7.3 %collective-permute-start.3 = (bf16[32,256]{1,0:T(8,128)(2,1)S(1)}, bf16[32,256]{1,0:T(8,128)(2,1)S(1)}, u32[]{:S(2)}, u32[]{:S(2)}) collective-permute-start(bf16[32,256]{1,0:T(8,128)(2,1)S(1)} %get-tuple-element.8), channel_id=1, source_target_pairs={{16,0},{20,4},{24,8},{28,12},{0,16},{4,20},{8,24},{12,28},{48,32},... | collective-permute-start | bytes 49160 | tf_op jit(solution)/shard_map/ppermute | solution.py:242
  9.4 3.7 %collective-permute-start.2 = (bf16[32,256]{1,0:T(8,128)(2,1)S(1)}, bf16[32,256]{1,0:T(8,128)(2,1)S(1)}, u32[]{:S(2)}, u32[]{:S(2)}) collective-permute-start(bf16[32,256]{1,0:T(8,128)(2,1)S(1)} %get-tuple-element.8), channel_id=1, source_target_pairs={{8,0},{12,4},{16,8},{20,12},{24,16},{28,20},{0,24},{4,28},{40,32},... | collective-permute-start | bytes 49160 | tf_op jit(solution)/shard_map/ppermute | solution.py:242
  13.2 5.3 %collective-permute-start.5 = (bf16[128,256]{1,0:T(8,128)(2,1)S(1)}, bf16[128,256]{1,0:T(8,128)(2,1)S(1)}, u32[]{:S(2)}, u32[]{:S(2)}) collective-permute-start(bf16[128,256]{1,0:T(8,128)(2,1)S(1)} %get-tuple-element.9), channel_id=1, source_target_pairs={{32,0},{36,4},{40,8},{44,12},{48,16},{52,20},{56,24},{60,28},{64,3... | collective-permute-start | bytes 196616 | tf_op jit(solution)/shard_map/ppermute | solution.py:244
  16.0 6.2 %collective-permute-start.7 = (bf16[128,256]{1,0:T(8,128)(2,1)S(1)}, bf16[128,256]{1,0:T(8,128)(2,1)S(1)}, u32[]{:S(2)}, u32[]{:S(2)}) collective-permute-start(bf16[128,256]{1,0:T(8,128)(2,1)S(1)} %get-tuple-element.9), channel_id=1, source_target_pairs={{96,0},{100,4},{104,8},{108,12},{112,16},{116,20},{120,24},{124,28... | collective-permute-start | bytes 196616 | tf_op jit(solution)/shard_map/ppermute | solution.py:244
  16.0 5.9 %collective-permute-start.6 = (bf16[128,256]{1,0:T(8,128)(2,1)S(1)}, bf16[128,256]{1,0:T(8,128)(2,1)S(1)}, u32[]{:S(2)}, u32[]{:S(2)}) collective-permute-start(bf16[128,256]{1,0:T(8,128)(2,1)S(1)} %get-tuple-element.9), channel_id=1, source_target_pairs={{64,0},{68,4},{72,8},{76,12},{80,16},{84,20},{88,24},{92,28},{96,3... | collective-permute-start | bytes 196616 | tf_op jit(solution)/shard_map/ppermute | solution.py:244
  22.2 13.0 %collective-permute-start.8 = (bf16[512,256]{1,0:T(8,128)(2,1)S(1)}, bf16[512,256]{1,0:T(8,128)(2,1)S(1)}, u32[]{:S(2)}, u32[]{:S(2)}) collective-permute-start(bf16[512,256]{1,0:T(8,128)(2,1)S(1)} %constant_dynamic-update-slice_fusion.4.mine_ref), channel_id=1, source_target_pairs={{4,0},{0,4},{12,8},{8,12},{20,16},{16,20},{28,24},{24,28},{36,32},... | collective-permute-start | bytes 786440 | tf_op jit(solution)/shard_map/ppermute | solution.py:246
  22.2 8.2 %collective-permute-start.1 = (bf16[4,32,128]{2,1,0:T(8,128)(2,1)S(1)}, bf16[4,32,128]{2,1,0:T(8,128)(2,1)S(1)}, u32[]{:S(2)}, u32[]{:S(2)}) collective-permute-start(bf16[4,32,128]{2,1,0:T(8,128)(2,1)S(1)} %get-tuple-element.7.own_ref), channel_id=1, source_target_pairs={{124,0},{8,4},{4,8},{16,12},{12,16},{24,20},{20,24},{32,28},{28,32... | collective-permute-start | bytes 98312 | tf_op jit(solution)/shard_map/ppermute | solution.py:249
  26.9 3.5 %collective-permute-start = (bf16[4,32,128]{2,1,0:T(8,128)(2,1)S(1)}, bf16[4,32,128]{2,1,0:T(8,128)(2,1)S(1)}, u32[]{:S(2)}, u32[]{:S(2)}) collective-permute-start(bf16[4,32,128]{2,1,0:T(8,128)(2,1)S(1)} %get-tuple-element.7.own_ref), channel_id=1, source_target_pairs={{4,0},{0,4},{12,8},{8,12},{20,16},{16,20},{28,24},{24,28},{36,32},... | collective-permute-start | bytes 98312 | tf_op jit(solution)/shard_map/ppermute | solution.py:248
  28.6 0.9 %copy-start.4 = (f32[2,1,64,316]{3,2,1,0:T(8,128)S(1)}, f32[2,1,64,316]{3,2,1,0:T(8,128)}, u32[]{:S(2)}) copy-start(f32[2,1,64,316]{3,2,1,0:T(8,128)} %param.13) | copy-start | bytes 485380
  30.4 2.2 %copy-start.1 = (bf16[32,2,2,128,128]{4,3,2,1,0:T(8,128)(2,1)S(1)}, bf16[32,2,2,128,128]{4,3,2,1,0:T(8,128)(2,1)}, u32[]{:S(2)}) copy-start(bf16[32,2,2,128,128]{4,3,2,1,0:T(8,128)(2,1)} %block_ref.1) | copy-start | bytes 12582916
  32.6 0.7 %copy-start.7 = (s32[32]{0:T(128)S(1)}, s32[32]{0:T(128)}, u32[]{:S(2)}) copy-start(s32[32]{0:T(128)} %pop_ref.5) | copy-start | bytes 388
  37.1 5.9 %collective-permute-start.11 = (f32[4,32,128]{2,1,0:T(8,128)S(1)}, f32[4,32,128]{2,1,0:T(8,128)S(1)}, u32[]{:S(2)}, u32[]{:S(2)}) collective-permute-start(f32[4,32,128]{2,1,0:T(8,128)S(1)} %shard_map.94), channel_id=1, source_target_pairs={{3,0},{0,1},{1,2},{2,3},{7,4},{4,5},{5,6},{6,7},{11,8},{8,9},{9,10... | collective-permute-start | bytes 196616 | tf_op jit(solution)/shard_map/ppermute | solution.py:277
  38.8 4.3 %collective-permute-start.10 = (f32[4,32,128]{2,1,0:T(8,128)S(1)}, f32[4,32,128]{2,1,0:T(8,128)S(1)}, u32[]{:S(2)}, u32[]{:S(2)}) collective-permute-start(f32[4,32,128]{2,1,0:T(8,128)S(1)} %shard_map.94), channel_id=1, source_target_pairs={{1,0},{2,1},{3,2},{0,3},{5,4},{6,5},{7,6},{4,7},{9,8},{10,9},{11,1... | collective-permute-start | bytes 196616 | tf_op jit(solution)/shard_map/ppermute | solution.py:277
  40.4 5.8 %collective-permute-start.9 = (f32[4,32,128]{2,1,0:T(8,128)S(1)}, f32[4,32,128]{2,1,0:T(8,128)S(1)}, u32[]{:S(2)}, u32[]{:S(2)}) collective-permute-start(f32[4,32,128]{2,1,0:T(8,128)S(1)} %shard_map.94), channel_id=1, source_target_pairs={{2,0},{3,1},{0,2},{1,3},{6,4},{7,5},{4,6},{5,7},{10,8},{11,9},{8,1... | collective-permute-start | bytes 196616 | tf_op jit(solution)/shard_map/ppermute | solution.py:277

commit v2 on v1

v2 whole, which is shorter than its diff:
```python
import jax
import jax.numpy as jnp
from jax import lax
from jax.experimental import pallas as pl
from jax.experimental.pallas import tpu as pltpu
from jax.sharding import PartitionSpec as P

F32 = jnp.float32
BF16 = jnp.bfloat16
NT = (((1,), (1,)), ((), ()))
NN = (((1,), (0,)), ((), ()))
VMEM = pl.BlockSpec(memory_space=pltpu.VMEM)
HBM = pl.BlockSpec(memory_space=pltpu.HBM)
XS = ZS = 4


def iota(shape, dim):
    return lax.broadcasted_iota(jnp.int32, shape, dim)


def dot(a, b, dims=NN):
    return lax.dot_general(a, b, dims, preferred_element_type=F32)


LINES = (
    ((0, False, False), (-1, False, True), (1, False, True), (2, True, False)),
    ((0, False, False), (1, False, True), (-1, False, True), (2, True, False)),
)
PLANES = (2, 3, 1)
REPS = (1, 3, 2)


def moved(chip, move, along_z):
    if along_z:
        return chip // ZS * ZS + (chip + move) % ZS
    return (chip + move) % (XS * ZS)


def box_perm(source):
    places = [(chip, core) for chip in range(XS * ZS) for core in range(2)]
    pairs = []
    for chip, core in places:
        from_chip, from_core = source(chip, core)
        pairs.append((from_chip * 2 + from_core, chip * 2 + core))
    return pairs


def from_line(step):
    def source(chip, core):
        move, along_z, cross = LINES[core][step]
        return moved(chip, move, along_z), 1 - core if cross else core

    return box_perm(source)


def from_plane(d):
    return box_perm(lambda chip, core: (moved(chip, d * ZS, False), core))


def from_core():
    return box_perm(lambda chip, core: (chip, 1 - core))


def column(row):
    boxes = row.shape[1]
    diagonal = iota((boxes, boxes), 0) == iota((boxes, boxes), 1)
    return jnp.sum(jnp.where(diagonal, row, 0).astype(F32), axis=1, keepdims=True).astype(jnp.int32)


def own_columns(tile, boxes):
    place = lax.axis_index("box")
    start = (place & (128 // boxes - 1)) * boxes
    moved = pltpu.roll(tile, lax.rem(128 - start, 128), 1)
    return jnp.transpose(moved.astype(F32))[:boxes].astype(jnp.int32)


def live_rows(pop_ref, boxes, slots):
    return iota((boxes, slots), 1) < column(pop_ref[...])


def pattern_kernel(
    pop_hbm, cur_hbm, rad_hbm, list_hbm, type_hbm, near_hbm, trans_hbm,
    pay_ref, pat_ref, masked_ref, pop_ref, list_ref, type_ref, near_ref, trans_ref,
    cur_ref, rad_ref, sems,
):
    lines, boxes, slots = cur_ref.shape
    place = lax.axis_index("box")
    tile = pl.multiple_of((place >> 2) * 128, 128)
    copies = [
        pltpu.make_async_copy(pop_hbm, pop_ref, sems.at[0]),
        pltpu.make_async_copy(cur_hbm, cur_ref, sems.at[1]),
        pltpu.make_async_copy(rad_hbm, rad_ref, sems.at[2]),
        pltpu.make_async_copy(list_hbm.at[:, pl.ds(tile, 128)], list_ref, sems.at[3]),
        pltpu.make_async_copy(type_hbm.at[:, pl.ds(tile, 128)], type_ref, sems.at[4]),
        pltpu.make_async_copy(near_hbm, near_ref, sems.at[5]),
        pltpu.make_async_copy(trans_hbm, trans_ref, sems.at[6]),
    ]
    for copy in copies:
        copy.start()
    copies[0].wait()
    live = live_rows(pop_ref, boxes, slots)
    copies[1].wait()
    masked = [jnp.where(live, cur_ref[j].astype(F32), 0.0) for j in range(lines)]
    for j in range(lines):
        pay_ref[:, (2 + j) * slots : (3 + j) * slots] = masked[j].astype(BF16)
        masked_ref[:, j * slots : (j + 1) * slots] = masked[j].astype(BF16)
    rows = jnp.concatenate(masked, axis=0)
    box_of_row = iota(rows.shape, 0) & (boxes - 1)
    copies[2].wait()
    total = jnp.zeros((lines * boxes, slots), F32)
    for b in range(0, boxes, 2):
        left = jnp.concatenate(
            [jnp.where(box_of_row == b + h, rows, 0.0).astype(BF16) for h in range(2)], axis=1
        )
        right = jnp.concatenate([rad_ref[b], rad_ref[b + 1]], axis=1)
        total = total + dot(left, right, NT)
    half = slots // 2
    sign = jnp.where(iota((boxes, slots), 1) < half, -1.0, 1.0)
    for i in range(2):
        real = total[i * boxes : (i + 1) * boxes]
        imag = total[(2 + i) * boxes : (3 + i) * boxes]
        out = real + sign * pltpu.roll(imag, half, 1)
        pay_ref[:, i * slots : (i + 1) * slots] = out.astype(BF16)
        pat_ref[:, i * slots : (i + 1) * slots] = out.astype(BF16)
    for copy in copies[3:]:
        copy.wait()


def coef_kernel(
    type_ref, trans_ref, pat_ref, block_hbm, coef_ref, pass_ref, block_ref, table_ref, sem
):
    fetch = pltpu.make_async_copy(block_hbm, block_ref, sem)
    fetch.start()
    far = type_ref.shape[0]
    boxes = pat_ref.shape[0]
    half, types = trans_ref.shape[1:]
    wide = table_ref.shape[2]
    pass_ref[...] = pat_ref[...]
    table_ref[...] = jnp.zeros_like(table_ref)
    for c in range(2):
        value = trans_ref[c]
        high = value.astype(BF16)
        low = (value - high.astype(F32)).astype(BF16)
        for k in range(2):
            place = pl.ds((2 * c + k) * half, half)
            table_ref[0, place, :types] = high
            table_ref[1, place, :types] = low
    lane = iota((boxes, wide), 1)
    kinds = own_columns(type_ref[...], boxes)
    pieces = []
    for f in range(far):
        pieces.append(jnp.where(lane == kinds[:, f : f + 1], 1.0, 0.0).astype(BF16))
    hot = jnp.concatenate(pieces, axis=0)
    coef_ref[...] = dot(hot, table_ref[0], NT) + dot(hot, table_ref[1], NT)
    fetch.wait()


def box_ids(boxes, theirs):
    place = lax.axis_index("box")
    core, chip = place & 1, place >> 1
    holder = 1 - core if theirs else core
    lane = iota((1, XS * ZS * boxes), 1)
    plane = lane // (ZS * boxes)
    slot = (lane // boxes) & (ZS - 1)
    first = jnp.full(lane.shape, 0, jnp.int32)
    for step in range(ZS):
        at = []
        for move, along_z, _ in (LINES[0][step], LINES[1][step]):
            at.append((chip & ~3) + ((chip + move) & 3) if along_z else (chip + move) & 15)
        first = jnp.where(slot == step, jnp.where(holder == 0, at[0], at[1]), first)
    shift = jnp.zeros_like(lane)
    for j, d in enumerate(PLANES):
        shift = jnp.where(plane == j + 1, d * ZS, shift)
    cross = jnp.where((slot == 1) | (slot == 2), 1, 0)
    return ((((first + shift) & 15) * 2 + (holder ^ cross)) * boxes) + (lane & (boxes - 1))


def translate(listed, ids, coef_ref, source_ref, acc):
    boxes, far = listed.shape
    slots = coef_ref.shape[1] // 2
    group = 8
    for f in range(0, far, group):
        hot = jnp.concatenate(
            [
                jnp.where(ids == listed[:, g : g + 1], 1.0, 0.0).astype(BF16)
                for g in range(f, f + group)
            ],
            axis=0,
        )
        source = dot(hot, source_ref[...])
        for g in range(group):
            rows = slice(g * boxes, (g + 1) * boxes)
            at = (f + g) * boxes
            straight = coef_ref[at : at + boxes, :slots]
            crossed = coef_ref[at : at + boxes, slots:]
            for i in range(2):
                value = source[rows, i * slots : (i + 1) * slots]
                acc[2 * i] = acc[2 * i] + straight * value
                acc[2 * i + 1] = acc[2 * i + 1] + crossed * value
    return acc


def near_kernel(
    list_ref, own_ref, core_ref, next_ref, held_ref, block_ref, out_ref, pass_ref
):
    pairs, boxes = list_ref.shape
    slots = out_ref.shape[1]
    lines = own_ref.shape[1] // slots
    pass_ref[...] = held_ref[...]
    place = lax.axis_index("box")
    core = place & 1
    beyond = place + 2 * core - 1
    lane = iota((boxes, slots), 1)
    first = jnp.where(
        lane < boxes,
        place * boxes,
        jnp.where(lane < 2 * boxes, (place + 1 - 2 * core) * boxes, beyond * boxes),
    )
    ids = jnp.where(lane < 3 * boxes, first + (lane & (boxes - 1)), -1000000)
    hot = jnp.concatenate(
        [
            jnp.where(ids == column(list_ref[n : n + 1, :]), 1.0, 0.0).astype(BF16)
            for n in range(pairs)
        ],
        axis=0,
    )
    zero = jnp.zeros((slots - 3 * boxes, lines * slots), BF16)
    source = jnp.concatenate([own_ref[...], core_ref[...], next_ref[...], zero], axis=0)
    found = dot(hot, source)
    picked = [found[:, j * slots : (j + 1) * slots] for j in range(lines)]
    box_of_row = iota((lines * boxes, slots), 0) & (boxes - 1)
    lefts = []
    for n in range(pairs):
        part = [value[n * boxes : (n + 1) * boxes] for value in picked]
        lefts.append(jnp.concatenate(part, axis=0))
        lefts.append(jnp.concatenate([-part[2], -part[3], part[0], part[1]], axis=0))
    total = jnp.zeros((lines * boxes, slots), F32)
    for b in range(boxes):
        mine = box_of_row == b
        for n in range(pairs):
            left = jnp.concatenate(
                [jnp.where(mine, lefts[2 * n + c], 0.0).astype(BF16) for c in range(2)], axis=1
            )
            right = jnp.concatenate([block_ref[b, n, 0], block_ref[b, n, 1]], axis=1)
            total = total + dot(left, right, NT)
    out_ref[...] = total


def mine_kernel(list_ref, coef_ref, mine_ref, acc_ref):
    boxes, slots = acc_ref.shape[1:]
    listed = own_columns(list_ref[...], boxes)
    ids = box_ids(boxes, False)
    acc = [jnp.zeros((boxes, slots), F32) for _ in range(4)]
    acc = translate(listed, ids, coef_ref, mine_ref, acc)
    for j in range(4):
        acc_ref[j] = acc[j]


def far_kernel(
    pop_ref, list_ref, coef_ref, near_ref, acc_ref, theirs_ref, receive_ref, out_ref
):
    boxes, slots = receive_ref.shape[0], receive_ref.shape[2]
    listed = own_columns(list_ref[...], boxes)
    ids = box_ids(boxes, True)
    acc = translate(listed, ids, coef_ref, theirs_ref, [acc_ref[j] for j in range(4)])
    half = slots // 2
    low = iota((boxes, slots), 1) < half
    minus = jnp.where(low, -1.0, 1.0)
    reals, imags = [], []
    for i in range(2):
        incoming = acc[2 * i] + minus * pltpu.roll(acc[2 * i + 1], half, 1)
        reals.append(-minus * incoming)
        imags.append(pltpu.roll(incoming, half, 1))
    exact = jnp.concatenate(reals + imags, axis=0)
    high = exact.astype(BF16).astype(F32)
    left_rows = jnp.concatenate([high, exact - high], axis=0)
    box_of_row = iota(left_rows.shape, 0) & (boxes - 1)
    total = jnp.zeros(left_rows.shape, F32)
    for b in range(0, boxes, 2):
        left = jnp.concatenate(
            [jnp.where(box_of_row == b + h, left_rows, 0.0).astype(BF16) for h in range(2)], axis=1
        )
        right = jnp.concatenate([receive_ref[b], receive_ref[b + 1]], axis=0)
        total = total + dot(left, right)
    total = (total[: 4 * boxes] + total[4 * boxes :]) + near_ref[...]
    live = live_rows(pop_ref, boxes, slots)
    for j in range(4):
        out_ref[j] = jnp.where(live, total[j * boxes : (j + 1) * boxes], 0.0)


def call(kernel, out_shape, specs, out_specs, scratch=(), flops=0, size=0):
    return pl.pallas_call(
        kernel,
        out_shape=out_shape,
        in_specs=specs,
        out_specs=out_specs,
        scratch_shapes=list(scratch),
        cost_estimate=pl.CostEstimate(flops=flops, bytes_accessed=size, transcendentals=0),
        compiler_params=pltpu.CompilerParams(vmem_limit_bytes=32 * 1024 * 1024),
    )


def stay(array):
    return pltpu.with_memory_space_constraint(array, pltpu.HBM)


def body(
    currents, populations, radiate, receive, translation, far_list, far_type, near_list, near_block
):
    incs, boxes, slots = currents.shape[1:]
    lines = 2 * incs
    half = radiate.shape[3]
    far = far_list.shape[1]
    types = translation.shape[3]
    pairs = near_list.shape[1]
    wide = incs * slots
    shape = jax.ShapeDtypeStruct

    payload, pattern, masked, pop, listed, kinds, partners, trans = call(
        pattern_kernel,
        (
            shape((boxes, wide + lines * slots), BF16),
            shape((boxes, wide), BF16),
            shape((boxes, lines * slots), BF16),
            shape((1, boxes), jnp.int32),
            shape((far, 128), jnp.int32),
            shape((far, 128), jnp.int32),
            shape((pairs, boxes), jnp.int32),
            shape((2, half, types), F32),
        ),
        [HBM] * 7,
        (VMEM,) * 8,
        [
            pltpu.VMEM((lines, boxes, slots), BF16),
            pltpu.VMEM((boxes, 2 * half, slots), BF16),
            pltpu.SemaphoreType.DMA((7,)),
        ],
        flops=2 * 128 * 4096 * 128,
        size=1 << 20,
    )(
        stay(populations.reshape(1, boxes)),
        stay(currents.reshape(lines, boxes, slots)),
        stay(radiate.reshape(boxes, 2 * half, slots)),
        stay(far_list.T),
        stay(far_type.T),
        stay(near_list.T),
        stay(translation.reshape(2, half, types)),
    )

    third = lax.ppermute(pattern, "box", from_line(2))
    second = lax.ppermute(payload, "box", from_line(1))
    fourth = lax.ppermute(pattern, "box", from_line(3))
    near_core = lax.ppermute(masked, "box", from_core())

    padded = -(-types // 128) * 128
    coef, pattern, block = call(
        coef_kernel,
        (
            shape((far * boxes, 2 * slots), F32),
            shape(pattern.shape, BF16),
            pltpu.VMEM(near_block.shape, BF16),
        ),
        [VMEM] * 3 + [HBM],
        (VMEM,) * 3,
        [pltpu.VMEM((2, 4 * half, padded), BF16), pltpu.SemaphoreType.DMA(())],
        flops=4 * far * boxes * padded * 2 * slots,
        size=4 << 20,
    )(kinds, trans, pattern, stay(near_block))

    held = jnp.concatenate([pattern, second[:, :wide], third, fourth], axis=0)
    planes = [lax.ppermute(held, "box", from_plane(d)) for d in PLANES]

    near, held = call(
        near_kernel,
        (shape((lines * boxes, slots), F32), shape(held.shape, BF16)),
        [VMEM] * 6,
        (VMEM, VMEM),
        flops=2 * 128 * near_block.size // 128 * 128,
        size=near_block.size,
    )(partners, masked, near_core, second[:, wide:], held, block)

    mine = jnp.concatenate([held] + planes, axis=0)
    theirs = lax.ppermute(mine, "box", from_core())
    acc = call(
        mine_kernel,
        shape((lines, boxes, slots), F32),
        [VMEM] * 3,
        VMEM,
        flops=1024 * 1024 * 256,
        size=2 << 20,
    )(listed, coef, mine)

    part = call(
        far_kernel,
        shape((lines, boxes, slots), F32),
        [VMEM] * 7,
        VMEM,
        flops=1024 * 1024 * 256,
        size=4 << 20,
    )(pop, listed, coef, near, acc, theirs, receive.reshape(boxes, 2 * half, slots))

    reps = lax.axis_size("rep")
    others = {
        d: lax.ppermute(part, "rep", [(r ^ d, r) for r in range(reps)]) for d in REPS
    }
    total = (part + others[1]) + (others[2] + others[3])
    return total.reshape(2, incs, boxes, slots)


def solution(mesh):
    return jax.shard_map(
        body,
        mesh=mesh,
        in_specs=(
            P(None, None, "box", None),
            P("box"),
            P("box", None, "rep", None, None),
            P("box", None, "rep", None, None),
            P(None, "rep", None, None),
            P(),
            P(),
            P("box", "rep"),
            P("box", "rep", None, None, None),
        ),
        out_specs=P(None, None, "box", None),
        check_vma=False,
    )
```

time: 47.2 us -> 32.9 us (0.70)
  local copies, waits for them, and re-layouts: 8.25 us -> 0.04 us
  starting transfers between devices: 21.8 us -> 15.6 us
  waiting for transfers between devices: 10.4 us -> 8.22 us
  Pallas kernels: 5.65 us -> 7.64 us
    unnamed x24 -> x5, local copies, waits for them, and re-layouts: 7.38 us -> 0.02 us
    ppermute x10 -> x9, starting transfers between devices: 21.8 us -> 14.8 us  [the longest x1 5.84 us: body(): second = lax.ppermute(payload, 'box', from_line(1))]
    ppermute x10 -> x9, waiting for transfers between devices: 10.4 us -> 7.4 us  [the longest x3 4.22 us: body(): lax.ppermute(part, 'rep', [(r ^ d, r) for r in range(reps)])]
    pallas_call x4 -> x5, Pallas kernels: 5.65 us -> 7.64 us  [the longest x1 2.21 us: body(): call(coef_kernel, (shape((far * boxes, 2 * slots), F32), shape(pattern.sh...]
    dynamic_slice x2 -> x0, local copies, waits for them, and re-layouts: 0.86 us -> none  [the longest x1 0.79 us: body(): own_type = lax.dynamic_slice_in_dim(far_type, place * boxes, boxes, 0)]
    ppermute x1, waiting for transfers between devices: 0.01 us -> 0.82 us  [body(): theirs = lax.ppermute(mine, 'box', from_core())]
    ppermute x1, starting transfers between devices: 0.01 us -> 0.76 us  [body(): near_core = lax.ppermute(masked, 'box', from_core())]
  transfers between devices with their start and end apart: 12 -> 11, of which waited for: 7 -> 8; matrix products, arithmetic and copies ran while one was open for 4% -> 0% of each run, Pallas kernels for 6% -> 13%
where the time goes in v2:
time: 32.9 us; the launch traced here: 32.3 us
  starting transfers between devices  15.6 us (47%)
  waiting for transfers between devices  8.22 us (25%)
  Pallas kernels  7.64 us (23%)
  other arithmetic  0.65 us (2%)
    ppermute x1, starting transfers between devices, body(): second = lax.ppermute(payload, 'box', from_line(1))  5.84 us
    ppermute x3, starting transfers between devices, body(): lax.ppermute(part, 'rep', [(r ^ d, r) for r in range(reps)])  4.78 us
    ppermute x3, waiting for transfers between devices, body(): lax.ppermute(part, 'rep', [(r ^ d, r) for r in range(reps)])  4.22 us
    ppermute x3, starting transfers between devices, body(): planes = [lax.ppermute(held, 'box', from_plane(d)) for d in PLANES]  4.14 us
    pallas_call x1, Pallas kernels, body(): call(coef_kernel, (shape((far * boxes, 2 * slots), F32), shape(pattern.sh...  2.21 us
    ppermute x1, waiting for transfers between devices, body(): fourth = lax.ppermute(pattern, 'box', from_line(3))  2.08 us
    pallas_call x1, Pallas kernels, body(): call(pattern_kernel, (shape((boxes, wide + lines * slots), BF16), shape((...  1.83 us
    pallas_call x1, Pallas kernels, body(): call(far_kernel, shape((lines, boxes, slots), F32), [VMEM] * 7, VMEM, flo...  1.5 us
  transfers between devices with their start and end apart: 11, of which 8 were waited for; matrix products, arithmetic and copies ran while one was open for 0% of the time, Pallas kernels for 13%

profile of v2, /device:TPU:0, one launch (start us, length us, event | category | flops | bytes accessed | tf_op | source)
XLA Modules:
  0.0 32.3 jit_solution(16904256414427724570)
XLA Ops:
  0.0 1.8 %shard_map.91 = (bf16[32,768]{1,0:T(8,128)(2,1)S(1)}, bf16[32,256]{1,0:T(8,128)(2,1)S(1)}, bf16[32,512]{1,0:T(8,128)(2,1)S(1)}, s32[1,32]{1,0:T(1,128)S(1)}, s32...) custom-call(s32[1,32]{1,0:T(1,128)} %bitcast.16, ...), custom_call_target="tpu_custom_call" | custom-call | flops 134217728 | bytes 1048576 | tf_op jit(solution)/shard_map/pallas_call | solution.py:319
  1.8 5.8 %collective-permute-start.1 = (bf16[32,768]{1,0:T(8,128)(2,1)S(1)}, bf16[32,768]{1,0:T(8,128)(2,1)S(1)}, u32[]{:S(2)}, u32[]{:S(2)}) collective-permute-start(bf16[32,768]{1,0:T(8,128)(2,1)S(1)} %get-tuple-element.26), channel_id=1, source_target_pairs={{124,0},{8,4},{4,8},{16,12},{12,16},{24,20},{20,24},{32,28},{28,32... | collective-permute-start | bytes 147464 | tf_op jit(solution)/shard_map/ppermute | solution.py:351
  7.7 0.8 %collective-permute-start = (bf16[32,512]{1,0:T(8,128)(2,1)S(1)}, bf16[32,512]{1,0:T(8,128)(2,1)S(1)}, u32[]{:S(2)}, u32[]{:S(2)}) collective-permute-start(bf16[32,512]{1,0:T(8,128)(2,1)S(1)} %get-tuple-element.25.own_ref), channel_id=1, source_target_pairs={{4,0},{0,4},{12,8},{8,12},{20,16},{16,20},{28,24},{24,28},{36,32},... | collective-permute-start | bytes 98312 | tf_op jit(solution)/shard_map/ppermute | solution.py:353
  8.4 2.2 %shard_map.92 = (f32[1024,256]{1,0:T(8,128)S(1)}, bf16[32,256]{1,0:T(8,128)(2,1)S(1)}, bf16[32,2,2,128,128]{4,3,2,1,0:T(8,128)(2,1)S(1)}) custom-call(s32[32,128]{1,0:T(8,128)S(1)} %get-tuple-element.20.type_ref, f32[2,64,316]{2,1,0:T(8,128)S(1)} %get-tuple-element.21.trans_ref, bf16[32,256]{1,0:T(8,128)(2,1)S(1)} %get-tuple-element.22.pat_ref, ...), custom_call_target="tpu_custom_call" | custom-call | flops 402653184 | bytes 4194304 | tf_op jit(solution)/shard_map/pallas_call | solution.py:356
  10.7 0.0 copy-start
  10.7 0.1 collective-permute-done.2
  10.8 2.1 %collective-permute-done.3 = bf16[32,256]{1,0:T(8,128)(2,1)S(1)} collective-permute-done((bf16[32,256]{1,0:T(8,128)(2,1)S(1)}, bf16[32,256]{1,0:T(8,128)(2,1)S(1)}, u32[]{:S(2)}, u32[]{:S(2)}) %collective-permute-start.3) | collective-permute-done | bytes 16416 | tf_op jit(solution)/shard_map/ppermute | solution.py:352
  12.9 0.9 %collective-permute-start.4 = (bf16[128,256]{1,0:T(8,128)(2,1)S(1)}, bf16[128,256]{1,0:T(8,128)(2,1)S(1)}, u32[]{:S(2)}, u32[]{:S(2)}) collective-permute-start(bf16[128,256]{1,0:T(8,128)(2,1)S(1)} %pad_maximum_fusion.held_ref), channel_id=1, source_target_pairs={{64,0},{68,4},{72,8},{76,12},{80,16},{84,20},{88,24},{92,28},{96,3... | collective-permute-start | bytes 196616 | tf_op jit(solution)/shard_map/ppermute | solution.py:371
  13.8 0.8 %collective-permute-start.5 = (bf16[128,256]{1,0:T(8,128)(2,1)S(1)}, bf16[128,256]{1,0:T(8,128)(2,1)S(1)}, u32[]{:S(2)}, u32[]{:S(2)}) collective-permute-start(bf16[128,256]{1,0:T(8,128)(2,1)S(1)} %pad_maximum_fusion.held_ref), channel_id=1, source_target_pairs={{96,0},{100,4},{104,8},{108,12},{112,16},{116,20},{120,24},{124,28... | collective-permute-start | bytes 196616 | tf_op jit(solution)/shard_map/ppermute | solution.py:371
  14.6 2.5 %collective-permute-start.6 = (bf16[128,256]{1,0:T(8,128)(2,1)S(1)}, bf16[128,256]{1,0:T(8,128)(2,1)S(1)}, u32[]{:S(2)}, u32[]{:S(2)}) collective-permute-start(bf16[128,256]{1,0:T(8,128)(2,1)S(1)} %pad_maximum_fusion.held_ref), channel_id=1, source_target_pairs={{32,0},{36,4},{40,8},{44,12},{48,16},{52,20},{56,24},{60,28},{64,3... | collective-permute-start | bytes 196616 | tf_op jit(solution)/shard_map/ppermute | solution.py:371
  17.1 1.4 %shard_map.93 = (f32[128,128]{1,0:T(8,128)S(1)}, bf16[128,256]{1,0:T(8,128)(2,1)S(1)}) custom-call(s32[2,32]{1,0:T(2,128)S(1)} %get-tuple-element.24.list_ref, bf16[32,512]{1,0:T(8,128)(2,1)S(1)} %get-tuple-element.25.own_ref, bf16[32,512]{1,0:T(8,128)(2,1)S(1)} %collective-permute-done.core_ref, bf16[32,512]{1,0:T(8,128)(2,1)S(1)} %slice.8.next_ref, ...), custom_call_target="tpu_custom_call" | custom-call | flops 536870912 | bytes 2097152 | tf_op jit(solution)/shard_map/pallas_call | solution.py:373
  18.5 0.3 collective-permute-done.4
  18.8 0.7 %collective-permute-done.5 = bf16[128,256]{1,0:T(8,128)(2,1)S(1)} collective-permute-done((bf16[128,256]{1,0:T(8,128)(2,1)S(1)}, bf16[128,256]{1,0:T(8,128)(2,1)S(1)}, u32[]{:S(2)}, u32[]{:S(2)}) %collective-permute-start.5) | collective-permute-done | bytes 65568 | tf_op jit(solution)/shard_map/ppermute | solution.py:371
  19.5 0.1 collective-permute-start.7
  19.6 0.7 %shard_map.94.acc_ref = f32[4,32,128]{2,1,0:T(8,128)S(1)} custom-call(s32[32,128]{1,0:T(8,128)S(1)} %get-tuple-element.19.list_ref, f32[1024,256]{1,0:T(8,128)S(1)} %get-tuple-element.23.coef_ref, bf16[512,256]{1,0:T(8,128)(2,1)S(1)} %constant_dynamic-update-slice_fusion.mine_ref), custom_call_target="tpu_custom_call" | custom-call | flops 268435456 | bytes 2097152 | tf_op jit(solution)/shard_map/pallas_call | solution.py:384
  20.3 0.8 %collective-permute-done.7.theirs_ref = bf16[512,256]{1,0:T(8,128)(2,1)S(1)} collective-permute-done((bf16[512,256]{1,0:T(8,128)(2,1)S(1)}, bf16[512,256]{1,0:T(8,128)(2,1)S(1)}, u32[]{:S(2)}, u32[]{:S(2)}) %collective-permute-start.7) | collective-permute-done | bytes 262176 | tf_op jit(solution)/shard_map/ppermute | solution.py:383
  21.1 1.5 %shard_map.95 = f32[4,32,128]{2,1,0:T(8,128)S(1)} custom-call(s32[1,32]{1,0:T(1,128)S(1)} %get-tuple-element.18.pop_ref, s32[32,128]{1,0:T(8,128)S(1)} %get-tuple-element.19.list_ref, f32[1024,256]{1,0:T(8,128)S(1)} %get-tuple-element.23.coef_ref, f32[128,128]{1,0:T(8,128)S(1)} %get-tuple-element.29.near_ref, f32[4,32,128]{2,1,0:T(8,128)S(1)} %shard_map.94.acc_ref, ...), custom_call_target="tpu_custom_call" | custom-call | flops 268435456 | bytes 4194304 | tf_op jit(solution)/shard_map/pallas_call | solution.py:393
  22.6 3.1 %collective-permute-start.10 = (f32[4,32,128]{2,1,0:T(8,128)S(1)}, f32[4,32,128]{2,1,0:T(8,128)S(1)}, u32[]{:S(2)}, u32[]{:S(2)}) collective-permute-start(f32[4,32,128]{2,1,0:T(8,128)S(1)} %shard_map.95), channel_id=1, source_target_pairs={{3,0},{2,1},{1,2},{0,3},{7,4},{6,5},{5,6},{4,7},{11,8},{10,9},{9,1... | collective-permute-start | bytes 196616 | tf_op jit(solution)/shard_map/ppermute | solution.py:404
  25.7 0.1 collective-permute-start.8
  25.8 1.5 %collective-permute-start.9 = (f32[4,32,128]{2,1,0:T(8,128)S(1)}, f32[4,32,128]{2,1,0:T(8,128)S(1)}, u32[]{:S(2)}, u32[]{:S(2)}) collective-permute-start(f32[4,32,128]{2,1,0:T(8,128)S(1)} %shard_map.95), channel_id=1, source_target_pairs={{2,0},{3,1},{0,2},{1,3},{6,4},{7,5},{4,6},{5,7},{10,8},{11,9},{8,1... | collective-permute-start | bytes 196616 | tf_op jit(solution)/shard_map/ppermute | solution.py:404
  27.4 0.8 %collective-permute-done.10 = f32[4,32,128]{2,1,0:T(8,128)S(1)} collective-permute-done((f32[4,32,128]{2,1,0:T(8,128)S(1)}, f32[4,32,128]{2,1,0:T(8,128)S(1)}, u32[]{:S(2)}, u32[]{:S(2)}) %collective-permute-start.10) | collective-permute-done | bytes 65568 | tf_op jit(solution)/shard_map/ppermute | solution.py:404
  28.2 2.1 %collective-permute-done.8 = f32[4,32,128]{2,1,0:T(8,128)S(1)} collective-permute-done((f32[4,32,128]{2,1,0:T(8,128)S(1)}, f32[4,32,128]{2,1,0:T(8,128)S(1)}, u32[]{:S(2)}, u32[]{:S(2)}) %collective-permute-start.8) | collective-permute-done | bytes 65568 | tf_op jit(solution)/shard_map/ppermute | solution.py:404
  30.2 1.4 %collective-permute-done.9 = f32[4,32,128]{2,1,0:T(8,128)S(1)} collective-permute-done((f32[4,32,128]{2,1,0:T(8,128)S(1)}, f32[4,32,128]{2,1,0:T(8,128)S(1)}, u32[]{:S(2)}, u32[]{:S(2)}) %collective-permute-start.9) | collective-permute-done | bytes 65568 | tf_op jit(solution)/shard_map/ppermute | solution.py:404
  31.6 0.6 %add_add_fusion = f32[4,32,128]{2,1,0:T(8,128)} fusion(f32[4,32,128]{2,1,0:T(8,128)S(1)} %collective-permute-done.9, f32[4,32,128]{2,1,0:T(8,128)S(1)} %collective-permute-done.10, f32[4,32,128]{2,1,0:T(8,128)S(1)} %shard_map.95, f32[4,32,128]{2,1,0:T(8,128)S(1)} %collective-permute-done.8), kind=kLoop, calls=%fused_computation.1 | loop fusion | flops 49152 | bytes 327680 | tf_op jit(solution)/shard_map/add | solution.py:406
  (13 shorter events, 0.1 us)
Async XLA Ops:
  1.8 8.8 %collective-permute-start.1 = (bf16[32,768]{1,0:T(8,128)(2,1)S(1)}, bf16[32,768]{1,0:T(8,128)(2,1)S(1)}, u32[]{:S(2)}, u32[]{:S(2)}) collective-permute-start(bf16[32,768]{1,0:T(8,128)(2,1)S(1)} %get-tuple-element.26), channel_id=1, source_target_pairs={{124,0},{8,4},{4,8},{16,12},{12,16},{24,20},{20,24},{32,28},{28,32... | collective-permute-start | bytes 147464 | tf_op jit(solution)/shard_map/ppermute | solution.py:351
  7.7 3.2 %collective-permute-start.2 = (bf16[32,256]{1,0:T(8,128)(2,1)S(1)}, bf16[32,256]{1,0:T(8,128)(2,1)S(1)}, u32[]{:S(2)}, u32[]{:S(2)}) collective-permute-start(bf16[32,256]{1,0:T(8,128)(2,1)S(1)} %get-tuple-element.22.pat_ref), channel_id=1, source_target_pairs={{12,0},{120,4},{20,8},{0,12},{28,16},{8,20},{36,24},{16,28},{44,32... | collective-permute-start | bytes 49160 | tf_op jit(solution)/shard_map/ppermute | solution.py:350
  7.7 5.2 %collective-permute-start.3 = (bf16[32,256]{1,0:T(8,128)(2,1)S(1)}, bf16[32,256]{1,0:T(8,128)(2,1)S(1)}, u32[]{:S(2)}, u32[]{:S(2)}) collective-permute-start(bf16[32,256]{1,0:T(8,128)(2,1)S(1)} %get-tuple-element.22.pat_ref), channel_id=1, source_target_pairs={{16,0},{20,4},{24,8},{28,12},{0,16},{4,20},{8,24},{12,28},{48,32},... | collective-permute-start | bytes 49160 | tf_op jit(solution)/shard_map/ppermute | solution.py:352
  7.7 9.4 %collective-permute-start = (bf16[32,512]{1,0:T(8,128)(2,1)S(1)}, bf16[32,512]{1,0:T(8,128)(2,1)S(1)}, u32[]{:S(2)}, u32[]{:S(2)}) collective-permute-start(bf16[32,512]{1,0:T(8,128)(2,1)S(1)} %get-tuple-element.25.own_ref), channel_id=1, source_target_pairs={{4,0},{0,4},{12,8},{8,12},{20,16},{16,20},{28,24},{24,28},{36,32},... | collective-permute-start | bytes 98312 | tf_op jit(solution)/shard_map/ppermute | solution.py:353
  10.7 10.4 %copy-start = (bf16[32,2,1,64,128]{4,3,2,1,0:T(8,128)(2,1)S(1)}, bf16[32,2,1,64,128]{4,3,2,1,0:T(8,128)(2,1)}, u32[]{:S(2)}) copy-start(bf16[32,2,1,64,128]{4,3,2,1,0:T(8,128)(2,1)} %param.12) | copy-start | bytes 3145732
  12.9 5.8 %collective-permute-start.4 = (bf16[128,256]{1,0:T(8,128)(2,1)S(1)}, bf16[128,256]{1,0:T(8,128)(2,1)S(1)}, u32[]{:S(2)}, u32[]{:S(2)}) collective-permute-start(bf16[128,256]{1,0:T(8,128)(2,1)S(1)} %pad_maximum_fusion.held_ref), channel_id=1, source_target_pairs={{64,0},{68,4},{72,8},{76,12},{80,16},{84,20},{88,24},{92,28},{96,3... | collective-permute-start | bytes 196616 | tf_op jit(solution)/shard_map/ppermute | solution.py:371
  13.8 5.6 %collective-permute-start.5 = (bf16[128,256]{1,0:T(8,128)(2,1)S(1)}, bf16[128,256]{1,0:T(8,128)(2,1)S(1)}, u32[]{:S(2)}, u32[]{:S(2)}) collective-permute-start(bf16[128,256]{1,0:T(8,128)(2,1)S(1)} %pad_maximum_fusion.held_ref), channel_id=1, source_target_pairs={{96,0},{100,4},{104,8},{108,12},{112,16},{116,20},{120,24},{124,28... | collective-permute-start | bytes 196616 | tf_op jit(solution)/shard_map/ppermute | solution.py:371
  14.6 4.8 %collective-permute-start.6 = (bf16[128,256]{1,0:T(8,128)(2,1)S(1)}, bf16[128,256]{1,0:T(8,128)(2,1)S(1)}, u32[]{:S(2)}, u32[]{:S(2)}) collective-permute-start(bf16[128,256]{1,0:T(8,128)(2,1)S(1)} %pad_maximum_fusion.held_ref), channel_id=1, source_target_pairs={{32,0},{36,4},{40,8},{44,12},{48,16},{52,20},{56,24},{60,28},{64,3... | collective-permute-start | bytes 196616 | tf_op jit(solution)/shard_map/ppermute | solution.py:371
  19.5 1.6 %collective-permute-start.7 = (bf16[512,256]{1,0:T(8,128)(2,1)S(1)}, bf16[512,256]{1,0:T(8,128)(2,1)S(1)}, u32[]{:S(2)}, u32[]{:S(2)}) collective-permute-start(bf16[512,256]{1,0:T(8,128)(2,1)S(1)} %constant_dynamic-update-slice_fusion.mine_ref), channel_id=1, source_target_pairs={{4,0},{0,4},{12,8},{8,12},{20,16},{16,20},{28,24},{24,28},{36,32},... | collective-permute-start | bytes 786440 | tf_op jit(solution)/shard_map/ppermute | solution.py:383
  22.6 5.6 %collective-permute-start.10 = (f32[4,32,128]{2,1,0:T(8,128)S(1)}, f32[4,32,128]{2,1,0:T(8,128)S(1)}, u32[]{:S(2)}, u32[]{:S(2)}) collective-permute-start(f32[4,32,128]{2,1,0:T(8,128)S(1)} %shard_map.95), channel_id=1, source_target_pairs={{3,0},{2,1},{1,2},{0,3},{7,4},{6,5},{5,6},{4,7},{11,8},{10,9},{9,1... | collective-permute-start | bytes 196616 | tf_op jit(solution)/shard_map/ppermute | solution.py:404
  25.7 4.5 %collective-permute-start.8 = (f32[4,32,128]{2,1,0:T(8,128)S(1)}, f32[4,32,128]{2,1,0:T(8,128)S(1)}, u32[]{:S(2)}, u32[]{:S(2)}) collective-permute-start(f32[4,32,128]{2,1,0:T(8,128)S(1)} %shard_map.95), channel_id=1, source_target_pairs={{1,0},{0,1},{3,2},{2,3},{5,4},{4,5},{7,6},{6,7},{9,8},{8,9},{11,10... | collective-permute-start | bytes 196616 | tf_op jit(solution)/shard_map/ppermute | solution.py:404
  25.8 5.8 %collective-permute-start.9 = (f32[4,32,128]{2,1,0:T(8,128)S(1)}, f32[4,32,128]{2,1,0:T(8,128)S(1)}, u32[]{:S(2)}, u32[]{:S(2)}) collective-permute-start(f32[4,32,128]{2,1,0:T(8,128)S(1)} %shard_map.95), channel_id=1, source_target_pairs={{2,0},{3,1},{0,2},{1,3},{6,4},{7,5},{4,6},{5,7},{10,8},{11,9},{8,1... | collective-permute-start | bytes 196616 | tf_op jit(solution)/shard_map/ppermute | solution.py:404

commit v3 on v2

--- a/solution.py
+++ b/solution.py
@@ -22,10 +22,14 @@
     return lax.dot_general(a, b, dims, preferred_element_type=F32)
 
 
-LINES = (
-    ((0, False, False), (-1, False, True), (1, False, True), (2, True, False)),
-    ((0, False, False), (1, False, True), (-1, False, True), (2, True, False)),
-)
+MOVES = {
+    "own": ((0, False, False), (0, False, False)),
+    "next": ((-1, False, True), (1, False, True)),
+    "back": ((1, False, True), (-1, False, True)),
+    "across": ((2, True, False), (2, True, False)),
+}
+ORDER = ("own", "next", "across", "back")
+LINES = tuple(tuple(MOVES[name][core] for name in ORDER) for core in range(2))
 PLANES = (2, 3, 1)
 REPS = (1, 3, 2)
 
@@ -129,7 +133,7 @@
 def coef_kernel(
     type_ref, trans_ref, pat_ref, block_hbm, coef_ref, pass_ref, block_ref, table_ref, sem
 ):
-    fetch = pltpu.make_async_copy(block_hbm, block_ref, sem)
+    fetch = pltpu.make_async_copy(block_hbm.at[pl.ds(0, block_ref.shape[0])], block_ref, sem)
     fetch.start()
     far = type_ref.shape[0]
     boxes = pat_ref.shape[0]
@@ -171,7 +175,10 @@
     shift = jnp.zeros_like(lane)
     for j, d in enumerate(PLANES):
         shift = jnp.where(plane == j + 1, d * ZS, shift)
-    cross = jnp.where((slot == 1) | (slot == 2), 1, 0)
+    cross = jnp.zeros_like(lane)
+    for step in range(ZS):
+        if LINES[0][step][2]:
+            cross = jnp.where(slot == step, 1, cross)
     return ((((first + shift) & 15) * 2 + (holder ^ cross)) * boxes) + (lane & (boxes - 1))
 
 
@@ -200,9 +207,35 @@
     return acc
 
 
+def add_near(total, found, block_ref, start):
+    lines, pairs = 4, block_ref.shape[1]
+    boxes, slots = found.shape[0] // pairs, found.shape[1] // lines
+    box_of_row = iota((lines * boxes, slots), 0) & (boxes - 1)
+    lefts = []
+    for n in range(pairs):
+        part = [
+            found[n * boxes : (n + 1) * boxes, j * slots : (j + 1) * slots] for j in range(lines)
+        ]
+        lefts.append(jnp.concatenate(part, axis=0))
+        lefts.append(jnp.concatenate([-part[2], -part[3], part[0], part[1]], axis=0))
+    for b in range(block_ref.shape[0]):
+        mine = box_of_row == start + b
+        for n in range(pairs):
+            left = jnp.concatenate(
+                [jnp.where(mine, lefts[2 * n + c], 0.0).astype(BF16) for c in range(2)], axis=1
+            )
+            right = jnp.concatenate([block_ref[b, n, 0], block_ref[b, n, 1]], axis=1)
+            total = total + dot(left, right, NT)
+    return total
+
+
 def near_kernel(
-    list_ref, own_ref, core_ref, next_ref, held_ref, block_ref, out_ref, pass_ref
-):
+    list_ref, own_ref, core_ref, next_ref, held_ref, block_ref, block_hbm,
+    out_ref, found_ref, pass_ref, rest_ref, sem,
+):
+    start = block_ref.shape[0]
+    fetch = pltpu.make_async_copy(block_hbm.at[pl.ds(start, rest_ref.shape[0])], rest_ref, sem)
+    fetch.start()
     pairs, boxes = list_ref.shape
     slots = out_ref.shape[1]
     lines = own_ref.shape[1] // slots
@@ -227,26 +260,14 @@
     zero = jnp.zeros((slots - 3 * boxes, lines * slots), BF16)
     source = jnp.concatenate([own_ref[...], core_ref[...], next_ref[...], zero], axis=0)
     found = dot(hot, source)
-    picked = [found[:, j * slots : (j + 1) * slots] for j in range(lines)]
-    box_of_row = iota((lines * boxes, slots), 0) & (boxes - 1)
-    lefts = []
-    for n in range(pairs):
-        part = [value[n * boxes : (n + 1) * boxes] for value in picked]
-        lefts.append(jnp.concatenate(part, axis=0))
-        lefts.append(jnp.concatenate([-part[2], -part[3], part[0], part[1]], axis=0))
-    total = jnp.zeros((lines * boxes, slots), F32)
-    for b in range(boxes):
-        mine = box_of_row == b
-        for n in range(pairs):
-            left = jnp.concatenate(
-                [jnp.where(mine, lefts[2 * n + c], 0.0).astype(BF16) for c in range(2)], axis=1
-            )
-            right = jnp.concatenate([block_ref[b, n, 0], block_ref[b, n, 1]], axis=1)
-            total = total + dot(left, right, NT)
-    out_ref[...] = total
-
-
-def mine_kernel(list_ref, coef_ref, mine_ref, acc_ref):
+    found_ref[...] = found
+    out_ref[...] = add_near(jnp.zeros(out_ref.shape, F32), found, block_ref, 0)
+    fetch.wait()
+
+
+def mine_kernel(
+    list_ref, coef_ref, mine_ref, near_ref, found_ref, block_ref, acc_ref, total_ref
+):
     boxes, slots = acc_ref.shape[1:]
     listed = own_columns(list_ref[...], boxes)
     ids = box_ids(boxes, False)
@@ -254,6 +275,8 @@
     acc = translate(listed, ids, coef_ref, mine_ref, acc)
     for j in range(4):
         acc_ref[j] = acc[j]
+    start = boxes - block_ref.shape[0]
+    total_ref[...] = add_near(near_ref[...], found_ref[...], block_ref, start)
 
 
 def far_kernel(
@@ -271,21 +294,26 @@
         incoming = acc[2 * i] + minus * pltpu.roll(acc[2 * i + 1], half, 1)
         reals.append(-minus * incoming)
         imags.append(pltpu.roll(incoming, half, 1))
-    exact = jnp.concatenate(reals + imags, axis=0)
-    high = exact.astype(BF16).astype(F32)
-    left_rows = jnp.concatenate([high, exact - high], axis=0)
-    box_of_row = iota(left_rows.shape, 0) & (boxes - 1)
-    total = jnp.zeros(left_rows.shape, F32)
-    for b in range(0, boxes, 2):
-        left = jnp.concatenate(
-            [jnp.where(box_of_row == b + h, left_rows, 0.0).astype(BF16) for h in range(2)], axis=1
-        )
-        right = jnp.concatenate([receive_ref[b], receive_ref[b + 1]], axis=0)
-        total = total + dot(left, right)
-    total = (total[: 4 * boxes] + total[4 * boxes :]) + near_ref[...]
+    group = 16
+    box_of_row = iota((8 * group, slots), 0) & (group - 1)
     live = live_rows(pop_ref, boxes, slots)
-    for j in range(4):
-        out_ref[j] = jnp.where(live, total[j * boxes : (j + 1) * boxes], 0.0)
+    for g in range(0, boxes, group):
+        exact = jnp.concatenate([row[g : g + group] for row in reals + imags], axis=0)
+        high = exact.astype(BF16).astype(F32)
+        left_rows = jnp.concatenate([high, exact - high], axis=0)
+        total = jnp.zeros(left_rows.shape, F32)
+        for b in range(0, group, 2):
+            left = jnp.concatenate(
+                [jnp.where(box_of_row == b + h, left_rows, 0.0).astype(BF16) for h in range(2)],
+                axis=1,
+            )
+            right = jnp.concatenate([receive_ref[g + b], receive_ref[g + b + 1]], axis=0)
+            total = total + dot(left, right)
+        total = total[: 4 * group] + total[4 * group :]
+        for j in range(4):
+            near = near_ref[j * boxes + g : j * boxes + g + group, :]
+            value = total[j * group : (j + 1) * group] + near
+            out_ref[j, g : g + group, :] = jnp.where(live[g : g + group], value, 0.0)
 
 
 def call(kernel, out_shape, specs, out_specs, scratch=(), flops=0, size=0):
@@ -347,18 +375,21 @@
         stay(translation.reshape(2, half, types)),
     )
 
-    third = lax.ppermute(pattern, "box", from_line(2))
-    second = lax.ppermute(payload, "box", from_line(1))
-    fourth = lax.ppermute(pattern, "box", from_line(3))
+    got = {}
+    for step, name in enumerate(ORDER):
+        if step:
+            sent = payload if name == "next" else pattern
+            got[name] = lax.ppermute(sent, "box", from_line(step))
     near_core = lax.ppermute(masked, "box", from_core())
 
     padded = -(-types // 128) * 128
+    ready = boxes // 2
     coef, pattern, block = call(
         coef_kernel,
         (
             shape((far * boxes, 2 * slots), F32),
             shape(pattern.shape, BF16),
-            pltpu.VMEM(near_block.shape, BF16),
+            pltpu.VMEM((ready,) + near_block.shape[1:], BF16),
         ),
         [VMEM] * 3 + [HBM],
         (VMEM,) * 3,
@@ -367,28 +398,35 @@
         size=4 << 20,
     )(kinds, trans, pattern, stay(near_block))
 
-    held = jnp.concatenate([pattern, second[:, :wide], third, fourth], axis=0)
+    around = [got[name][:, :wide] for name in ORDER[1:]]
+    held = jnp.concatenate([pattern] + around, axis=0)
     planes = [lax.ppermute(held, "box", from_plane(d)) for d in PLANES]
 
-    near, held = call(
+    near, found, held, rest = call(
         near_kernel,
-        (shape((lines * boxes, slots), F32), shape(held.shape, BF16)),
+        (
+            shape((lines * boxes, slots), F32),
+            shape((pairs * boxes, lines * slots), F32),
+            shape(held.shape, BF16),
+            pltpu.VMEM((boxes - ready,) + near_block.shape[1:], BF16),
+        ),
+        [VMEM] * 6 + [HBM],
+        (VMEM,) * 4,
+        [pltpu.SemaphoreType.DMA(())],
+        flops=2 * 64 * near_block.size,
+        size=near_block.size,
+    )(partners, masked, near_core, got["next"][:, wide:], held, block, stay(near_block))
+
+    mine = jnp.concatenate([held] + planes, axis=0)
+    theirs = lax.ppermute(mine, "box", from_core())
+    acc, near = call(
+        mine_kernel,
+        (shape((lines, boxes, slots), F32), shape(near.shape, F32)),
         [VMEM] * 6,
         (VMEM, VMEM),
-        flops=2 * 128 * near_block.size // 128 * 128,
-        size=near_block.size,
-    )(partners, masked, near_core, second[:, wide:], held, block)
-
-    mine = jnp.concatenate([held] + planes, axis=0)
-    theirs = lax.ppermute(mine, "box", from_core())
-    acc = call(
-        mine_kernel,
-        shape((lines, boxes, slots), F32),
-        [VMEM] * 3,
-        VMEM,
         flops=1024 * 1024 * 256,
         size=2 << 20,
-    )(listed, coef, mine)
+    )(listed, coef, mine, near, found, rest)
 
     part = call(
         far_kernel,

time: 32.9 us -> 32.1 us (0.976)
  starting transfers between devices: 15.6 us -> 15.2 us
    pallas_call x2, Pallas kernels: 2.09 us -> 2.79 us  [the longest x1 1.61 us: body(): call(near_kernel, (shape((lines * boxes, slots), F32), shape((pairs * box...]
    ppermute x3, waiting for transfers between devices: 2.23 us -> 2.84 us  [body(): got[name] = lax.ppermute(sent, 'box', from_line(step))]
    pallas_call x1, Pallas kernels: 2.21 us -> 1.61 us  [body(): call(coef_kernel, (shape((far * boxes, 2 * slots), F32), shape(pattern.sh...]
    ppermute x1, waiting for transfers between devices: 0.82 us -> 0.34 us  [body(): theirs = lax.ppermute(mine, 'box', from_core())]
    ppermute x3, starting transfers between devices: 4.78 us -> 4.33 us  [body(): lax.ppermute(part, 'rep', [(r ^ d, r) for r in range(reps)])]
  transfers between devices with their start and end apart: 11 -> 11, of which waited for: 8 -> 6; matrix products, arithmetic and copies ran while one was open for 0% -> 0% of each run, Pallas kernels for 13% -> 14%
where the time goes in v3:
time: 32.1 us; the launch traced here: 31.8 us
  starting transfers between devices  15.2 us (47%)
  waiting for transfers between devices  8.32 us (26%)
  Pallas kernels  7.48 us (23%)
  other arithmetic  0.66 us (2%)
    ppermute x3, starting transfers between devices, body(): got[name] = lax.ppermute(sent, 'box', from_line(step))  5.84 us
    ppermute x3, waiting for transfers between devices, body(): lax.ppermute(part, 'rep', [(r ^ d, r) for r in range(reps)])  4.42 us
    ppermute x3, starting transfers between devices, body(): lax.ppermute(part, 'rep', [(r ^ d, r) for r in range(reps)])  4.33 us
    ppermute x3, starting transfers between devices, body(): planes = [lax.ppermute(held, 'box', from_plane(d)) for d in PLANES]  4.14 us
    ppermute x3, waiting for transfers between devices, body(): got[name] = lax.ppermute(sent, 'box', from_line(step))  2.84 us
    pallas_call x1, Pallas kernels, body(): call(pattern_kernel, (shape((boxes, wide + lines * slots), BF16), shape((...  1.83 us
    pallas_call x1, Pallas kernels, body(): call(near_kernel, (shape((lines * boxes, slots), F32), shape((pairs * box...  1.61 us
    pallas_call x1, Pallas kernels, body(): call(coef_kernel, (shape((far * boxes, 2 * slots), F32), shape(pattern.sh...  1.61 us
  transfers between devices with their start and end apart: 11, of which 6 were waited for; matrix products, arithmetic and copies ran while one was open for 0% of the time, Pallas kernels for 14%

profile of v3, /device:TPU:0, one launch (start us, length us, event | category | flops | bytes accessed | tf_op | source)
XLA Modules:
  0.0 31.8 jit_solution(12266635612131737411)
XLA Ops:
  0.0 1.8 %shard_map.91 = (bf16[32,768]{1,0:T(8,128)(2,1)S(1)}, bf16[32,256]{1,0:T(8,128)(2,1)S(1)}, bf16[32,512]{1,0:T(8,128)(2,1)S(1)}, s32[1,32]{1,0:T(1,128)S(1)}, s32...) custom-call(s32[1,32]{1,0:T(1,128)} %bitcast.16, ...), custom_call_target="tpu_custom_call" | custom-call | flops 134217728 | bytes 1048576 | tf_op jit(solution)/shard_map/pallas_call | solution.py:347
  1.8 5.8 %collective-permute-start.1 = (bf16[32,768]{1,0:T(8,128)(2,1)S(1)}, bf16[32,768]{1,0:T(8,128)(2,1)S(1)}, u32[]{:S(2)}, u32[]{:S(2)}) collective-permute-start(bf16[32,768]{1,0:T(8,128)(2,1)S(1)} %get-tuple-element.30), channel_id=1, source_target_pairs={{124,0},{8,4},{4,8},{16,12},{12,16},{24,20},{20,24},{32,28},{28,32... | collective-permute-start | bytes 147464 | tf_op jit(solution)/shard_map/ppermute | solution.py:382
  7.7 0.0 collective-permute-start.3
  7.7 0.8 %collective-permute-start = (bf16[32,512]{1,0:T(8,128)(2,1)S(1)}, bf16[32,512]{1,0:T(8,128)(2,1)S(1)}, u32[]{:S(2)}, u32[]{:S(2)}) collective-permute-start(bf16[32,512]{1,0:T(8,128)(2,1)S(1)} %get-tuple-element.29.own_ref), channel_id=1, source_target_pairs={{4,0},{0,4},{12,8},{8,12},{20,16},{16,20},{28,24},{24,28},{36,32},... | collective-permute-start | bytes 98312 | tf_op jit(solution)/shard_map/ppermute | solution.py:383
  8.4 1.6 %shard_map.92 = (f32[1024,256]{1,0:T(8,128)S(1)}, bf16[32,256]{1,0:T(8,128)(2,1)S(1)}, bf16[16,2,2,128,128]{4,3,2,1,0:T(8,128)(2,1)S(1)}) custom-call(s32[32,128]{1,0:T(8,128)S(1)} %get-tuple-element.24.type_ref, f32[2,64,316]{2,1,0:T(8,128)S(1)} %get-tuple-element.25.trans_ref, bf16[32,256]{1,0:T(8,128)(2,1)S(1)} %get-tuple-element.26.pat_ref, ...), custom_call_target="tpu_custom_call" | custom-call | flops 402653184 | bytes 4194304 | tf_op jit(solution)/shard_map/pallas_call | solution.py:387
  10.1 0.0 collective-permute-done.1
  10.1 0.8 %collective-permute-done.3 = bf16[32,256]{1,0:T(8,128)(2,1)S(1)} collective-permute-done((bf16[32,256]{1,0:T(8,128)(2,1)S(1)}, bf16[32,256]{1,0:T(8,128)(2,1)S(1)}, u32[]{:S(2)}, u32[]{:S(2)}) %collective-permute-start.3) | collective-permute-done | bytes 16416 | tf_op jit(solution)/shard_map/ppermute | solution.py:382
  10.8 2.1 %collective-permute-done.2 = bf16[32,256]{1,0:T(8,128)(2,1)S(1)} collective-permute-done((bf16[32,256]{1,0:T(8,128)(2,1)S(1)}, bf16[32,256]{1,0:T(8,128)(2,1)S(1)}, u32[]{:S(2)}, u32[]{:S(2)}) %collective-permute-start.2) | collective-permute-done | bytes 16416 | tf_op jit(solution)/shard_map/ppermute | solution.py:382
  12.9 0.9 %collective-permute-start.4 = (bf16[128,256]{1,0:T(8,128)(2,1)S(1)}, bf16[128,256]{1,0:T(8,128)(2,1)S(1)}, u32[]{:S(2)}, u32[]{:S(2)}) collective-permute-start(bf16[128,256]{1,0:T(8,128)(2,1)S(1)} %pad_maximum_fusion.held_ref), channel_id=1, source_target_pairs={{64,0},{68,4},{72,8},{76,12},{80,16},{84,20},{88,24},{92,28},{96,3... | collective-permute-start | bytes 196616 | tf_op jit(solution)/shard_map/ppermute | solution.py:403
  13.8 0.8 %collective-permute-start.5 = (bf16[128,256]{1,0:T(8,128)(2,1)S(1)}, bf16[128,256]{1,0:T(8,128)(2,1)S(1)}, u32[]{:S(2)}, u32[]{:S(2)}) collective-permute-start(bf16[128,256]{1,0:T(8,128)(2,1)S(1)} %pad_maximum_fusion.held_ref), channel_id=1, source_target_pairs={{96,0},{100,4},{104,8},{108,12},{112,16},{116,20},{120,24},{124,28... | collective-permute-start | bytes 196616 | tf_op jit(solution)/shard_map/ppermute | solution.py:403
  14.6 2.5 %collective-permute-start.6 = (bf16[128,256]{1,0:T(8,128)(2,1)S(1)}, bf16[128,256]{1,0:T(8,128)(2,1)S(1)}, u32[]{:S(2)}, u32[]{:S(2)}) collective-permute-start(bf16[128,256]{1,0:T(8,128)(2,1)S(1)} %pad_maximum_fusion.held_ref), channel_id=1, source_target_pairs={{32,0},{36,4},{40,8},{44,12},{48,16},{52,20},{56,24},{60,28},{64,3... | collective-permute-start | bytes 196616 | tf_op jit(solution)/shard_map/ppermute | solution.py:403
  17.1 1.6 %shard_map.93 = (f32[128,128]{1,0:T(8,128)S(1)}, f32[64,512]{1,0:T(8,128)S(1)}, bf16[128,256]{1,0:T(8,128)(2,1)S(1)}, bf16[16,2,2,128,128]{4,3,2,1,0:T(8,128)(2,1)S(1)}) custom-call(s32[2,32]{1,0:T(2,128)S(1)} %get-tuple-element.28.list_ref, bf16[32,512]{1,0:T(8,128)(2,1)S(1)} %get-tuple-element.29.own_ref, ...), custom_call_target="tpu_custom_call" | custom-call | flops 268435456 | bytes 2097152 | tf_op jit(solution)/shard_map/pallas_call | solution.py:405
  18.7 0.0 copy-start
  18.7 0.0 collective-permute-done.4
  18.8 0.7 %collective-permute-done.5 = bf16[128,256]{1,0:T(8,128)(2,1)S(1)} collective-permute-done((bf16[128,256]{1,0:T(8,128)(2,1)S(1)}, bf16[128,256]{1,0:T(8,128)(2,1)S(1)}, u32[]{:S(2)}, u32[]{:S(2)}) %collective-permute-start.5) | collective-permute-done | bytes 65568 | tf_op jit(solution)/shard_map/ppermute | solution.py:403
  19.5 0.1 collective-permute-start.7
  19.6 1.2 %shard_map.94 = (f32[4,32,128]{2,1,0:T(8,128)S(1)}, f32[128,128]{1,0:T(8,128)S(1)}) custom-call(s32[32,128]{1,0:T(8,128)S(1)} %get-tuple-element.23.list_ref, f32[1024,256]{1,0:T(8,128)S(1)} %get-tuple-element.27.coef_ref, bf16[512,256]{1,0:T(8,128)(2,1)S(1)} %constant_dynamic-update-slice_fusion.mine_ref, f32[128,128]{1,0:T(8,128)S(1)} %get-tuple-element.34.near_ref, ...), custom_call_target="tpu_custom_call" | custom-call | flops 268435456 | bytes 2097152 | tf_op jit(solution)/shard_map/pallas_call | solution.py:422
  20.8 0.3 %collective-permute-done.7.theirs_ref = bf16[512,256]{1,0:T(8,128)(2,1)S(1)} collective-permute-done((bf16[512,256]{1,0:T(8,128)(2,1)S(1)}, bf16[512,256]{1,0:T(8,128)(2,1)S(1)}, u32[]{:S(2)}, u32[]{:S(2)}) %collective-permute-start.7) | collective-permute-done | bytes 262176 | tf_op jit(solution)/shard_map/ppermute | solution.py:421
  21.1 1.2 %shard_map.95 = f32[4,32,128]{2,1,0:T(8,128)S(1)} custom-call(s32[1,32]{1,0:T(1,128)S(1)} %get-tuple-element.22.pop_ref, s32[32,128]{1,0:T(8,128)S(1)} %get-tuple-element.23.list_ref, f32[1024,256]{1,0:T(8,128)S(1)} %get-tuple-element.27.coef_ref, f32[128,128]{1,0:T(8,128)S(1)} %get-tuple-element.37.near_ref, f32[4,32,128]{2,1,0:T(8,128)S(1)} %get-tuple-element.38.acc_ref, ...), custom_call_target="tpu_custom_call" | custom-call | flops 268435456 | bytes 4194304 | tf_op jit(solution)/shard_map/pallas_call | solution.py:431
  22.4 3.3 %collective-permute-start.9 = (f32[4,32,128]{2,1,0:T(8,128)S(1)}, f32[4,32,128]{2,1,0:T(8,128)S(1)}, u32[]{:S(2)}, u32[]{:S(2)}) collective-permute-start(f32[4,32,128]{2,1,0:T(8,128)S(1)} %shard_map.95), channel_id=1, source_target_pairs={{2,0},{3,1},{0,2},{1,3},{6,4},{7,5},{4,6},{5,7},{10,8},{11,9},{8,1... | collective-permute-start | bytes 196616 | tf_op jit(solution)/shard_map/ppermute | solution.py:442
  25.6 1.1 %collective-permute-start.10 = (f32[4,32,128]{2,1,0:T(8,128)S(1)}, f32[4,32,128]{2,1,0:T(8,128)S(1)}, u32[]{:S(2)}, u32[]{:S(2)}) collective-permute-start(f32[4,32,128]{2,1,0:T(8,128)S(1)} %shard_map.95), channel_id=1, source_target_pairs={{3,0},{2,1},{1,2},{0,3},{7,4},{6,5},{5,6},{4,7},{11,8},{10,9},{9,1... | collective-permute-start | bytes 196616 | tf_op jit(solution)/shard_map/ppermute | solution.py:442
  26.7 1.5 %collective-permute-done.9 = f32[4,32,128]{2,1,0:T(8,128)S(1)} collective-permute-done((f32[4,32,128]{2,1,0:T(8,128)S(1)}, f32[4,32,128]{2,1,0:T(8,128)S(1)}, u32[]{:S(2)}, u32[]{:S(2)}) %collective-permute-start.9) | collective-permute-done | bytes 65568 | tf_op jit(solution)/shard_map/ppermute | solution.py:442
  28.2 2.9 %collective-permute-done.10 = f32[4,32,128]{2,1,0:T(8,128)S(1)} collective-permute-done((f32[4,32,128]{2,1,0:T(8,128)S(1)}, f32[4,32,128]{2,1,0:T(8,128)S(1)}, u32[]{:S(2)}, u32[]{:S(2)}) %collective-permute-start.10) | collective-permute-done | bytes 65568 | tf_op jit(solution)/shard_map/ppermute | solution.py:442
  31.1 0.7 %add_add_fusion = f32[4,32,128]{2,1,0:T(8,128)} fusion(f32[4,32,128]{2,1,0:T(8,128)S(1)} %collective-permute-done.9, f32[4,32,128]{2,1,0:T(8,128)S(1)} %collective-permute-done.10, f32[4,32,128]{2,1,0:T(8,128)S(1)} %shard_map.95, f32[4,32,128]{2,1,0:T(8,128)S(1)} %collective-permute-done.8), kind=kLoop, calls=%fused_computation.1 | loop fusion | flops 49152 | bytes 327680 | tf_op jit(solution)/shard_map/add | solution.py:444
  (13 shorter events, 0.1 us)
Async XLA Ops:
  1.8 8.2 %collective-permute-start.1 = (bf16[32,768]{1,0:T(8,128)(2,1)S(1)}, bf16[32,768]{1,0:T(8,128)(2,1)S(1)}, u32[]{:S(2)}, u32[]{:S(2)}) collective-permute-start(bf16[32,768]{1,0:T(8,128)(2,1)S(1)} %get-tuple-element.30), channel_id=1, source_target_pairs={{124,0},{8,4},{4,8},{16,12},{12,16},{24,20},{20,24},{32,28},{28,32... | collective-permute-start | bytes 147464 | tf_op jit(solution)/shard_map/ppermute | solution.py:382
  7.7 3.2 %collective-permute-start.3 = (bf16[32,256]{1,0:T(8,128)(2,1)S(1)}, bf16[32,256]{1,0:T(8,128)(2,1)S(1)}, u32[]{:S(2)}, u32[]{:S(2)}) collective-permute-start(bf16[32,256]{1,0:T(8,128)(2,1)S(1)} %get-tuple-element.26.pat_ref), channel_id=1, source_target_pairs={{12,0},{120,4},{20,8},{0,12},{28,16},{8,20},{36,24},{16,28},{44,32... | collective-permute-start | bytes 49160 | tf_op jit(solution)/shard_map/ppermute | solution.py:382
  7.7 5.2 %collective-permute-start.2 = (bf16[32,256]{1,0:T(8,128)(2,1)S(1)}, bf16[32,256]{1,0:T(8,128)(2,1)S(1)}, u32[]{:S(2)}, u32[]{:S(2)}) collective-permute-start(bf16[32,256]{1,0:T(8,128)(2,1)S(1)} %get-tuple-element.26.pat_ref), channel_id=1, source_target_pairs={{16,0},{20,4},{24,8},{28,12},{0,16},{4,20},{8,24},{12,28},{48,32},... | collective-permute-start | bytes 49160 | tf_op jit(solution)/shard_map/ppermute | solution.py:382
  7.7 9.4 %collective-permute-start = (bf16[32,512]{1,0:T(8,128)(2,1)S(1)}, bf16[32,512]{1,0:T(8,128)(2,1)S(1)}, u32[]{:S(2)}, u32[]{:S(2)}) collective-permute-start(bf16[32,512]{1,0:T(8,128)(2,1)S(1)} %get-tuple-element.29.own_ref), channel_id=1, source_target_pairs={{4,0},{0,4},{12,8},{8,12},{20,16},{16,20},{28,24},{24,28},{36,32},... | collective-permute-start | bytes 98312 | tf_op jit(solution)/shard_map/ppermute | solution.py:383
  12.9 5.8 %collective-permute-start.4 = (bf16[128,256]{1,0:T(8,128)(2,1)S(1)}, bf16[128,256]{1,0:T(8,128)(2,1)S(1)}, u32[]{:S(2)}, u32[]{:S(2)}) collective-permute-start(bf16[128,256]{1,0:T(8,128)(2,1)S(1)} %pad_maximum_fusion.held_ref), channel_id=1, source_target_pairs={{64,0},{68,4},{72,8},{76,12},{80,16},{84,20},{88,24},{92,28},{96,3... | collective-permute-start | bytes 196616 | tf_op jit(solution)/shard_map/ppermute | solution.py:403
  13.8 5.6 %collective-permute-start.5 = (bf16[128,256]{1,0:T(8,128)(2,1)S(1)}, bf16[128,256]{1,0:T(8,128)(2,1)S(1)}, u32[]{:S(2)}, u32[]{:S(2)}) collective-permute-start(bf16[128,256]{1,0:T(8,128)(2,1)S(1)} %pad_maximum_fusion.held_ref), channel_id=1, source_target_pairs={{96,0},{100,4},{104,8},{108,12},{112,16},{116,20},{120,24},{124,28... | collective-permute-start | bytes 196616 | tf_op jit(solution)/shard_map/ppermute | solution.py:403
  14.6 4.8 %collective-permute-start.6 = (bf16[128,256]{1,0:T(8,128)(2,1)S(1)}, bf16[128,256]{1,0:T(8,128)(2,1)S(1)}, u32[]{:S(2)}, u32[]{:S(2)}) collective-permute-start(bf16[128,256]{1,0:T(8,128)(2,1)S(1)} %pad_maximum_fusion.held_ref), channel_id=1, source_target_pairs={{32,0},{36,4},{40,8},{44,12},{48,16},{52,20},{56,24},{60,28},{64,3... | collective-permute-start | bytes 196616 | tf_op jit(solution)/shard_map/ppermute | solution.py:403
  18.7 2.4 %copy-start = (bf16[32,2,1,64,128]{4,3,2,1,0:T(8,128)(2,1)S(1)}, bf16[32,2,1,64,128]{4,3,2,1,0:T(8,128)(2,1)}, u32[]{:S(2)}) copy-start(bf16[32,2,1,64,128]{4,3,2,1,0:T(8,128)(2,1)} %param.12) | copy-start | bytes 3145732
  19.5 1.6 %collective-permute-start.7 = (bf16[512,256]{1,0:T(8,128)(2,1)S(1)}, bf16[512,256]{1,0:T(8,128)(2,1)S(1)}, u32[]{:S(2)}, u32[]{:S(2)}) collective-permute-start(bf16[512,256]{1,0:T(8,128)(2,1)S(1)} %constant_dynamic-update-slice_fusion.mine_ref), channel_id=1, source_target_pairs={{4,0},{0,4},{12,8},{8,12},{20,16},{16,20},{28,24},{24,28},{36,32},... | collective-permute-start | bytes 786440 | tf_op jit(solution)/shard_map/ppermute | solution.py:421
  22.4 5.8 %collective-permute-start.9 = (f32[4,32,128]{2,1,0:T(8,128)S(1)}, f32[4,32,128]{2,1,0:T(8,128)S(1)}, u32[]{:S(2)}, u32[]{:S(2)}) collective-permute-start(f32[4,32,128]{2,1,0:T(8,128)S(1)} %shard_map.95), channel_id=1, source_target_pairs={{2,0},{3,1},{0,2},{1,3},{6,4},{7,5},{4,6},{5,7},{10,8},{11,9},{8,1... | collective-permute-start | bytes 196616 | tf_op jit(solution)/shard_map/ppermute | solution.py:442
  25.6 5.5 %collective-permute-start.10 = (f32[4,32,128]{2,1,0:T(8,128)S(1)}, f32[4,32,128]{2,1,0:T(8,128)S(1)}, u32[]{:S(2)}, u32[]{:S(2)}) collective-permute-start(f32[4,32,128]{2,1,0:T(8,128)S(1)} %shard_map.95), channel_id=1, source_target_pairs={{3,0},{2,1},{1,2},{0,3},{7,4},{6,5},{5,6},{4,7},{11,8},{10,9},{9,1... | collective-permute-start | bytes 196616 | tf_op jit(solution)/shard_map/ppermute | solution.py:442
  26.7 4.4 %collective-permute-start.8 = (f32[4,32,128]{2,1,0:T(8,128)S(1)}, f32[4,32,128]{2,1,0:T(8,128)S(1)}, u32[]{:S(2)}, u32[]{:S(2)}) collective-permute-start(f32[4,32,128]{2,1,0:T(8,128)S(1)} %shard_map.95), channel_id=1, source_target_pairs={{1,0},{0,1},{3,2},{2,3},{5,4},{4,5},{7,6},{6,7},{9,8},{8,9},{11,10... | collective-permute-start | bytes 196616 | tf_op jit(solution)/shard_map/ppermute | solution.py:442

commit v4 on v3

--- a/solution.py
+++ b/solution.py
@@ -182,26 +182,17 @@
     return ((((first + shift) & 15) * 2 + (holder ^ cross)) * boxes) + (lane & (boxes - 1))
 
 
-def translate(listed, ids, coef_ref, source_ref, acc):
-    boxes, far = listed.shape
-    slots = coef_ref.shape[1] // 2
-    group = 8
-    for f in range(0, far, group):
-        hot = jnp.concatenate(
-            [
-                jnp.where(ids == listed[:, g : g + 1], 1.0, 0.0).astype(BF16)
-                for g in range(f, f + group)
-            ],
-            axis=0,
-        )
-        source = dot(hot, source_ref[...])
-        for g in range(group):
-            rows = slice(g * boxes, (g + 1) * boxes)
-            at = (f + g) * boxes
+def translate(hot_ref, side, coef_ref, source_ref, acc):
+    boxes, slots = acc[0].shape
+    group = 8 * boxes
+    for start in range(0, hot_ref.shape[1], group):
+        source = dot(hot_ref[side, start : start + group, :], source_ref[...])
+        for row in range(0, group, boxes):
+            at = start + row
             straight = coef_ref[at : at + boxes, :slots]
             crossed = coef_ref[at : at + boxes, slots:]
             for i in range(2):
-                value = source[rows, i * slots : (i + 1) * slots]
+                value = source[row : row + boxes, i * slots : (i + 1) * slots]
                 acc[2 * i] = acc[2 * i] + straight * value
                 acc[2 * i + 1] = acc[2 * i + 1] + crossed * value
     return acc
@@ -230,8 +221,8 @@
 
 
 def near_kernel(
-    list_ref, own_ref, core_ref, next_ref, held_ref, block_ref, block_hbm,
-    out_ref, found_ref, pass_ref, rest_ref, sem,
+    list_ref, far_ref, own_ref, core_ref, next_ref, held_ref, block_ref, block_hbm,
+    out_ref, found_ref, pass_ref, hot_ref, rest_ref, sem,
 ):
     start = block_ref.shape[0]
     fetch = pltpu.make_async_copy(block_hbm.at[pl.ds(start, rest_ref.shape[0])], rest_ref, sem)
@@ -262,17 +253,21 @@
     found = dot(hot, source)
     found_ref[...] = found
     out_ref[...] = add_near(jnp.zeros(out_ref.shape, F32), found, block_ref, 0)
+    listed = own_columns(far_ref[...], boxes)
+    for side in range(2):
+        wanted = box_ids(boxes, side == 1)
+        for f in range(far_ref.shape[0]):
+            match = jnp.where(wanted == listed[:, f : f + 1], 1.0, 0.0).astype(BF16)
+            hot_ref[side, f * boxes : (f + 1) * boxes, :] = match
     fetch.wait()
 
 
 def mine_kernel(
-    list_ref, coef_ref, mine_ref, near_ref, found_ref, block_ref, acc_ref, total_ref
+    hot_ref, coef_ref, mine_ref, near_ref, found_ref, block_ref, acc_ref, total_ref
 ):
     boxes, slots = acc_ref.shape[1:]
-    listed = own_columns(list_ref[...], boxes)
-    ids = box_ids(boxes, False)
     acc = [jnp.zeros((boxes, slots), F32) for _ in range(4)]
-    acc = translate(listed, ids, coef_ref, mine_ref, acc)
+    acc = translate(hot_ref, 0, coef_ref, mine_ref, acc)
     for j in range(4):
         acc_ref[j] = acc[j]
     start = boxes - block_ref.shape[0]
@@ -280,12 +275,10 @@
 
 
 def far_kernel(
-    pop_ref, list_ref, coef_ref, near_ref, acc_ref, theirs_ref, receive_ref, out_ref
+    pop_ref, hot_ref, coef_ref, near_ref, acc_ref, theirs_ref, receive_ref, out_ref
 ):
     boxes, slots = receive_ref.shape[0], receive_ref.shape[2]
-    listed = own_columns(list_ref[...], boxes)
-    ids = box_ids(boxes, True)
-    acc = translate(listed, ids, coef_ref, theirs_ref, [acc_ref[j] for j in range(4)])
+    acc = translate(hot_ref, 1, coef_ref, theirs_ref, [acc_ref[j] for j in range(4)])
     half = slots // 2
     low = iota((boxes, slots), 1) < half
     minus = jnp.where(low, -1.0, 1.0)
@@ -402,20 +395,21 @@
     held = jnp.concatenate([pattern] + around, axis=0)
     planes = [lax.ppermute(held, "box", from_plane(d)) for d in PLANES]
 
-    near, found, held, rest = call(
+    near, found, held, hot, rest = call(
         near_kernel,
         (
             shape((lines * boxes, slots), F32),
             shape((pairs * boxes, lines * slots), F32),
             shape(held.shape, BF16),
+            shape((2, far * boxes, XS * ZS * boxes), BF16),
             pltpu.VMEM((boxes - ready,) + near_block.shape[1:], BF16),
         ),
-        [VMEM] * 6 + [HBM],
-        (VMEM,) * 4,
+        [VMEM] * 7 + [HBM],
+        (VMEM,) * 5,
         [pltpu.SemaphoreType.DMA(())],
         flops=2 * 64 * near_block.size,
         size=near_block.size,
-    )(partners, masked, near_core, got["next"][:, wide:], held, block, stay(near_block))
+    )(partners, listed, masked, near_core, got["next"][:, wide:], held, block, stay(near_block))
 
     mine = jnp.concatenate([held] + planes, axis=0)
     theirs = lax.ppermute(mine, "box", from_core())
@@ -426,7 +420,7 @@
         (VMEM, VMEM),
         flops=1024 * 1024 * 256,
         size=2 << 20,
-    )(listed, coef, mine, near, found, rest)
+    )(hot, coef, mine, near, found, rest)
 
     part = call(
         far_kernel,
@@ -435,7 +429,7 @@
         VMEM,
         flops=1024 * 1024 * 256,
         size=4 << 20,
-    )(pop, listed, coef, near, acc, theirs, receive.reshape(boxes, 2 * half, slots))
+    )(pop, hot, coef, near, acc, theirs, receive.reshape(boxes, 2 * half, slots))
 
     reps = lax.axis_size("rep")
     others = {

time: 32.1 us -> 31.9 us (level)
    ppermute x3, waiting for transfers between devices: 0.72 us -> 0.32 us  [body(): planes = [lax.ppermute(held, 'box', from_plane(d)) for d in PLANES]]
    pallas_call x1, Pallas kernels: 1.61 us -> 2.01 us  [body(): call(near_kernel, (shape((lines * boxes, slots), F32), shape((pairs * box...]
  transfers between devices with their start and end apart: 11 -> 11, of which waited for: 6 -> 6; matrix products, arithmetic and copies ran while one was open for 0% -> 0% of each run, Pallas kernels for 14% -> 15%
where the time goes in v4:
time: 31.9 us; the launch traced here: 31.5 us
  starting transfers between devices  15.2 us (48%)
  waiting for transfers between devices  8.1 us (25%)
  Pallas kernels  7.45 us (23%)
  other arithmetic  0.66 us (2%)
    ppermute x3, starting transfers between devices, body(): got[name] = lax.ppermute(sent, 'box', from_line(step))  5.84 us
    ppermute x3, waiting for transfers between devices, body(): lax.ppermute(part, 'rep', [(r ^ d, r) for r in range(reps)])  4.42 us
    ppermute x3, starting transfers between devices, body(): lax.ppermute(part, 'rep', [(r ^ d, r) for r in range(reps)])  4.34 us
    ppermute x3, starting transfers between devices, body(): planes = [lax.ppermute(held, 'box', from_plane(d)) for d in PLANES]  4.14 us
    ppermute x3, waiting for transfers between devices, body(): got[name] = lax.ppermute(sent, 'box', from_line(step))  2.84 us
    pallas_call x1, Pallas kernels, body(): call(near_kernel, (shape((lines * boxes, slots), F32), shape((pairs * box...  2.01 us
    pallas_call x1, Pallas kernels, body(): call(pattern_kernel, (shape((boxes, wide + lines * slots), BF16), shape((...  1.83 us
    pallas_call x1, Pallas kernels, body(): call(coef_kernel, (shape((far * boxes, 2 * slots), F32), shape(pattern.sh...  1.61 us
  transfers between devices with their start and end apart: 11, of which 6 were waited for; matrix products, arithmetic and copies ran while one was open for 0% of the time, Pallas kernels for 15%

profile of v4, /device:TPU:0, one launch (start us, length us, event | category | flops | bytes accessed | tf_op | source)
XLA Modules:
  0.0 31.5 jit_solution(138804840040714352)
XLA Ops:
  0.0 1.8 %shard_map.91 = (bf16[32,768]{1,0:T(8,128)(2,1)S(1)}, bf16[32,256]{1,0:T(8,128)(2,1)S(1)}, bf16[32,512]{1,0:T(8,128)(2,1)S(1)}, s32[1,32]{1,0:T(1,128)S(1)}, s32...) custom-call(s32[1,32]{1,0:T(1,128)} %bitcast.16, ...), custom_call_target="tpu_custom_call" | custom-call | flops 134217728 | bytes 1048576 | tf_op jit(solution)/shard_map/pallas_call | solution.py:340
  1.8 5.8 %collective-permute-start.1 = (bf16[32,768]{1,0:T(8,128)(2,1)S(1)}, bf16[32,768]{1,0:T(8,128)(2,1)S(1)}, u32[]{:S(2)}, u32[]{:S(2)}) collective-permute-start(bf16[32,768]{1,0:T(8,128)(2,1)S(1)} %get-tuple-element.27), channel_id=1, source_target_pairs={{124,0},{8,4},{4,8},{16,12},{12,16},{24,20},{20,24},{32,28},{28,32... | collective-permute-start | bytes 147464 | tf_op jit(solution)/shard_map/ppermute | solution.py:375
  7.7 0.0 collective-permute-start.3
  7.7 0.0 collective-permute-start.2
  7.7 0.8 %collective-permute-start = (bf16[32,512]{1,0:T(8,128)(2,1)S(1)}, bf16[32,512]{1,0:T(8,128)(2,1)S(1)}, u32[]{:S(2)}, u32[]{:S(2)}) collective-permute-start(bf16[32,512]{1,0:T(8,128)(2,1)S(1)} %get-tuple-element.26.own_ref), channel_id=1, source_target_pairs={{4,0},{0,4},{12,8},{8,12},{20,16},{16,20},{28,24},{24,28},{36,32},... | collective-permute-start | bytes 98312 | tf_op jit(solution)/shard_map/ppermute | solution.py:376
  8.4 1.6 %shard_map.92 = (f32[1024,256]{1,0:T(8,128)S(1)}, bf16[32,256]{1,0:T(8,128)(2,1)S(1)}, bf16[16,2,2,128,128]{4,3,2,1,0:T(8,128)(2,1)S(1)}) custom-call(s32[32,128]{1,0:T(8,128)S(1)} %get-tuple-element.28.type_ref, f32[2,64,316]{2,1,0:T(8,128)S(1)} %get-tuple-element.29.trans_ref, bf16[32,256]{1,0:T(8,128)(2,1)S(1)} %get-tuple-element.30.pat_ref, ...), custom_call_target="tpu_custom_call" | custom-call | flops 402653184 | bytes 4194304 | tf_op jit(solution)/shard_map/pallas_call | solution.py:380
  10.1 0.8 %collective-permute-done.3 = bf16[32,256]{1,0:T(8,128)(2,1)S(1)} collective-permute-done((bf16[32,256]{1,0:T(8,128)(2,1)S(1)}, bf16[32,256]{1,0:T(8,128)(2,1)S(1)}, u32[]{:S(2)}, u32[]{:S(2)}) %collective-permute-start.3) | collective-permute-done | bytes 16416 | tf_op jit(solution)/shard_map/ppermute | solution.py:375
  10.8 2.1 %collective-permute-done.2 = bf16[32,256]{1,0:T(8,128)(2,1)S(1)} collective-permute-done((bf16[32,256]{1,0:T(8,128)(2,1)S(1)}, bf16[32,256]{1,0:T(8,128)(2,1)S(1)}, u32[]{:S(2)}, u32[]{:S(2)}) %collective-permute-start.2) | collective-permute-done | bytes 16416 | tf_op jit(solution)/shard_map/ppermute | solution.py:375
  12.9 0.9 %collective-permute-start.4 = (bf16[128,256]{1,0:T(8,128)(2,1)S(1)}, bf16[128,256]{1,0:T(8,128)(2,1)S(1)}, u32[]{:S(2)}, u32[]{:S(2)}) collective-permute-start(bf16[128,256]{1,0:T(8,128)(2,1)S(1)} %pad_maximum_fusion.held_ref), channel_id=1, source_target_pairs={{64,0},{68,4},{72,8},{76,12},{80,16},{84,20},{88,24},{92,28},{96,3... | collective-permute-start | bytes 196616 | tf_op jit(solution)/shard_map/ppermute | solution.py:396
  13.8 0.8 %collective-permute-start.5 = (bf16[128,256]{1,0:T(8,128)(2,1)S(1)}, bf16[128,256]{1,0:T(8,128)(2,1)S(1)}, u32[]{:S(2)}, u32[]{:S(2)}) collective-permute-start(bf16[128,256]{1,0:T(8,128)(2,1)S(1)} %pad_maximum_fusion.held_ref), channel_id=1, source_target_pairs={{96,0},{100,4},{104,8},{108,12},{112,16},{116,20},{120,24},{124,28... | collective-permute-start | bytes 196616 | tf_op jit(solution)/shard_map/ppermute | solution.py:396
  14.6 2.5 %collective-permute-start.6 = (bf16[128,256]{1,0:T(8,128)(2,1)S(1)}, bf16[128,256]{1,0:T(8,128)(2,1)S(1)}, u32[]{:S(2)}, u32[]{:S(2)}) collective-permute-start(bf16[128,256]{1,0:T(8,128)(2,1)S(1)} %pad_maximum_fusion.held_ref), channel_id=1, source_target_pairs={{32,0},{36,4},{40,8},{44,12},{48,16},{52,20},{56,24},{60,28},{64,3... | collective-permute-start | bytes 196616 | tf_op jit(solution)/shard_map/ppermute | solution.py:396
  17.1 2.0 %shard_map.93 = (f32[128,128]{1,0:T(8,128)S(1)}, f32[64,512]{1,0:T(8,128)S(1)}, bf16[128,256]{1,0:T(8,128)(2,1)S(1)}, bf16[2,1024,512]{2,1,0:T(8,128)(2,1)S(1)}, bf16[16,2,2,128,128]{4,3,2,1,0:T(8,128)(2,1)S(1)}) custom-call(s32[2,32]{1,0:T(2,128)S(1)} %get-tuple-element.24.list_ref, s32[32,128]{1,0:T(8,128)S(1)} %get-tuple-element.25.far_ref, ...), custom_call_target="tpu_custom_call" | custom-call | flops 268435456 | bytes 2097152 | tf_op jit(solution)/shard_map/pallas_call | solution.py:398
  19.1 0.3 collective-permute-done.5
  19.5 0.1 collective-permute-start.7
  19.6 0.0 copy-start
  19.6 1.0 %shard_map.94 = (f32[4,32,128]{2,1,0:T(8,128)S(1)}, f32[128,128]{1,0:T(8,128)S(1)}) custom-call(bf16[2,1024,512]{2,1,0:T(8,128)(2,1)S(1)} %get-tuple-element.33.hot_ref, f32[1024,256]{1,0:T(8,128)S(1)} %get-tuple-element.34.coef_ref, bf16[512,256]{1,0:T(8,128)(2,1)S(1)} %constant_dynamic-update-slice_fusion.mine_ref, ...), custom_call_target="tpu_custom_call" | custom-call | flops 268435456 | bytes 2097152 | tf_op jit(solution)/shard_map/pallas_call | solution.py:416
  20.6 0.5 %collective-permute-done.7.theirs_ref = bf16[512,256]{1,0:T(8,128)(2,1)S(1)} collective-permute-done((bf16[512,256]{1,0:T(8,128)(2,1)S(1)}, bf16[512,256]{1,0:T(8,128)(2,1)S(1)}, u32[]{:S(2)}, u32[]{:S(2)}) %collective-permute-start.7) | collective-permute-done | bytes 262176 | tf_op jit(solution)/shard_map/ppermute | solution.py:415
  21.1 1.0 %shard_map.95 = f32[4,32,128]{2,1,0:T(8,128)S(1)} custom-call(s32[1,32]{1,0:T(1,128)S(1)} %get-tuple-element.23.pop_ref, bf16[2,1024,512]{2,1,0:T(8,128)(2,1)S(1)} %get-tuple-element.33.hot_ref, f32[1024,256]{1,0:T(8,128)S(1)} %get-tuple-element.34.coef_ref, f32[128,128]{1,0:T(8,128)S(1)} %get-tuple-element.39.near_ref, ...), custom_call_target="tpu_custom_call" | custom-call | flops 268435456 | bytes 4194304 | tf_op jit(solution)/shard_map/pallas_call | solution.py:425
  22.1 3.3 %collective-permute-start.9 = (f32[4,32,128]{2,1,0:T(8,128)S(1)}, f32[4,32,128]{2,1,0:T(8,128)S(1)}, u32[]{:S(2)}, u32[]{:S(2)}) collective-permute-start(f32[4,32,128]{2,1,0:T(8,128)S(1)} %shard_map.95), channel_id=1, source_target_pairs={{2,0},{3,1},{0,2},{1,3},{6,4},{7,5},{4,6},{5,7},{10,8},{11,9},{8,1... | collective-permute-start | bytes 196616 | tf_op jit(solution)/shard_map/ppermute | solution.py:436
  25.4 1.1 %collective-permute-start.10 = (f32[4,32,128]{2,1,0:T(8,128)S(1)}, f32[4,32,128]{2,1,0:T(8,128)S(1)}, u32[]{:S(2)}, u32[]{:S(2)}) collective-permute-start(f32[4,32,128]{2,1,0:T(8,128)S(1)} %shard_map.95), channel_id=1, source_target_pairs={{3,0},{2,1},{1,2},{0,3},{7,4},{6,5},{5,6},{4,7},{11,8},{10,9},{9,1... | collective-permute-start | bytes 196616 | tf_op jit(solution)/shard_map/ppermute | solution.py:436
  26.5 0.0 collective-permute-start.8
  26.5 1.5 %collective-permute-done.9 = f32[4,32,128]{2,1,0:T(8,128)S(1)} collective-permute-done((f32[4,32,128]{2,1,0:T(8,128)S(1)}, f32[4,32,128]{2,1,0:T(8,128)S(1)}, u32[]{:S(2)}, u32[]{:S(2)}) %collective-permute-start.9) | collective-permute-done | bytes 65568 | tf_op jit(solution)/shard_map/ppermute | solution.py:436
  28.0 2.9 %collective-permute-done.10 = f32[4,32,128]{2,1,0:T(8,128)S(1)} collective-permute-done((f32[4,32,128]{2,1,0:T(8,128)S(1)}, f32[4,32,128]{2,1,0:T(8,128)S(1)}, u32[]{:S(2)}, u32[]{:S(2)}) %collective-permute-start.10) | collective-permute-done | bytes 65568 | tf_op jit(solution)/shard_map/ppermute | solution.py:436
  30.9 0.7 %add_add_fusion = f32[4,32,128]{2,1,0:T(8,128)} fusion(f32[4,32,128]{2,1,0:T(8,128)S(1)} %collective-permute-done.9, f32[4,32,128]{2,1,0:T(8,128)S(1)} %collective-permute-done.10, f32[4,32,128]{2,1,0:T(8,128)S(1)} %shard_map.95, f32[4,32,128]{2,1,0:T(8,128)S(1)} %collective-permute-done.8), kind=kLoop, calls=%fused_computation.1 | loop fusion | flops 49152 | bytes 327680 | tf_op jit(solution)/shard_map/add | solution.py:438
  (13 shorter events, 0.1 us)
Async XLA Ops:
  1.8 8.2 %collective-permute-start.1 = (bf16[32,768]{1,0:T(8,128)(2,1)S(1)}, bf16[32,768]{1,0:T(8,128)(2,1)S(1)}, u32[]{:S(2)}, u32[]{:S(2)}) collective-permute-start(bf16[32,768]{1,0:T(8,128)(2,1)S(1)} %get-tuple-element.27), channel_id=1, source_target_pairs={{124,0},{8,4},{4,8},{16,12},{12,16},{24,20},{20,24},{32,28},{28,32... | collective-permute-start | bytes 147464 | tf_op jit(solution)/shard_map/ppermute | solution.py:375
  7.7 3.2 %collective-permute-start.3 = (bf16[32,256]{1,0:T(8,128)(2,1)S(1)}, bf16[32,256]{1,0:T(8,128)(2,1)S(1)}, u32[]{:S(2)}, u32[]{:S(2)}) collective-permute-start(bf16[32,256]{1,0:T(8,128)(2,1)S(1)} %get-tuple-element.30.pat_ref), channel_id=1, source_target_pairs={{12,0},{120,4},{20,8},{0,12},{28,16},{8,20},{36,24},{16,28},{44,32... | collective-permute-start | bytes 49160 | tf_op jit(solution)/shard_map/ppermute | solution.py:375
  7.7 5.2 %collective-permute-start.2 = (bf16[32,256]{1,0:T(8,128)(2,1)S(1)}, bf16[32,256]{1,0:T(8,128)(2,1)S(1)}, u32[]{:S(2)}, u32[]{:S(2)}) collective-permute-start(bf16[32,256]{1,0:T(8,128)(2,1)S(1)} %get-tuple-element.30.pat_ref), channel_id=1, source_target_pairs={{16,0},{20,4},{24,8},{28,12},{0,16},{4,20},{8,24},{12,28},{48,32},... | collective-permute-start | bytes 49160 | tf_op jit(solution)/shard_map/ppermute | solution.py:375
  7.7 9.4 %collective-permute-start = (bf16[32,512]{1,0:T(8,128)(2,1)S(1)}, bf16[32,512]{1,0:T(8,128)(2,1)S(1)}, u32[]{:S(2)}, u32[]{:S(2)}) collective-permute-start(bf16[32,512]{1,0:T(8,128)(2,1)S(1)} %get-tuple-element.26.own_ref), channel_id=1, source_target_pairs={{4,0},{0,4},{12,8},{8,12},{20,16},{16,20},{28,24},{24,28},{36,32},... | collective-permute-start | bytes 98312 | tf_op jit(solution)/shard_map/ppermute | solution.py:376
  12.9 6.2 %collective-permute-start.4 = (bf16[128,256]{1,0:T(8,128)(2,1)S(1)}, bf16[128,256]{1,0:T(8,128)(2,1)S(1)}, u32[]{:S(2)}, u32[]{:S(2)}) collective-permute-start(bf16[128,256]{1,0:T(8,128)(2,1)S(1)} %pad_maximum_fusion.held_ref), channel_id=1, source_target_pairs={{64,0},{68,4},{72,8},{76,12},{80,16},{84,20},{88,24},{92,28},{96,3... | collective-permute-start | bytes 196616 | tf_op jit(solution)/shard_map/ppermute | solution.py:396
  13.8 5.6 %collective-permute-start.5 = (bf16[128,256]{1,0:T(8,128)(2,1)S(1)}, bf16[128,256]{1,0:T(8,128)(2,1)S(1)}, u32[]{:S(2)}, u32[]{:S(2)}) collective-permute-start(bf16[128,256]{1,0:T(8,128)(2,1)S(1)} %pad_maximum_fusion.held_ref), channel_id=1, source_target_pairs={{96,0},{100,4},{104,8},{108,12},{112,16},{116,20},{120,24},{124,28... | collective-permute-start | bytes 196616 | tf_op jit(solution)/shard_map/ppermute | solution.py:396
  14.6 4.8 %collective-permute-start.6 = (bf16[128,256]{1,0:T(8,128)(2,1)S(1)}, bf16[128,256]{1,0:T(8,128)(2,1)S(1)}, u32[]{:S(2)}, u32[]{:S(2)}) collective-permute-start(bf16[128,256]{1,0:T(8,128)(2,1)S(1)} %pad_maximum_fusion.held_ref), channel_id=1, source_target_pairs={{32,0},{36,4},{40,8},{44,12},{48,16},{52,20},{56,24},{60,28},{64,3... | collective-permute-start | bytes 196616 | tf_op jit(solution)/shard_map/ppermute | solution.py:396
  19.5 1.6 %collective-permute-start.7 = (bf16[512,256]{1,0:T(8,128)(2,1)S(1)}, bf16[512,256]{1,0:T(8,128)(2,1)S(1)}, u32[]{:S(2)}, u32[]{:S(2)}) collective-permute-start(bf16[512,256]{1,0:T(8,128)(2,1)S(1)} %constant_dynamic-update-slice_fusion.mine_ref), channel_id=1, source_target_pairs={{4,0},{0,4},{12,8},{8,12},{20,16},{16,20},{28,24},{24,28},{36,32},... | collective-permute-start | bytes 786440 | tf_op jit(solution)/shard_map/ppermute | solution.py:415
  19.6 1.5 %copy-start = (bf16[32,2,1,64,128]{4,3,2,1,0:T(8,128)(2,1)S(1)}, bf16[32,2,1,64,128]{4,3,2,1,0:T(8,128)(2,1)}, u32[]{:S(2)}) copy-start(bf16[32,2,1,64,128]{4,3,2,1,0:T(8,128)(2,1)} %param.12) | copy-start | bytes 3145732
  22.1 5.8 %collective-permute-start.9 = (f32[4,32,128]{2,1,0:T(8,128)S(1)}, f32[4,32,128]{2,1,0:T(8,128)S(1)}, u32[]{:S(2)}, u32[]{:S(2)}) collective-permute-start(f32[4,32,128]{2,1,0:T(8,128)S(1)} %shard_map.95), channel_id=1, source_target_pairs={{2,0},{3,1},{0,2},{1,3},{6,4},{7,5},{4,6},{5,7},{10,8},{11,9},{8,1... | collective-permute-start | bytes 196616 | tf_op jit(solution)/shard_map/ppermute | solution.py:436
  25.4 5.5 %collective-permute-start.10 = (f32[4,32,128]{2,1,0:T(8,128)S(1)}, f32[4,32,128]{2,1,0:T(8,128)S(1)}, u32[]{:S(2)}, u32[]{:S(2)}) collective-permute-start(f32[4,32,128]{2,1,0:T(8,128)S(1)} %shard_map.95), channel_id=1, source_target_pairs={{3,0},{2,1},{1,2},{0,3},{7,4},{6,5},{5,6},{4,7},{11,8},{10,9},{9,1... | collective-permute-start | bytes 196616 | tf_op jit(solution)/shard_map/ppermute | solution.py:436
  26.5 4.4 %collective-permute-start.8 = (f32[4,32,128]{2,1,0:T(8,128)S(1)}, f32[4,32,128]{2,1,0:T(8,128)S(1)}, u32[]{:S(2)}, u32[]{:S(2)}) collective-permute-start(f32[4,32,128]{2,1,0:T(8,128)S(1)} %shard_map.95), channel_id=1, source_target_pairs={{1,0},{0,1},{3,2},{2,3},{5,4},{4,5},{7,6},{6,7},{9,8},{8,9},{11,10... | collective-permute-start | bytes 196616 | tf_op jit(solution)/shard_map/ppermute | solution.py:436

commit v5 on v4

--- a/solution.py
+++ b/solution.py
@@ -287,7 +287,7 @@
         incoming = acc[2 * i] + minus * pltpu.roll(acc[2 * i + 1], half, 1)
         reals.append(-minus * incoming)
         imags.append(pltpu.roll(incoming, half, 1))
-    group = 16
+    group = 8
     box_of_row = iota((8 * group, slots), 0) & (group - 1)
     live = live_rows(pop_ref, boxes, slots)
     for g in range(0, boxes, group):

time: 31.9 us -> 31.7 us (level)
  no operation moved by 1% of the time
where the time goes in v5:
time: 31.7 us; the launch traced here: 31.4 us
  starting transfers between devices  15.2 us (48%)
  waiting for transfers between devices  8.1 us (26%)
  Pallas kernels  7.33 us (23%)
  other arithmetic  0.66 us (2%)
    ppermute x3, starting transfers between devices, body(): got[name] = lax.ppermute(sent, 'box', from_line(step))  5.84 us
    ppermute x3, waiting for transfers between devices, body(): lax.ppermute(part, 'rep', [(r ^ d, r) for r in range(reps)])  4.42 us
    ppermute x3, starting transfers between devices, body(): lax.ppermute(part, 'rep', [(r ^ d, r) for r in range(reps)])  4.33 us
    ppermute x3, starting transfers between devices, body(): planes = [lax.ppermute(held, 'box', from_plane(d)) for d in PLANES]  4.14 us
    ppermute x3, waiting for transfers between devices, body(): got[name] = lax.ppermute(sent, 'box', from_line(step))  2.84 us
    pallas_call x1, Pallas kernels, body(): call(near_kernel, (shape((lines * boxes, slots), F32), shape((pairs * box...  2.01 us
    pallas_call x1, Pallas kernels, body(): call(pattern_kernel, (shape((boxes, wide + lines * slots), BF16), shape((...  1.83 us
    pallas_call x1, Pallas kernels, body(): call(coef_kernel, (shape((far * boxes, 2 * slots), F32), shape(pattern.sh...  1.61 us
  transfers between devices with their start and end apart: 11, of which 6 were waited for; matrix products, arithmetic and copies ran while one was open for 0% of the time, Pallas kernels for 15%

profile of v5, /device:TPU:0, one launch (start us, length us, event | category | flops | bytes accessed | tf_op | source)
XLA Modules:
  0.0 31.4 jit_solution(16326210719263925258)
XLA Ops:
  0.0 1.8 %shard_map.91 = (bf16[32,768]{1,0:T(8,128)(2,1)S(1)}, bf16[32,256]{1,0:T(8,128)(2,1)S(1)}, bf16[32,512]{1,0:T(8,128)(2,1)S(1)}, s32[1,32]{1,0:T(1,128)S(1)}, s32...) custom-call(s32[1,32]{1,0:T(1,128)} %bitcast.16, ...), custom_call_target="tpu_custom_call" | custom-call | flops 134217728 | bytes 1048576 | tf_op jit(solution)/shard_map/pallas_call | solution.py:340
  1.8 5.8 %collective-permute-start.1 = (bf16[32,768]{1,0:T(8,128)(2,1)S(1)}, bf16[32,768]{1,0:T(8,128)(2,1)S(1)}, u32[]{:S(2)}, u32[]{:S(2)}) collective-permute-start(bf16[32,768]{1,0:T(8,128)(2,1)S(1)} %get-tuple-element.27), channel_id=1, source_target_pairs={{124,0},{8,4},{4,8},{16,12},{12,16},{24,20},{20,24},{32,28},{28,32... | collective-permute-start | bytes 147464 | tf_op jit(solution)/shard_map/ppermute | solution.py:375
  7.7 0.8 %collective-permute-start = (bf16[32,512]{1,0:T(8,128)(2,1)S(1)}, bf16[32,512]{1,0:T(8,128)(2,1)S(1)}, u32[]{:S(2)}, u32[]{:S(2)}) collective-permute-start(bf16[32,512]{1,0:T(8,128)(2,1)S(1)} %get-tuple-element.26.own_ref), channel_id=1, source_target_pairs={{4,0},{0,4},{12,8},{8,12},{20,16},{16,20},{28,24},{24,28},{36,32},... | collective-permute-start | bytes 98312 | tf_op jit(solution)/shard_map/ppermute | solution.py:376
  8.4 1.6 %shard_map.92 = (f32[1024,256]{1,0:T(8,128)S(1)}, bf16[32,256]{1,0:T(8,128)(2,1)S(1)}, bf16[16,2,2,128,128]{4,3,2,1,0:T(8,128)(2,1)S(1)}) custom-call(s32[32,128]{1,0:T(8,128)S(1)} %get-tuple-element.28.type_ref, f32[2,64,316]{2,1,0:T(8,128)S(1)} %get-tuple-element.29.trans_ref, bf16[32,256]{1,0:T(8,128)(2,1)S(1)} %get-tuple-element.30.pat_ref, ...), custom_call_target="tpu_custom_call" | custom-call | flops 402653184 | bytes 4194304 | tf_op jit(solution)/shard_map/pallas_call | solution.py:380
  10.1 0.0 collective-permute-done.1
  10.1 0.8 %collective-permute-done.3 = bf16[32,256]{1,0:T(8,128)(2,1)S(1)} collective-permute-done((bf16[32,256]{1,0:T(8,128)(2,1)S(1)}, bf16[32,256]{1,0:T(8,128)(2,1)S(1)}, u32[]{:S(2)}, u32[]{:S(2)}) %collective-permute-start.3) | collective-permute-done | bytes 16416 | tf_op jit(solution)/shard_map/ppermute | solution.py:375
  10.8 2.1 %collective-permute-done.2 = bf16[32,256]{1,0:T(8,128)(2,1)S(1)} collective-permute-done((bf16[32,256]{1,0:T(8,128)(2,1)S(1)}, bf16[32,256]{1,0:T(8,128)(2,1)S(1)}, u32[]{:S(2)}, u32[]{:S(2)}) %collective-permute-start.2) | collective-permute-done | bytes 16416 | tf_op jit(solution)/shard_map/ppermute | solution.py:375
  12.9 0.9 %collective-permute-start.4 = (bf16[128,256]{1,0:T(8,128)(2,1)S(1)}, bf16[128,256]{1,0:T(8,128)(2,1)S(1)}, u32[]{:S(2)}, u32[]{:S(2)}) collective-permute-start(bf16[128,256]{1,0:T(8,128)(2,1)S(1)} %pad_maximum_fusion.held_ref), channel_id=1, source_target_pairs={{64,0},{68,4},{72,8},{76,12},{80,16},{84,20},{88,24},{92,28},{96,3... | collective-permute-start | bytes 196616 | tf_op jit(solution)/shard_map/ppermute | solution.py:396
  13.8 0.8 %collective-permute-start.5 = (bf16[128,256]{1,0:T(8,128)(2,1)S(1)}, bf16[128,256]{1,0:T(8,128)(2,1)S(1)}, u32[]{:S(2)}, u32[]{:S(2)}) collective-permute-start(bf16[128,256]{1,0:T(8,128)(2,1)S(1)} %pad_maximum_fusion.held_ref), channel_id=1, source_target_pairs={{96,0},{100,4},{104,8},{108,12},{112,16},{116,20},{120,24},{124,28... | collective-permute-start | bytes 196616 | tf_op jit(solution)/shard_map/ppermute | solution.py:396
  14.6 2.5 %collective-permute-start.6 = (bf16[128,256]{1,0:T(8,128)(2,1)S(1)}, bf16[128,256]{1,0:T(8,128)(2,1)S(1)}, u32[]{:S(2)}, u32[]{:S(2)}) collective-permute-start(bf16[128,256]{1,0:T(8,128)(2,1)S(1)} %pad_maximum_fusion.held_ref), channel_id=1, source_target_pairs={{32,0},{36,4},{40,8},{44,12},{48,16},{52,20},{56,24},{60,28},{64,3... | collective-permute-start | bytes 196616 | tf_op jit(solution)/shard_map/ppermute | solution.py:396
  17.1 0.0 collective-permute-done.core_ref
  17.1 2.0 %shard_map.93 = (f32[128,128]{1,0:T(8,128)S(1)}, f32[64,512]{1,0:T(8,128)S(1)}, bf16[128,256]{1,0:T(8,128)(2,1)S(1)}, bf16[2,1024,512]{2,1,0:T(8,128)(2,1)S(1)}, bf16[16,2,2,128,128]{4,3,2,1,0:T(8,128)(2,1)S(1)}) custom-call(s32[2,32]{1,0:T(2,128)S(1)} %get-tuple-element.24.list_ref, s32[32,128]{1,0:T(8,128)S(1)} %get-tuple-element.25.far_ref, ...), custom_call_target="tpu_custom_call" | custom-call | flops 268435456 | bytes 2097152 | tf_op jit(solution)/shard_map/pallas_call | solution.py:398
  19.1 0.0 collective-permute-done.4
  19.1 0.3 collective-permute-done.5
  19.5 0.1 collective-permute-start.7
  19.6 0.0 copy-start
  19.6 1.0 %shard_map.94 = (f32[4,32,128]{2,1,0:T(8,128)S(1)}, f32[128,128]{1,0:T(8,128)S(1)}) custom-call(bf16[2,1024,512]{2,1,0:T(8,128)(2,1)S(1)} %get-tuple-element.33.hot_ref, f32[1024,256]{1,0:T(8,128)S(1)} %get-tuple-element.34.coef_ref, bf16[512,256]{1,0:T(8,128)(2,1)S(1)} %constant_dynamic-update-slice_fusion.mine_ref, ...), custom_call_target="tpu_custom_call" | custom-call | flops 268435456 | bytes 2097152 | tf_op jit(solution)/shard_map/pallas_call | solution.py:416
  20.6 0.5 %collective-permute-done.7.theirs_ref = bf16[512,256]{1,0:T(8,128)(2,1)S(1)} collective-permute-done((bf16[512,256]{1,0:T(8,128)(2,1)S(1)}, bf16[512,256]{1,0:T(8,128)(2,1)S(1)}, u32[]{:S(2)}, u32[]{:S(2)}) %collective-permute-start.7) | collective-permute-done | bytes 262176 | tf_op jit(solution)/shard_map/ppermute | solution.py:415
  21.1 0.9 %shard_map.95 = f32[4,32,128]{2,1,0:T(8,128)S(1)} custom-call(s32[1,32]{1,0:T(1,128)S(1)} %get-tuple-element.23.pop_ref, bf16[2,1024,512]{2,1,0:T(8,128)(2,1)S(1)} %get-tuple-element.33.hot_ref, f32[1024,256]{1,0:T(8,128)S(1)} %get-tuple-element.34.coef_ref, f32[128,128]{1,0:T(8,128)S(1)} %get-tuple-element.39.near_ref, ...), custom_call_target="tpu_custom_call" | custom-call | flops 268435456 | bytes 4194304 | tf_op jit(solution)/shard_map/pallas_call | solution.py:425
  22.0 3.3 %collective-permute-start.9 = (f32[4,32,128]{2,1,0:T(8,128)S(1)}, f32[4,32,128]{2,1,0:T(8,128)S(1)}, u32[]{:S(2)}, u32[]{:S(2)}) collective-permute-start(f32[4,32,128]{2,1,0:T(8,128)S(1)} %shard_map.95), channel_id=1, source_target_pairs={{2,0},{3,1},{0,2},{1,3},{6,4},{7,5},{4,6},{5,7},{10,8},{11,9},{8,1... | collective-permute-start | bytes 196616 | tf_op jit(solution)/shard_map/ppermute | solution.py:436
  25.3 1.1 %collective-permute-start.10 = (f32[4,32,128]{2,1,0:T(8,128)S(1)}, f32[4,32,128]{2,1,0:T(8,128)S(1)}, u32[]{:S(2)}, u32[]{:S(2)}) collective-permute-start(f32[4,32,128]{2,1,0:T(8,128)S(1)} %shard_map.95), channel_id=1, source_target_pairs={{3,0},{2,1},{1,2},{0,3},{7,4},{6,5},{5,6},{4,7},{11,8},{10,9},{9,1... | collective-permute-start | bytes 196616 | tf_op jit(solution)/shard_map/ppermute | solution.py:436
  26.3 1.5 %collective-permute-done.9 = f32[4,32,128]{2,1,0:T(8,128)S(1)} collective-permute-done((f32[4,32,128]{2,1,0:T(8,128)S(1)}, f32[4,32,128]{2,1,0:T(8,128)S(1)}, u32[]{:S(2)}, u32[]{:S(2)}) %collective-permute-start.9) | collective-permute-done | bytes 65568 | tf_op jit(solution)/shard_map/ppermute | solution.py:436
  27.8 2.9 %collective-permute-done.10 = f32[4,32,128]{2,1,0:T(8,128)S(1)} collective-permute-done((f32[4,32,128]{2,1,0:T(8,128)S(1)}, f32[4,32,128]{2,1,0:T(8,128)S(1)}, u32[]{:S(2)}, u32[]{:S(2)}) %collective-permute-start.10) | collective-permute-done | bytes 65568 | tf_op jit(solution)/shard_map/ppermute | solution.py:436
  30.8 0.7 %add_add_fusion = f32[4,32,128]{2,1,0:T(8,128)} fusion(f32[4,32,128]{2,1,0:T(8,128)S(1)} %collective-permute-done.9, f32[4,32,128]{2,1,0:T(8,128)S(1)} %collective-permute-done.10, f32[4,32,128]{2,1,0:T(8,128)S(1)} %shard_map.95, f32[4,32,128]{2,1,0:T(8,128)S(1)} %collective-permute-done.8), kind=kLoop, calls=%fused_computation.1 | loop fusion | flops 49152 | bytes 327680 | tf_op jit(solution)/shard_map/add | solution.py:438
  (13 shorter events, 0.1 us)
Async XLA Ops:
  1.8 8.2 %collective-permute-start.1 = (bf16[32,768]{1,0:T(8,128)(2,1)S(1)}, bf16[32,768]{1,0:T(8,128)(2,1)S(1)}, u32[]{:S(2)}, u32[]{:S(2)}) collective-permute-start(bf16[32,768]{1,0:T(8,128)(2,1)S(1)} %get-tuple-element.27), channel_id=1, source_target_pairs={{124,0},{8,4},{4,8},{16,12},{12,16},{24,20},{20,24},{32,28},{28,32... | collective-permute-start | bytes 147464 | tf_op jit(solution)/shard_map/ppermute | solution.py:375
  7.7 3.2 %collective-permute-start.3 = (bf16[32,256]{1,0:T(8,128)(2,1)S(1)}, bf16[32,256]{1,0:T(8,128)(2,1)S(1)}, u32[]{:S(2)}, u32[]{:S(2)}) collective-permute-start(bf16[32,256]{1,0:T(8,128)(2,1)S(1)} %get-tuple-element.30.pat_ref), channel_id=1, source_target_pairs={{12,0},{120,4},{20,8},{0,12},{28,16},{8,20},{36,24},{16,28},{44,32... | collective-permute-start | bytes 49160 | tf_op jit(solution)/shard_map/ppermute | solution.py:375
  7.7 5.2 %collective-permute-start.2 = (bf16[32,256]{1,0:T(8,128)(2,1)S(1)}, bf16[32,256]{1,0:T(8,128)(2,1)S(1)}, u32[]{:S(2)}, u32[]{:S(2)}) collective-permute-start(bf16[32,256]{1,0:T(8,128)(2,1)S(1)} %get-tuple-element.30.pat_ref), channel_id=1, source_target_pairs={{16,0},{20,4},{24,8},{28,12},{0,16},{4,20},{8,24},{12,28},{48,32},... | collective-permute-start | bytes 49160 | tf_op jit(solution)/shard_map/ppermute | solution.py:375
  7.7 9.4 %collective-permute-start = (bf16[32,512]{1,0:T(8,128)(2,1)S(1)}, bf16[32,512]{1,0:T(8,128)(2,1)S(1)}, u32[]{:S(2)}, u32[]{:S(2)}) collective-permute-start(bf16[32,512]{1,0:T(8,128)(2,1)S(1)} %get-tuple-element.26.own_ref), channel_id=1, source_target_pairs={{4,0},{0,4},{12,8},{8,12},{20,16},{16,20},{28,24},{24,28},{36,32},... | collective-permute-start | bytes 98312 | tf_op jit(solution)/shard_map/ppermute | solution.py:376
  12.9 6.2 %collective-permute-start.4 = (bf16[128,256]{1,0:T(8,128)(2,1)S(1)}, bf16[128,256]{1,0:T(8,128)(2,1)S(1)}, u32[]{:S(2)}, u32[]{:S(2)}) collective-permute-start(bf16[128,256]{1,0:T(8,128)(2,1)S(1)} %pad_maximum_fusion.held_ref), channel_id=1, source_target_pairs={{64,0},{68,4},{72,8},{76,12},{80,16},{84,20},{88,24},{92,28},{96,3... | collective-permute-start | bytes 196616 | tf_op jit(solution)/shard_map/ppermute | solution.py:396
  13.8 5.6 %collective-permute-start.5 = (bf16[128,256]{1,0:T(8,128)(2,1)S(1)}, bf16[128,256]{1,0:T(8,128)(2,1)S(1)}, u32[]{:S(2)}, u32[]{:S(2)}) collective-permute-start(bf16[128,256]{1,0:T(8,128)(2,1)S(1)} %pad_maximum_fusion.held_ref), channel_id=1, source_target_pairs={{96,0},{100,4},{104,8},{108,12},{112,16},{116,20},{120,24},{124,28... | collective-permute-start | bytes 196616 | tf_op jit(solution)/shard_map/ppermute | solution.py:396
  14.6 4.8 %collective-permute-start.6 = (bf16[128,256]{1,0:T(8,128)(2,1)S(1)}, bf16[128,256]{1,0:T(8,128)(2,1)S(1)}, u32[]{:S(2)}, u32[]{:S(2)}) collective-permute-start(bf16[128,256]{1,0:T(8,128)(2,1)S(1)} %pad_maximum_fusion.held_ref), channel_id=1, source_target_pairs={{32,0},{36,4},{40,8},{44,12},{48,16},{52,20},{56,24},{60,28},{64,3... | collective-permute-start | bytes 196616 | tf_op jit(solution)/shard_map/ppermute | solution.py:396
  19.5 1.6 %collective-permute-start.7 = (bf16[512,256]{1,0:T(8,128)(2,1)S(1)}, bf16[512,256]{1,0:T(8,128)(2,1)S(1)}, u32[]{:S(2)}, u32[]{:S(2)}) collective-permute-start(bf16[512,256]{1,0:T(8,128)(2,1)S(1)} %constant_dynamic-update-slice_fusion.mine_ref), channel_id=1, source_target_pairs={{4,0},{0,4},{12,8},{8,12},{20,16},{16,20},{28,24},{24,28},{36,32},... | collective-permute-start | bytes 786440 | tf_op jit(solution)/shard_map/ppermute | solution.py:415
  19.6 1.5 %copy-start = (bf16[32,2,1,64,128]{4,3,2,1,0:T(8,128)(2,1)S(1)}, bf16[32,2,1,64,128]{4,3,2,1,0:T(8,128)(2,1)}, u32[]{:S(2)}) copy-start(bf16[32,2,1,64,128]{4,3,2,1,0:T(8,128)(2,1)} %param.12) | copy-start | bytes 3145732
  22.0 5.8 %collective-permute-start.9 = (f32[4,32,128]{2,1,0:T(8,128)S(1)}, f32[4,32,128]{2,1,0:T(8,128)S(1)}, u32[]{:S(2)}, u32[]{:S(2)}) collective-permute-start(f32[4,32,128]{2,1,0:T(8,128)S(1)} %shard_map.95), channel_id=1, source_target_pairs={{2,0},{3,1},{0,2},{1,3},{6,4},{7,5},{4,6},{5,7},{10,8},{11,9},{8,1... | collective-permute-start | bytes 196616 | tf_op jit(solution)/shard_map/ppermute | solution.py:436
  25.3 5.5 %collective-permute-start.10 = (f32[4,32,128]{2,1,0:T(8,128)S(1)}, f32[4,32,128]{2,1,0:T(8,128)S(1)}, u32[]{:S(2)}, u32[]{:S(2)}) collective-permute-start(f32[4,32,128]{2,1,0:T(8,128)S(1)} %shard_map.95), channel_id=1, source_target_pairs={{3,0},{2,1},{1,2},{0,3},{7,4},{6,5},{5,6},{4,7},{11,8},{10,9},{9,1... | collective-permute-start | bytes 196616 | tf_op jit(solution)/shard_map/ppermute | solution.py:436
  26.3 4.4 %collective-permute-start.8 = (f32[4,32,128]{2,1,0:T(8,128)S(1)}, f32[4,32,128]{2,1,0:T(8,128)S(1)}, u32[]{:S(2)}, u32[]{:S(2)}) collective-permute-start(f32[4,32,128]{2,1,0:T(8,128)S(1)} %shard_map.95), channel_id=1, source_target_pairs={{1,0},{0,1},{3,2},{2,3},{5,4},{4,5},{7,6},{6,7},{9,8},{8,9},{11,10... | collective-permute-start | bytes 196616 | tf_op jit(solution)/shard_map/ppermute | solution.py:436

commit v6 on v5

--- a/solution.py
+++ b/solution.py
@@ -83,21 +83,13 @@
 
 
 def pattern_kernel(
-    pop_hbm, cur_hbm, rad_hbm, list_hbm, type_hbm, near_hbm, trans_hbm,
-    pay_ref, pat_ref, masked_ref, pop_ref, list_ref, type_ref, near_ref, trans_ref,
-    cur_ref, rad_ref, sems,
+    pop_hbm, cur_hbm, rad_hbm, pay_ref, pat_ref, masked_ref, pop_ref, cur_ref, rad_ref, sems
 ):
     lines, boxes, slots = cur_ref.shape
-    place = lax.axis_index("box")
-    tile = pl.multiple_of((place >> 2) * 128, 128)
     copies = [
         pltpu.make_async_copy(pop_hbm, pop_ref, sems.at[0]),
         pltpu.make_async_copy(cur_hbm, cur_ref, sems.at[1]),
         pltpu.make_async_copy(rad_hbm, rad_ref, sems.at[2]),
-        pltpu.make_async_copy(list_hbm.at[:, pl.ds(tile, 128)], list_ref, sems.at[3]),
-        pltpu.make_async_copy(type_hbm.at[:, pl.ds(tile, 128)], type_ref, sems.at[4]),
-        pltpu.make_async_copy(near_hbm, near_ref, sems.at[5]),
-        pltpu.make_async_copy(trans_hbm, trans_ref, sems.at[6]),
     ]
     for copy in copies:
         copy.start()
@@ -126,13 +118,21 @@
         out = real + sign * pltpu.roll(imag, half, 1)
         pay_ref[:, i * slots : (i + 1) * slots] = out.astype(BF16)
         pat_ref[:, i * slots : (i + 1) * slots] = out.astype(BF16)
-    for copy in copies[3:]:
-        copy.wait()
-
 
 def coef_kernel(
-    type_ref, trans_ref, pat_ref, block_hbm, coef_ref, pass_ref, block_ref, table_ref, sem
-):
+    list_hbm, type_hbm, near_hbm, trans_hbm, pat_ref, block_hbm,
+    coef_ref, pass_ref, block_ref, list_ref, near_ref, type_ref, trans_ref, table_ref, sem, sems,
+):
+    place = lax.axis_index("box")
+    tile = pl.multiple_of((place >> 2) * 128, 128)
+    copies = [
+        pltpu.make_async_copy(type_hbm.at[:, pl.ds(tile, 128)], type_ref, sems.at[0]),
+        pltpu.make_async_copy(trans_hbm, trans_ref, sems.at[1]),
+        pltpu.make_async_copy(list_hbm.at[:, pl.ds(tile, 128)], list_ref, sems.at[2]),
+        pltpu.make_async_copy(near_hbm, near_ref, sems.at[3]),
+    ]
+    for copy in copies:
+        copy.start()
     fetch = pltpu.make_async_copy(block_hbm.at[pl.ds(0, block_ref.shape[0])], block_ref, sem)
     fetch.start()
     far = type_ref.shape[0]
@@ -141,14 +141,16 @@
     wide = table_ref.shape[2]
     pass_ref[...] = pat_ref[...]
     table_ref[...] = jnp.zeros_like(table_ref)
+    copies[0].wait()
+    copies[1].wait()
     for c in range(2):
         value = trans_ref[c]
         high = value.astype(BF16)
         low = (value - high.astype(F32)).astype(BF16)
         for k in range(2):
-            place = pl.ds((2 * c + k) * half, half)
-            table_ref[0, place, :types] = high
-            table_ref[1, place, :types] = low
+            at = pl.ds((2 * c + k) * half, half)
+            table_ref[0, at, :types] = high
+            table_ref[1, at, :types] = low
     lane = iota((boxes, wide), 1)
     kinds = own_columns(type_ref[...], boxes)
     pieces = []
@@ -156,6 +158,8 @@
         pieces.append(jnp.where(lane == kinds[:, f : f + 1], 1.0, 0.0).astype(BF16))
     hot = jnp.concatenate(pieces, axis=0)
     coef_ref[...] = dot(hot, table_ref[0], NT) + dot(hot, table_ref[1], NT)
+    copies[2].wait()
+    copies[3].wait()
     fetch.wait()
 
 
@@ -337,24 +341,20 @@
     wide = incs * slots
     shape = jax.ShapeDtypeStruct
 
-    payload, pattern, masked, pop, listed, kinds, partners, trans = call(
+    payload, pattern, masked, pop = call(
         pattern_kernel,
         (
             shape((boxes, wide + lines * slots), BF16),
             shape((boxes, wide), BF16),
             shape((boxes, lines * slots), BF16),
             shape((1, boxes), jnp.int32),
-            shape((far, 128), jnp.int32),
-            shape((far, 128), jnp.int32),
-            shape((pairs, boxes), jnp.int32),
-            shape((2, half, types), F32),
         ),
-        [HBM] * 7,
-        (VMEM,) * 8,
+        [HBM] * 3,
+        (VMEM,) * 4,
         [
             pltpu.VMEM((lines, boxes, slots), BF16),
             pltpu.VMEM((boxes, 2 * half, slots), BF16),
-            pltpu.SemaphoreType.DMA((7,)),
+            pltpu.SemaphoreType.DMA((3,)),
         ],
         flops=2 * 128 * 4096 * 128,
         size=1 << 20,
@@ -362,10 +362,6 @@
         stay(populations.reshape(1, boxes)),
         stay(currents.reshape(lines, boxes, slots)),
         stay(radiate.reshape(boxes, 2 * half, slots)),
-        stay(far_list.T),
-        stay(far_type.T),
-        stay(near_list.T),
-        stay(translation.reshape(2, half, types)),
     )
 
     got = {}
@@ -377,19 +373,34 @@
 
     padded = -(-types // 128) * 128
     ready = boxes // 2
-    coef, pattern, block = call(
+    coef, pattern, block, listed, partners = call(
         coef_kernel,
         (
             shape((far * boxes, 2 * slots), F32),
             shape(pattern.shape, BF16),
             pltpu.VMEM((ready,) + near_block.shape[1:], BF16),
+            shape((far, 128), jnp.int32),
+            shape((pairs, boxes), jnp.int32),
         ),
-        [VMEM] * 3 + [HBM],
-        (VMEM,) * 3,
-        [pltpu.VMEM((2, 4 * half, padded), BF16), pltpu.SemaphoreType.DMA(())],
+        [HBM] * 4 + [VMEM, HBM],
+        (VMEM,) * 5,
+        [
+            pltpu.VMEM((far, 128), jnp.int32),
+            pltpu.VMEM((2, half, types), F32),
+            pltpu.VMEM((2, 4 * half, padded), BF16),
+            pltpu.SemaphoreType.DMA(()),
+            pltpu.SemaphoreType.DMA((4,)),
+        ],
         flops=4 * far * boxes * padded * 2 * slots,
         size=4 << 20,
-    )(kinds, trans, pattern, stay(near_block))
+    )(
+        stay(far_list.T),
+        stay(far_type.T),
+        stay(near_list.T),
+        stay(translation.reshape(2, half, types)),
+        pattern,
+        stay(near_block),
+    )
 
     around = [got[name][:, :wide] for name in ORDER[1:]]
     held = jnp.concatenate([pattern] + around, axis=0)

time: 31.7 us -> 31.7 us (level)
  waiting for transfers between devices: 8.1 us -> 7.15 us
  Pallas kernels: 7.33 us -> 8.23 us
    ppermute x3, waiting for transfers between devices: 2.84 us -> 1.89 us  [body(): got[name] = lax.ppermute(sent, 'box', from_line(step))]
    pallas_call x1, Pallas kernels: 1.61 us -> 2.55 us  [body(): call(coef_kernel, (shape((far * boxes, 2 * slots), F32), shape(pattern.sh...]
  transfers between devices with their start and end apart: 11 -> 11, of which waited for: 6 -> 5; matrix products, arithmetic and copies ran while one was open for 0% -> 0% of each run, Pallas kernels for 15% -> 18%
where the time goes in v6:
time: 31.7 us; the launch traced here: 31.4 us
  starting transfers between devices  15.2 us (48%)
  Pallas kernels  8.23 us (26%)
  waiting for transfers between devices  7.15 us (23%)
  other arithmetic  0.66 us (2%)
    ppermute x3, starting transfers between devices, body(): got[name] = lax.ppermute(sent, 'box', from_line(step))  5.84 us
    ppermute x3, waiting for transfers between devices, body(): lax.ppermute(part, 'rep', [(r ^ d, r) for r in range(reps)])  4.42 us
    ppermute x3, starting transfers between devices, body(): lax.ppermute(part, 'rep', [(r ^ d, r) for r in range(reps)])  4.33 us
    ppermute x3, starting transfers between devices, body(): planes = [lax.ppermute(held, 'box', from_plane(d)) for d in PLANES]  4.14 us
    pallas_call x1, Pallas kernels, body(): call(coef_kernel, (shape((far * boxes, 2 * slots), F32), shape(pattern.sh...  2.55 us
    pallas_call x1, Pallas kernels, body(): call(near_kernel, (shape((lines * boxes, slots), F32), shape((pairs * box...  2.01 us
    ppermute x3, waiting for transfers between devices, body(): got[name] = lax.ppermute(sent, 'box', from_line(step))  1.89 us
    pallas_call x1, Pallas kernels, body(): call(pattern_kernel, (shape((boxes, wide + lines * slots), BF16), shape((...  1.79 us
  transfers between devices with their start and end apart: 11, of which 5 were waited for; matrix products, arithmetic and copies ran while one was open for 0% of the time, Pallas kernels for 18%

profile of v6, /device:TPU:0, one launch (start us, length us, event | category | flops | bytes accessed | tf_op | source)
XLA Modules:
  0.0 31.4 jit_solution(11726237099698431797)
XLA Ops:
  0.0 1.8 %shard_map.91 = (bf16[32,768]{1,0:T(8,128)(2,1)S(1)}, bf16[32,256]{1,0:T(8,128)(2,1)S(1)}, bf16[32,512]{1,0:T(8,128)(2,1)S(1)}, s32[1,32]{1,0:T(1,128)S(1)}) custom-call(s32[1,32]{1,0:T(1,128)} %bitcast.16, bf16[4,32,128]{2,1,0:T(8,128)(2,1)} %bitcast.14, bf16[32,128,128]{2,1,0:T(8,128)(2,1)} %bitcast.10), custom_call_target="tpu_custom_call" | custom-call | flops 134217728 | bytes 1048576 | tf_op jit(solution)/shard_map/pallas_call | solution.py:344
  1.8 5.8 %collective-permute-start.1 = (bf16[32,768]{1,0:T(8,128)(2,1)S(1)}, bf16[32,768]{1,0:T(8,128)(2,1)S(1)}, u32[]{:S(2)}, u32[]{:S(2)}) collective-permute-start(bf16[32,768]{1,0:T(8,128)(2,1)S(1)} %get-tuple-element.26), channel_id=1, source_target_pairs={{124,0},{8,4},{4,8},{16,12},{12,16},{24,20},{20,24},{32,28},{28,32... | collective-permute-start | bytes 147464 | tf_op jit(solution)/shard_map/ppermute | solution.py:371
  7.6 0.8 %collective-permute-start = (bf16[32,512]{1,0:T(8,128)(2,1)S(1)}, bf16[32,512]{1,0:T(8,128)(2,1)S(1)}, u32[]{:S(2)}, u32[]{:S(2)}) collective-permute-start(bf16[32,512]{1,0:T(8,128)(2,1)S(1)} %get-tuple-element.25.own_ref), channel_id=1, source_target_pairs={{4,0},{0,4},{12,8},{8,12},{20,16},{16,20},{28,24},{24,28},{36,32},... | collective-permute-start | bytes 98312 | tf_op jit(solution)/shard_map/ppermute | solution.py:372
  8.4 2.5 %shard_map.92 = (f32[1024,256]{1,0:T(8,128)S(1)}, bf16[32,256]{1,0:T(8,128)(2,1)S(1)}, bf16[16,2,2,128,128]{4,3,2,1,0:T(8,128)(2,1)S(1)}, s32[32,128]{1,0:T(8,128)S(1)}, s32[2,32]{1,0:T(2,128)S(1)}) custom-call(s32[32,1024]{1,0:T(8,128)} %bitcast.12, s32[32,1024]{1,0:T(8,128)} %bitcast.13, s32[2,32]{1,0:T(2,128)} %bitcast.15, f32[2,64,316]{2,1,0:T(8,128)} %bitcast.11, ...), custom_call_target="tpu_custom_call" | custom-call | flops 402653184 | bytes 4194304 | tf_op jit(solution)/shard_map/pallas_call | solution.py:376
  11.0 0.0 collective-permute-done.1
  11.0 0.0 collective-permute-done.3
  11.0 1.9 %collective-permute-done.2 = bf16[32,256]{1,0:T(8,128)(2,1)S(1)} collective-permute-done((bf16[32,256]{1,0:T(8,128)(2,1)S(1)}, bf16[32,256]{1,0:T(8,128)(2,1)S(1)}, u32[]{:S(2)}, u32[]{:S(2)}) %collective-permute-start.2) | collective-permute-done | bytes 16416 | tf_op jit(solution)/shard_map/ppermute | solution.py:371
  12.9 0.9 %collective-permute-start.4 = (bf16[128,256]{1,0:T(8,128)(2,1)S(1)}, bf16[128,256]{1,0:T(8,128)(2,1)S(1)}, u32[]{:S(2)}, u32[]{:S(2)}) collective-permute-start(bf16[128,256]{1,0:T(8,128)(2,1)S(1)} %pad_maximum_fusion.held_ref), channel_id=1, source_target_pairs={{64,0},{68,4},{72,8},{76,12},{80,16},{84,20},{88,24},{92,28},{96,3... | collective-permute-start | bytes 196616 | tf_op jit(solution)/shard_map/ppermute | solution.py:407
  13.8 0.8 %collective-permute-start.5 = (bf16[128,256]{1,0:T(8,128)(2,1)S(1)}, bf16[128,256]{1,0:T(8,128)(2,1)S(1)}, u32[]{:S(2)}, u32[]{:S(2)}) collective-permute-start(bf16[128,256]{1,0:T(8,128)(2,1)S(1)} %pad_maximum_fusion.held_ref), channel_id=1, source_target_pairs={{96,0},{100,4},{104,8},{108,12},{112,16},{116,20},{120,24},{124,28... | collective-permute-start | bytes 196616 | tf_op jit(solution)/shard_map/ppermute | solution.py:407
  14.6 2.5 %collective-permute-start.6 = (bf16[128,256]{1,0:T(8,128)(2,1)S(1)}, bf16[128,256]{1,0:T(8,128)(2,1)S(1)}, u32[]{:S(2)}, u32[]{:S(2)}) collective-permute-start(bf16[128,256]{1,0:T(8,128)(2,1)S(1)} %pad_maximum_fusion.held_ref), channel_id=1, source_target_pairs={{32,0},{36,4},{40,8},{44,12},{48,16},{52,20},{56,24},{60,28},{64,3... | collective-permute-start | bytes 196616 | tf_op jit(solution)/shard_map/ppermute | solution.py:407
  17.0 0.0 collective-permute-done.core_ref
  17.0 2.0 %shard_map.93 = (f32[128,128]{1,0:T(8,128)S(1)}, f32[64,512]{1,0:T(8,128)S(1)}, bf16[128,256]{1,0:T(8,128)(2,1)S(1)}, bf16[2,1024,512]{2,1,0:T(8,128)(2,1)S(1)}, bf16[16,2,2,128,128]{4,3,2,1,0:T(8,128)(2,1)S(1)}) custom-call(s32[2,32]{1,0:T(2,128)S(1)} %get-tuple-element.23.list_ref, s32[32,128]{1,0:T(8,128)S(1)} %get-tuple-element.24.far_ref, ...), custom_call_target="tpu_custom_call" | custom-call | flops 268435456 | bytes 2097152 | tf_op jit(solution)/shard_map/pallas_call | solution.py:409
  19.1 0.0 collective-permute-done.4
  19.1 0.3 collective-permute-done.5
  19.4 0.1 collective-permute-start.7
  19.5 0.0 copy-start
  19.5 1.0 %shard_map.94 = (f32[4,32,128]{2,1,0:T(8,128)S(1)}, f32[128,128]{1,0:T(8,128)S(1)}) custom-call(bf16[2,1024,512]{2,1,0:T(8,128)(2,1)S(1)} %get-tuple-element.29.hot_ref, f32[1024,256]{1,0:T(8,128)S(1)} %get-tuple-element.30.coef_ref, bf16[512,256]{1,0:T(8,128)(2,1)S(1)} %constant_dynamic-update-slice_fusion.mine_ref, ...), custom_call_target="tpu_custom_call" | custom-call | flops 268435456 | bytes 2097152 | tf_op jit(solution)/shard_map/pallas_call | solution.py:427
  20.5 0.5 %collective-permute-done.7.theirs_ref = bf16[512,256]{1,0:T(8,128)(2,1)S(1)} collective-permute-done((bf16[512,256]{1,0:T(8,128)(2,1)S(1)}, bf16[512,256]{1,0:T(8,128)(2,1)S(1)}, u32[]{:S(2)}, u32[]{:S(2)}) %collective-permute-start.7) | collective-permute-done | bytes 262176 | tf_op jit(solution)/shard_map/ppermute | solution.py:426
  21.1 0.9 %shard_map.95 = f32[4,32,128]{2,1,0:T(8,128)S(1)} custom-call(s32[1,32]{1,0:T(1,128)S(1)} %get-tuple-element.21.pop_ref, bf16[2,1024,512]{2,1,0:T(8,128)(2,1)S(1)} %get-tuple-element.29.hot_ref, f32[1024,256]{1,0:T(8,128)S(1)} %get-tuple-element.30.coef_ref, f32[128,128]{1,0:T(8,128)S(1)} %get-tuple-element.35.near_ref, ...), custom_call_target="tpu_custom_call" | custom-call | flops 268435456 | bytes 4194304 | tf_op jit(solution)/shard_map/pallas_call | solution.py:436
  22.0 3.3 %collective-permute-start.9 = (f32[4,32,128]{2,1,0:T(8,128)S(1)}, f32[4,32,128]{2,1,0:T(8,128)S(1)}, u32[]{:S(2)}, u32[]{:S(2)}) collective-permute-start(f32[4,32,128]{2,1,0:T(8,128)S(1)} %shard_map.95), channel_id=1, source_target_pairs={{2,0},{3,1},{0,2},{1,3},{6,4},{7,5},{4,6},{5,7},{10,8},{11,9},{8,1... | collective-permute-start | bytes 196616 | tf_op jit(solution)/shard_map/ppermute | solution.py:447
  25.2 1.1 %collective-permute-start.10 = (f32[4,32,128]{2,1,0:T(8,128)S(1)}, f32[4,32,128]{2,1,0:T(8,128)S(1)}, u32[]{:S(2)}, u32[]{:S(2)}) collective-permute-start(f32[4,32,128]{2,1,0:T(8,128)S(1)} %shard_map.95), channel_id=1, source_target_pairs={{3,0},{2,1},{1,2},{0,3},{7,4},{6,5},{5,6},{4,7},{11,8},{10,9},{9,1... | collective-permute-start | bytes 196616 | tf_op jit(solution)/shard_map/ppermute | solution.py:447
  26.3 1.5 %collective-permute-done.9 = f32[4,32,128]{2,1,0:T(8,128)S(1)} collective-permute-done((f32[4,32,128]{2,1,0:T(8,128)S(1)}, f32[4,32,128]{2,1,0:T(8,128)S(1)}, u32[]{:S(2)}, u32[]{:S(2)}) %collective-permute-start.9) | collective-permute-done | bytes 65568 | tf_op jit(solution)/shard_map/ppermute | solution.py:447
  27.8 2.9 %collective-permute-done.10 = f32[4,32,128]{2,1,0:T(8,128)S(1)} collective-permute-done((f32[4,32,128]{2,1,0:T(8,128)S(1)}, f32[4,32,128]{2,1,0:T(8,128)S(1)}, u32[]{:S(2)}, u32[]{:S(2)}) %collective-permute-start.10) | collective-permute-done | bytes 65568 | tf_op jit(solution)/shard_map/ppermute | solution.py:447
  30.7 0.7 %add_add_fusion = f32[4,32,128]{2,1,0:T(8,128)} fusion(f32[4,32,128]{2,1,0:T(8,128)S(1)} %collective-permute-done.9, f32[4,32,128]{2,1,0:T(8,128)S(1)} %collective-permute-done.10, f32[4,32,128]{2,1,0:T(8,128)S(1)} %shard_map.95, f32[4,32,128]{2,1,0:T(8,128)S(1)} %collective-permute-done.8), kind=kLoop, calls=%fused_computation.1 | loop fusion | flops 49152 | bytes 327680 | tf_op jit(solution)/shard_map/add | solution.py:449
  (13 shorter events, 0.1 us)
Async XLA Ops:
  1.8 9.2 %collective-permute-start.1 = (bf16[32,768]{1,0:T(8,128)(2,1)S(1)}, bf16[32,768]{1,0:T(8,128)(2,1)S(1)}, u32[]{:S(2)}, u32[]{:S(2)}) collective-permute-start(bf16[32,768]{1,0:T(8,128)(2,1)S(1)} %get-tuple-element.26), channel_id=1, source_target_pairs={{124,0},{8,4},{4,8},{16,12},{12,16},{24,20},{20,24},{32,28},{28,32... | collective-permute-start | bytes 147464 | tf_op jit(solution)/shard_map/ppermute | solution.py:371
  7.6 3.4 %collective-permute-start.3 = (bf16[32,256]{1,0:T(8,128)(2,1)S(1)}, bf16[32,256]{1,0:T(8,128)(2,1)S(1)}, u32[]{:S(2)}, u32[]{:S(2)}) collective-permute-start(bf16[32,256]{1,0:T(8,128)(2,1)S(1)} %get-tuple-element.22.pat_ref), channel_id=1, source_target_pairs={{12,0},{120,4},{20,8},{0,12},{28,16},{8,20},{36,24},{16,28},{44,32... | collective-permute-start | bytes 49160 | tf_op jit(solution)/shard_map/ppermute | solution.py:371
  7.6 5.2 %collective-permute-start.2 = (bf16[32,256]{1,0:T(8,128)(2,1)S(1)}, bf16[32,256]{1,0:T(8,128)(2,1)S(1)}, u32[]{:S(2)}, u32[]{:S(2)}) collective-permute-start(bf16[32,256]{1,0:T(8,128)(2,1)S(1)} %get-tuple-element.22.pat_ref), channel_id=1, source_target_pairs={{16,0},{20,4},{24,8},{28,12},{0,16},{4,20},{8,24},{12,28},{48,32},... | collective-permute-start | bytes 49160 | tf_op jit(solution)/shard_map/ppermute | solution.py:371
  7.6 9.4 %collective-permute-start = (bf16[32,512]{1,0:T(8,128)(2,1)S(1)}, bf16[32,512]{1,0:T(8,128)(2,1)S(1)}, u32[]{:S(2)}, u32[]{:S(2)}) collective-permute-start(bf16[32,512]{1,0:T(8,128)(2,1)S(1)} %get-tuple-element.25.own_ref), channel_id=1, source_target_pairs={{4,0},{0,4},{12,8},{8,12},{20,16},{16,20},{28,24},{24,28},{36,32},... | collective-permute-start | bytes 98312 | tf_op jit(solution)/shard_map/ppermute | solution.py:372
  12.9 6.2 %collective-permute-start.4 = (bf16[128,256]{1,0:T(8,128)(2,1)S(1)}, bf16[128,256]{1,0:T(8,128)(2,1)S(1)}, u32[]{:S(2)}, u32[]{:S(2)}) collective-permute-start(bf16[128,256]{1,0:T(8,128)(2,1)S(1)} %pad_maximum_fusion.held_ref), channel_id=1, source_target_pairs={{64,0},{68,4},{72,8},{76,12},{80,16},{84,20},{88,24},{92,28},{96,3... | collective-permute-start | bytes 196616 | tf_op jit(solution)/shard_map/ppermute | solution.py:407
  13.8 5.6 %collective-permute-start.5 = (bf16[128,256]{1,0:T(8,128)(2,1)S(1)}, bf16[128,256]{1,0:T(8,128)(2,1)S(1)}, u32[]{:S(2)}, u32[]{:S(2)}) collective-permute-start(bf16[128,256]{1,0:T(8,128)(2,1)S(1)} %pad_maximum_fusion.held_ref), channel_id=1, source_target_pairs={{96,0},{100,4},{104,8},{108,12},{112,16},{116,20},{120,24},{124,28... | collective-permute-start | bytes 196616 | tf_op jit(solution)/shard_map/ppermute | solution.py:407
  14.6 4.8 %collective-permute-start.6 = (bf16[128,256]{1,0:T(8,128)(2,1)S(1)}, bf16[128,256]{1,0:T(8,128)(2,1)S(1)}, u32[]{:S(2)}, u32[]{:S(2)}) collective-permute-start(bf16[128,256]{1,0:T(8,128)(2,1)S(1)} %pad_maximum_fusion.held_ref), channel_id=1, source_target_pairs={{32,0},{36,4},{40,8},{44,12},{48,16},{52,20},{56,24},{60,28},{64,3... | collective-permute-start | bytes 196616 | tf_op jit(solution)/shard_map/ppermute | solution.py:407
  19.4 1.6 %collective-permute-start.7 = (bf16[512,256]{1,0:T(8,128)(2,1)S(1)}, bf16[512,256]{1,0:T(8,128)(2,1)S(1)}, u32[]{:S(2)}, u32[]{:S(2)}) collective-permute-start(bf16[512,256]{1,0:T(8,128)(2,1)S(1)} %constant_dynamic-update-slice_fusion.mine_ref), channel_id=1, source_target_pairs={{4,0},{0,4},{12,8},{8,12},{20,16},{16,20},{28,24},{24,28},{36,32},... | collective-permute-start | bytes 786440 | tf_op jit(solution)/shard_map/ppermute | solution.py:426
  19.5 1.5 %copy-start = (bf16[32,2,1,64,128]{4,3,2,1,0:T(8,128)(2,1)S(1)}, bf16[32,2,1,64,128]{4,3,2,1,0:T(8,128)(2,1)}, u32[]{:S(2)}) copy-start(bf16[32,2,1,64,128]{4,3,2,1,0:T(8,128)(2,1)} %param.12) | copy-start | bytes 3145732
  22.0 5.8 %collective-permute-start.9 = (f32[4,32,128]{2,1,0:T(8,128)S(1)}, f32[4,32,128]{2,1,0:T(8,128)S(1)}, u32[]{:S(2)}, u32[]{:S(2)}) collective-permute-start(f32[4,32,128]{2,1,0:T(8,128)S(1)} %shard_map.95), channel_id=1, source_target_pairs={{2,0},{3,1},{0,2},{1,3},{6,4},{7,5},{4,6},{5,7},{10,8},{11,9},{8,1... | collective-permute-start | bytes 196616 | tf_op jit(solution)/shard_map/ppermute | solution.py:447
  25.2 5.5 %collective-permute-start.10 = (f32[4,32,128]{2,1,0:T(8,128)S(1)}, f32[4,32,128]{2,1,0:T(8,128)S(1)}, u32[]{:S(2)}, u32[]{:S(2)}) collective-permute-start(f32[4,32,128]{2,1,0:T(8,128)S(1)} %shard_map.95), channel_id=1, source_target_pairs={{3,0},{2,1},{1,2},{0,3},{7,4},{6,5},{5,6},{4,7},{11,8},{10,9},{9,1... | collective-permute-start | bytes 196616 | tf_op jit(solution)/shard_map/ppermute | solution.py:447
  26.3 4.4 %collective-permute-start.8 = (f32[4,32,128]{2,1,0:T(8,128)S(1)}, f32[4,32,128]{2,1,0:T(8,128)S(1)}, u32[]{:S(2)}, u32[]{:S(2)}) collective-permute-start(f32[4,32,128]{2,1,0:T(8,128)S(1)} %shard_map.95), channel_id=1, source_target_pairs={{1,0},{0,1},{3,2},{2,3},{5,4},{4,5},{7,6},{6,7},{9,8},{8,9},{11,10... | collective-permute-start | bytes 196616 | tf_op jit(solution)/shard_map/ppermute | solution.py:447

commit v7 on v6

--- a/solution.py
+++ b/solution.py
@@ -372,7 +372,7 @@
     near_core = lax.ppermute(masked, "box", from_core())
 
     padded = -(-types // 128) * 128
-    ready = boxes // 2
+    ready = 3 * boxes // 8
     coef, pattern, block, listed, partners = call(
         coef_kernel,
         (

time: 31.7 us -> 31.7 us (level)
  no operation moved by 1% of the time
where the time goes in v7:
time: 31.7 us; the launch traced here: 31.4 us
  starting transfers between devices  15.2 us (48%)
  Pallas kernels  8.24 us (26%)
  waiting for transfers between devices  7.15 us (23%)
  other arithmetic  0.66 us (2%)
    ppermute x3, starting transfers between devices, body(): got[name] = lax.ppermute(sent, 'box', from_line(step))  5.84 us
    ppermute x3, waiting for transfers between devices, body(): lax.ppermute(part, 'rep', [(r ^ d, r) for r in range(reps)])  4.42 us
    ppermute x3, starting transfers between devices, body(): lax.ppermute(part, 'rep', [(r ^ d, r) for r in range(reps)])  4.33 us
    ppermute x3, starting transfers between devices, body(): planes = [lax.ppermute(held, 'box', from_plane(d)) for d in PLANES]  4.14 us
    pallas_call x1, Pallas kernels, body(): call(coef_kernel, (shape((far * boxes, 2 * slots), F32), shape(pattern.sh...  2.39 us
    ppermute x3, waiting for transfers between devices, body(): got[name] = lax.ppermute(sent, 'box', from_line(step))  2.05 us
    pallas_call x1, Pallas kernels, body(): call(near_kernel, (shape((lines * boxes, slots), F32), shape((pairs * box...  2.03 us
    pallas_call x1, Pallas kernels, body(): call(pattern_kernel, (shape((boxes, wide + lines * slots), BF16), shape((...  1.79 us
  transfers between devices with their start and end apart: 11, of which 5 were waited for; matrix products, arithmetic and copies ran while one was open for 0% of the time, Pallas kernels for 18%

profile of v7, /device:TPU:0, one launch (start us, length us, event | category | flops | bytes accessed | tf_op | source)
XLA Modules:
  0.0 31.4 jit_solution(12416858253339444774)
XLA Ops:
  0.0 1.8 %shard_map.91 = (bf16[32,768]{1,0:T(8,128)(2,1)S(1)}, bf16[32,256]{1,0:T(8,128)(2,1)S(1)}, bf16[32,512]{1,0:T(8,128)(2,1)S(1)}, s32[1,32]{1,0:T(1,128)S(1)}) custom-call(s32[1,32]{1,0:T(1,128)} %bitcast.16, bf16[4,32,128]{2,1,0:T(8,128)(2,1)} %bitcast.14, bf16[32,128,128]{2,1,0:T(8,128)(2,1)} %bitcast.10), custom_call_target="tpu_custom_call" | custom-call | flops 134217728 | bytes 1048576 | tf_op jit(solution)/shard_map/pallas_call | solution.py:344
  1.8 5.8 %collective-permute-start.1 = (bf16[32,768]{1,0:T(8,128)(2,1)S(1)}, bf16[32,768]{1,0:T(8,128)(2,1)S(1)}, u32[]{:S(2)}, u32[]{:S(2)}) collective-permute-start(bf16[32,768]{1,0:T(8,128)(2,1)S(1)} %get-tuple-element.26), channel_id=1, source_target_pairs={{124,0},{8,4},{4,8},{16,12},{12,16},{24,20},{20,24},{32,28},{28,32... | collective-permute-start | bytes 147464 | tf_op jit(solution)/shard_map/ppermute | solution.py:371
  7.6 0.8 %collective-permute-start = (bf16[32,512]{1,0:T(8,128)(2,1)S(1)}, bf16[32,512]{1,0:T(8,128)(2,1)S(1)}, u32[]{:S(2)}, u32[]{:S(2)}) collective-permute-start(bf16[32,512]{1,0:T(8,128)(2,1)S(1)} %get-tuple-element.25.own_ref), channel_id=1, source_target_pairs={{4,0},{0,4},{12,8},{8,12},{20,16},{16,20},{28,24},{24,28},{36,32},... | collective-permute-start | bytes 98312 | tf_op jit(solution)/shard_map/ppermute | solution.py:372
  8.4 2.4 %shard_map.92 = (f32[1024,256]{1,0:T(8,128)S(1)}, bf16[32,256]{1,0:T(8,128)(2,1)S(1)}, bf16[12,2,2,128,128]{4,3,2,1,0:T(8,128)(2,1)S(1)}, s32[32,128]{1,0:T(8,128)S(1)}, s32[2,32]{1,0:T(2,128)S(1)}) custom-call(s32[32,1024]{1,0:T(8,128)} %bitcast.12, s32[32,1024]{1,0:T(8,128)} %bitcast.13, s32[2,32]{1,0:T(2,128)} %bitcast.15, f32[2,64,316]{2,1,0:T(8,128)} %bitcast.11, ...), custom_call_target="tpu_custom_call" | custom-call | flops 402653184 | bytes 4194304 | tf_op jit(solution)/shard_map/pallas_call | solution.py:376
  10.8 0.0 collective-permute-done.1
  10.8 0.0 collective-permute-done.3
  10.8 2.0 %collective-permute-done.2 = bf16[32,256]{1,0:T(8,128)(2,1)S(1)} collective-permute-done((bf16[32,256]{1,0:T(8,128)(2,1)S(1)}, bf16[32,256]{1,0:T(8,128)(2,1)S(1)}, u32[]{:S(2)}, u32[]{:S(2)}) %collective-permute-start.2) | collective-permute-done | bytes 16416 | tf_op jit(solution)/shard_map/ppermute | solution.py:371
  12.9 0.9 %collective-permute-start.4 = (bf16[128,256]{1,0:T(8,128)(2,1)S(1)}, bf16[128,256]{1,0:T(8,128)(2,1)S(1)}, u32[]{:S(2)}, u32[]{:S(2)}) collective-permute-start(bf16[128,256]{1,0:T(8,128)(2,1)S(1)} %pad_maximum_fusion.held_ref), channel_id=1, source_target_pairs={{64,0},{68,4},{72,8},{76,12},{80,16},{84,20},{88,24},{92,28},{96,3... | collective-permute-start | bytes 196616 | tf_op jit(solution)/shard_map/ppermute | solution.py:407
  13.8 0.8 %collective-permute-start.5 = (bf16[128,256]{1,0:T(8,128)(2,1)S(1)}, bf16[128,256]{1,0:T(8,128)(2,1)S(1)}, u32[]{:S(2)}, u32[]{:S(2)}) collective-permute-start(bf16[128,256]{1,0:T(8,128)(2,1)S(1)} %pad_maximum_fusion.held_ref), channel_id=1, source_target_pairs={{96,0},{100,4},{104,8},{108,12},{112,16},{116,20},{120,24},{124,28... | collective-permute-start | bytes 196616 | tf_op jit(solution)/shard_map/ppermute | solution.py:407
  14.6 2.5 %collective-permute-start.6 = (bf16[128,256]{1,0:T(8,128)(2,1)S(1)}, bf16[128,256]{1,0:T(8,128)(2,1)S(1)}, u32[]{:S(2)}, u32[]{:S(2)}) collective-permute-start(bf16[128,256]{1,0:T(8,128)(2,1)S(1)} %pad_maximum_fusion.held_ref), channel_id=1, source_target_pairs={{32,0},{36,4},{40,8},{44,12},{48,16},{52,20},{56,24},{60,28},{64,3... | collective-permute-start | bytes 196616 | tf_op jit(solution)/shard_map/ppermute | solution.py:407
  17.0 0.0 collective-permute-done.core_ref
  17.0 2.0 %shard_map.93 = (f32[128,128]{1,0:T(8,128)S(1)}, f32[64,512]{1,0:T(8,128)S(1)}, bf16[128,256]{1,0:T(8,128)(2,1)S(1)}, bf16[2,1024,512]{2,1,0:T(8,128)(2,1)S(1)}, bf16[20,2,2,128,128]{4,3,2,1,0:T(8,128)(2,1)S(1)}) custom-call(s32[2,32]{1,0:T(2,128)S(1)} %get-tuple-element.23.list_ref, s32[32,128]{1,0:T(8,128)S(1)} %get-tuple-element.24.far_ref, ...), custom_call_target="tpu_custom_call" | custom-call | flops 268435456 | bytes 2097152 | tf_op jit(solution)/shard_map/pallas_call | solution.py:409
  19.1 0.0 collective-permute-done.4
  19.1 0.3 collective-permute-done.5
  19.4 0.1 collective-permute-start.7
  19.5 0.0 copy-start
  19.5 1.1 %shard_map.94 = (f32[4,32,128]{2,1,0:T(8,128)S(1)}, f32[128,128]{1,0:T(8,128)S(1)}) custom-call(bf16[2,1024,512]{2,1,0:T(8,128)(2,1)S(1)} %get-tuple-element.29.hot_ref, f32[1024,256]{1,0:T(8,128)S(1)} %get-tuple-element.30.coef_ref, bf16[512,256]{1,0:T(8,128)(2,1)S(1)} %constant_dynamic-update-slice_fusion.mine_ref, ...), custom_call_target="tpu_custom_call" | custom-call | flops 268435456 | bytes 2097152 | tf_op jit(solution)/shard_map/pallas_call | solution.py:427
  20.7 0.4 %collective-permute-done.7.theirs_ref = bf16[512,256]{1,0:T(8,128)(2,1)S(1)} collective-permute-done((bf16[512,256]{1,0:T(8,128)(2,1)S(1)}, bf16[512,256]{1,0:T(8,128)(2,1)S(1)}, u32[]{:S(2)}, u32[]{:S(2)}) %collective-permute-start.7) | collective-permute-done | bytes 262176 | tf_op jit(solution)/shard_map/ppermute | solution.py:426
  21.1 0.9 %shard_map.95 = f32[4,32,128]{2,1,0:T(8,128)S(1)} custom-call(s32[1,32]{1,0:T(1,128)S(1)} %get-tuple-element.21.pop_ref, bf16[2,1024,512]{2,1,0:T(8,128)(2,1)S(1)} %get-tuple-element.29.hot_ref, f32[1024,256]{1,0:T(8,128)S(1)} %get-tuple-element.30.coef_ref, f32[128,128]{1,0:T(8,128)S(1)} %get-tuple-element.35.near_ref, ...), custom_call_target="tpu_custom_call" | custom-call | flops 268435456 | bytes 4194304 | tf_op jit(solution)/shard_map/pallas_call | solution.py:436
  22.0 3.3 %collective-permute-start.9 = (f32[4,32,128]{2,1,0:T(8,128)S(1)}, f32[4,32,128]{2,1,0:T(8,128)S(1)}, u32[]{:S(2)}, u32[]{:S(2)}) collective-permute-start(f32[4,32,128]{2,1,0:T(8,128)S(1)} %shard_map.95), channel_id=1, source_target_pairs={{2,0},{3,1},{0,2},{1,3},{6,4},{7,5},{4,6},{5,7},{10,8},{11,9},{8,1... | collective-permute-start | bytes 196616 | tf_op jit(solution)/shard_map/ppermute | solution.py:447
  25.2 1.1 %collective-permute-start.10 = (f32[4,32,128]{2,1,0:T(8,128)S(1)}, f32[4,32,128]{2,1,0:T(8,128)S(1)}, u32[]{:S(2)}, u32[]{:S(2)}) collective-permute-start(f32[4,32,128]{2,1,0:T(8,128)S(1)} %shard_map.95), channel_id=1, source_target_pairs={{3,0},{2,1},{1,2},{0,3},{7,4},{6,5},{5,6},{4,7},{11,8},{10,9},{9,1... | collective-permute-start | bytes 196616 | tf_op jit(solution)/shard_map/ppermute | solution.py:447
  26.3 1.5 %collective-permute-done.9 = f32[4,32,128]{2,1,0:T(8,128)S(1)} collective-permute-done((f32[4,32,128]{2,1,0:T(8,128)S(1)}, f32[4,32,128]{2,1,0:T(8,128)S(1)}, u32[]{:S(2)}, u32[]{:S(2)}) %collective-permute-start.9) | collective-permute-done | bytes 65568 | tf_op jit(solution)/shard_map/ppermute | solution.py:447
  27.8 2.9 %collective-permute-done.10 = f32[4,32,128]{2,1,0:T(8,128)S(1)} collective-permute-done((f32[4,32,128]{2,1,0:T(8,128)S(1)}, f32[4,32,128]{2,1,0:T(8,128)S(1)}, u32[]{:S(2)}, u32[]{:S(2)}) %collective-permute-start.10) | collective-permute-done | bytes 65568 | tf_op jit(solution)/shard_map/ppermute | solution.py:447
  30.7 0.7 %add_add_fusion = f32[4,32,128]{2,1,0:T(8,128)} fusion(f32[4,32,128]{2,1,0:T(8,128)S(1)} %collective-permute-done.9, f32[4,32,128]{2,1,0:T(8,128)S(1)} %collective-permute-done.10, f32[4,32,128]{2,1,0:T(8,128)S(1)} %shard_map.95, f32[4,32,128]{2,1,0:T(8,128)S(1)} %collective-permute-done.8), kind=kLoop, calls=%fused_computation.1 | loop fusion | flops 49152 | bytes 327680 | tf_op jit(solution)/shard_map/add | solution.py:449
  (13 shorter events, 0.1 us)
Async XLA Ops:
  1.8 9.0 %collective-permute-start.1 = (bf16[32,768]{1,0:T(8,128)(2,1)S(1)}, bf16[32,768]{1,0:T(8,128)(2,1)S(1)}, u32[]{:S(2)}, u32[]{:S(2)}) collective-permute-start(bf16[32,768]{1,0:T(8,128)(2,1)S(1)} %get-tuple-element.26), channel_id=1, source_target_pairs={{124,0},{8,4},{4,8},{16,12},{12,16},{24,20},{20,24},{32,28},{28,32... | collective-permute-start | bytes 147464 | tf_op jit(solution)/shard_map/ppermute | solution.py:371
  7.6 3.2 %collective-permute-start.3 = (bf16[32,256]{1,0:T(8,128)(2,1)S(1)}, bf16[32,256]{1,0:T(8,128)(2,1)S(1)}, u32[]{:S(2)}, u32[]{:S(2)}) collective-permute-start(bf16[32,256]{1,0:T(8,128)(2,1)S(1)} %get-tuple-element.22.pat_ref), channel_id=1, source_target_pairs={{12,0},{120,4},{20,8},{0,12},{28,16},{8,20},{36,24},{16,28},{44,32... | collective-permute-start | bytes 49160 | tf_op jit(solution)/shard_map/ppermute | solution.py:371
  7.6 5.2 %collective-permute-start.2 = (bf16[32,256]{1,0:T(8,128)(2,1)S(1)}, bf16[32,256]{1,0:T(8,128)(2,1)S(1)}, u32[]{:S(2)}, u32[]{:S(2)}) collective-permute-start(bf16[32,256]{1,0:T(8,128)(2,1)S(1)} %get-tuple-element.22.pat_ref), channel_id=1, source_target_pairs={{16,0},{20,4},{24,8},{28,12},{0,16},{4,20},{8,24},{12,28},{48,32},... | collective-permute-start | bytes 49160 | tf_op jit(solution)/shard_map/ppermute | solution.py:371
  7.6 9.4 %collective-permute-start = (bf16[32,512]{1,0:T(8,128)(2,1)S(1)}, bf16[32,512]{1,0:T(8,128)(2,1)S(1)}, u32[]{:S(2)}, u32[]{:S(2)}) collective-permute-start(bf16[32,512]{1,0:T(8,128)(2,1)S(1)} %get-tuple-element.25.own_ref), channel_id=1, source_target_pairs={{4,0},{0,4},{12,8},{8,12},{20,16},{16,20},{28,24},{24,28},{36,32},... | collective-permute-start | bytes 98312 | tf_op jit(solution)/shard_map/ppermute | solution.py:372
  12.9 6.2 %collective-permute-start.4 = (bf16[128,256]{1,0:T(8,128)(2,1)S(1)}, bf16[128,256]{1,0:T(8,128)(2,1)S(1)}, u32[]{:S(2)}, u32[]{:S(2)}) collective-permute-start(bf16[128,256]{1,0:T(8,128)(2,1)S(1)} %pad_maximum_fusion.held_ref), channel_id=1, source_target_pairs={{64,0},{68,4},{72,8},{76,12},{80,16},{84,20},{88,24},{92,28},{96,3... | collective-permute-start | bytes 196616 | tf_op jit(solution)/shard_map/ppermute | solution.py:407
  13.8 5.6 %collective-permute-start.5 = (bf16[128,256]{1,0:T(8,128)(2,1)S(1)}, bf16[128,256]{1,0:T(8,128)(2,1)S(1)}, u32[]{:S(2)}, u32[]{:S(2)}) collective-permute-start(bf16[128,256]{1,0:T(8,128)(2,1)S(1)} %pad_maximum_fusion.held_ref), channel_id=1, source_target_pairs={{96,0},{100,4},{104,8},{108,12},{112,16},{116,20},{120,24},{124,28... | collective-permute-start | bytes 196616 | tf_op jit(solution)/shard_map/ppermute | solution.py:407
  14.6 4.8 %collective-permute-start.6 = (bf16[128,256]{1,0:T(8,128)(2,1)S(1)}, bf16[128,256]{1,0:T(8,128)(2,1)S(1)}, u32[]{:S(2)}, u32[]{:S(2)}) collective-permute-start(bf16[128,256]{1,0:T(8,128)(2,1)S(1)} %pad_maximum_fusion.held_ref), channel_id=1, source_target_pairs={{32,0},{36,4},{40,8},{44,12},{48,16},{52,20},{56,24},{60,28},{64,3... | collective-permute-start | bytes 196616 | tf_op jit(solution)/shard_map/ppermute | solution.py:407
  19.4 1.6 %collective-permute-start.7 = (bf16[512,256]{1,0:T(8,128)(2,1)S(1)}, bf16[512,256]{1,0:T(8,128)(2,1)S(1)}, u32[]{:S(2)}, u32[]{:S(2)}) collective-permute-start(bf16[512,256]{1,0:T(8,128)(2,1)S(1)} %constant_dynamic-update-slice_fusion.mine_ref), channel_id=1, source_target_pairs={{4,0},{0,4},{12,8},{8,12},{20,16},{16,20},{28,24},{24,28},{36,32},... | collective-permute-start | bytes 786440 | tf_op jit(solution)/shard_map/ppermute | solution.py:426
  19.5 1.5 %copy-start = (bf16[32,2,1,64,128]{4,3,2,1,0:T(8,128)(2,1)S(1)}, bf16[32,2,1,64,128]{4,3,2,1,0:T(8,128)(2,1)}, u32[]{:S(2)}) copy-start(bf16[32,2,1,64,128]{4,3,2,1,0:T(8,128)(2,1)} %param.12) | copy-start | bytes 3145732
  22.0 5.8 %collective-permute-start.9 = (f32[4,32,128]{2,1,0:T(8,128)S(1)}, f32[4,32,128]{2,1,0:T(8,128)S(1)}, u32[]{:S(2)}, u32[]{:S(2)}) collective-permute-start(f32[4,32,128]{2,1,0:T(8,128)S(1)} %shard_map.95), channel_id=1, source_target_pairs={{2,0},{3,1},{0,2},{1,3},{6,4},{7,5},{4,6},{5,7},{10,8},{11,9},{8,1... | collective-permute-start | bytes 196616 | tf_op jit(solution)/shard_map/ppermute | solution.py:447
  25.2 5.5 %collective-permute-start.10 = (f32[4,32,128]{2,1,0:T(8,128)S(1)}, f32[4,32,128]{2,1,0:T(8,128)S(1)}, u32[]{:S(2)}, u32[]{:S(2)}) collective-permute-start(f32[4,32,128]{2,1,0:T(8,128)S(1)} %shard_map.95), channel_id=1, source_target_pairs={{3,0},{2,1},{1,2},{0,3},{7,4},{6,5},{5,6},{4,7},{11,8},{10,9},{9,1... | collective-permute-start | bytes 196616 | tf_op jit(solution)/shard_map/ppermute | solution.py:447
  26.3 4.4 %collective-permute-start.8 = (f32[4,32,128]{2,1,0:T(8,128)S(1)}, f32[4,32,128]{2,1,0:T(8,128)S(1)}, u32[]{:S(2)}, u32[]{:S(2)}) collective-permute-start(f32[4,32,128]{2,1,0:T(8,128)S(1)} %shard_map.95), channel_id=1, source_target_pairs={{1,0},{0,1},{3,2},{2,3},{5,4},{4,5},{7,6},{6,7},{9,8},{8,9},{11,10... | collective-permute-start | bytes 196616 | tf_op jit(solution)/shard_map/ppermute | solution.py:447
